TPU v7x, 256 devices: a whole 4x4x8 slice. The times are simulated.
256 devices in a mesh: blocks: 64 (over z, y, core), group: 4 (over x).
Axes of the slice: x: 4, y: 4, z: 8, core: 2. Of those that a mesh axis runs over, the one named last changes fastest.
Arguments:
- populations: float32 [4, 27, 524288], P('group', None, 'blocks'), may hold values from 0.5 to 1.5
- solid_mask: int32 [4, 524288], P('group', 'blocks'), may hold values 0 or 1
- relax_rates: float32 [27], replicated, may hold values from 0.5 to 1.9
- coarse_pops: bfloat16 [4, 128, 3456], P('group', 'blocks'), may hold values from 0.5 to 1.5
- interface_pairs: int32 [4, 128], P('group'), may hold values from 0 to 127, as said below
Outputs:
- populations_next: float32 [4, 27, 524288], P('group', None, 'blocks')
- coarse_update: float32 [4, 128, 3456], P('group', 'blocks')
Inputs may be any that keep to these rules, and one draw needn't show every extreme that they name: `interface_pairs`: each row q is a permutation of the fine columns. In each aligned block of 2 records (the records of one index of blocks), the owners (column // 2) are each named either 0 times or exactly 2 times.
All inputs are finite; a program needn't handle non-finite values. No bound on the sum of `solid_mask` on one device may be relied on, other than what follows from the above.
Results may differ from a plain program's by a relative error of at most 0.0015.
Values may be sent and summed in bfloat16 or wider, within the bound.
No kernel may reach another device: no remote copies, remote signals or barrier semaphores. Data moves between devices by JAX's collectives and lax.ppermute only.
A program may use at most 64 MiB of HBM per device.

v0:
```python
import jax
import jax.numpy as jnp
import numpy as np
from jax import lax
from jax.experimental import pallas as pl
from jax.experimental.pallas import tpu as pltpu
from jax.sharding import PartitionSpec as P

Q = 27
EDGE = 16
HALF = 8
NX = 32
LANES = 128
PITCH = 48
FIRST = 8
PLANE = 8
BLOCKS = PLANE * PLANE
ROWS = 64
PAIRS = [(i // 9, i // 3 % 3, i % 3) for i in range(Q)]
F32 = jnp.float32
BF16 = jnp.bfloat16


def interp_table():
    fine = np.arange(EDGE)[:, None]
    coarse = np.arange(HALF)[None, :]
    raw = np.maximum(0.0, 1.0 - np.abs((fine - 0.5) / 2.0 - coarse))
    return raw / raw.sum(axis=1, keepdims=True)


def side_tables():
    interp = interp_table()
    pair = interp[0::2] + interp[1::2]
    pools, ghosts, coarse, cell_masks, pop_masks = [], [], [], [], []
    for q in range(4):
        side_y, side_z = q % 2, q // 2
        out_y, out_z = 15 * side_y, 15 * side_z
        next_y = 1 if side_y == 0 else 14
        next_z = 1 if side_z == 0 else 14
        pool = np.zeros((16, 16, 2, 8, 8))
        for s in range(16):
            pool[out_y, s, 0, :, s // 2] = 0.125
            pool[next_y, s, 0, :, s // 2] = 0.125
            pool[s, out_z, 1, :, s // 2] = 0.125
            pool[s, next_z, 1, :, s // 2] = 0.125
        pools.append(pool.reshape(256, 128))
        ghost = np.zeros((2, 8, 8, 2, 16, 16))
        for s in range(16):
            ghost[0, :, :, 0, out_y, s] = interp[s][None, :]
            ghost[1, :, :, 1, s, out_z] = interp[s][None, :]
        ghost = ghost.reshape(128, 512)
        ghosts.append(np.concatenate([ghost, ghost], 0))
        part = np.zeros((2, 8, 8, 3, 2, 8, 8))
        pair_y, pair_z = out_y // 2, out_z // 2
        for a in range(8):
            for b in range(8):
                part[0, :, :, 0, 0, a, b] = np.outer(pair[a], pair[b])
                part[1, :, :, 1, 1, a, b] = np.outer(pair[a], pair[b])
            part[0, :, :, 0, 1, a, pair_y] = np.outer(pair[a], interp[out_z] + interp[next_z])
            part[1, :, :, 1, 0, a, pair_z] = np.outer(pair[a], interp[out_y] + interp[next_y])
            part[1, :, :, 2, 0, a, pair_z] = np.outer(pair[a], interp[out_y])
            part[1, :, :, 2, 1, a, pair_y] = np.outer(pair[a], interp[out_y])
        coarse.append(0.125 * part.reshape(128, 384))
        in_y, in_z = 2 * (1 - side_y), 2 * (1 - side_z)
        cells = np.zeros((2, 32, 16, 16))
        pops = np.zeros((2, 32, 128))
        for i, (a, b, c) in enumerate(PAIRS):
            if b == in_y:
                cells[0, i, out_y, :] = 1.0
                pops[0, i] = 1.0
            if c == in_z:
                cells[1, i, :, out_z] = 1.0
                pops[1, i] = 1.0
            if b == in_y:
                cells[1, i, out_y, :] = 0.0
        cell_masks.append(cells.reshape(64, 256))
        pop_masks.append(pops.reshape(64, 128))
    return (
        np.stack(pools),
        np.stack(ghosts),
        np.stack(coarse),
        np.stack(cell_masks),
        np.stack(pop_masks),
    )


def sides():
    position = lax.axis_index("group")
    return position % 2, position // 2


def lane_ids(rows=8):
    return lax.broadcasted_iota(jnp.int32, (rows, LANES), 1)


def rolled(value, shift):
    return pltpu.roll(value, shift, 1)


def split_bf16(value):
    high = value.astype(BF16)
    return high, (value - high.astype(F32)).astype(BF16)


def dot(left, right):
    return jnp.dot(left, right, preferred_element_type=F32)


def along(table, axis, line):
    out = {}
    for first in range(3):
        for second in range(3):
            keys = []
            for third in range(3):
                key = [first, second]
                key.insert(axis, third)
                keys.append(tuple(key))
            values = line(*[table[key] for key in keys])
            for key, value in zip(keys, values):
                out[key] = value
    return out


def line_moments(low, mid, high):
    both = low + high
    return both + 4.0 * mid, high - low, both


def line_inverse(zeroth, first, second):
    return second - first, zeroth - 0.5 * second, first + second


def collide_cells(current, rates):
    table = {PAIRS[i]: current[i] for i in range(Q)}
    moments = table
    for axis in range(3):
        moments = along(moments, axis, line_moments)
    density = moments[0, 0, 0]
    inverse = 1.0 / density
    flow = [moments[1, 0, 0], moments[0, 1, 0], moments[0, 0, 1]]
    speed = [part * inverse for part in flow]
    carried = [density * part for part in speed]
    square = [carried[axis] * speed[axis] for axis in range(3)]
    third = density * (1.0 / 3.0)
    relaxed = {}
    for index, key in enumerate(PAIRS):
        ones = [axis for axis in range(3) if key[axis] == 1]
        twos = [axis for axis in range(3) if key[axis] == 2]
        scale = (1.0 / 3.0) ** len(twos)
        if len(ones) == 0:
            if len(twos) == 0:
                balance = density
            elif len(twos) == 1:
                balance = third + square[twos[0]]
            elif len(twos) == 2:
                balance = (third + square[twos[0]] + square[twos[1]]) * (1.0 / 3.0)
            else:
                balance = (third + square[0] + square[1] + square[2]) * (1.0 / 9.0)
        elif len(ones) == 1:
            balance = carried[ones[0]] * scale if twos else carried[ones[0]]
        elif len(ones) == 2:
            balance = carried[ones[0]] * speed[ones[1]]
            balance = balance * scale if twos else balance
        else:
            balance = None
        rest = moments[key] if balance is None else moments[key] - balance
        relaxed[key] = rates[index] * rest
    change = relaxed
    for axis in range(3):
        change = along(change, axis, line_inverse)
    return [current[i] - change[PAIRS[i]] for i in range(Q)]


def collide_kernel(g_ref, solid_ref, rates_ref, w_ref, y_ref, z_ref, e_ref):
    side_y, side_z = sides()
    for group in range(4):
        count = min(8, Q - 8 * group)
        for x in range(NX):
            for h in range(2):
                start = 256 * x + LANES * h
                w_ref[h, pl.ds(8 * group * NX + x, count, stride=NX), :] = g_ref[
                    0, 8 * group : 8 * group + count, start : start + LANES
                ]
    rates = []
    for i in range(Q):
        scale = 1.0 / 216.0
        for part in PAIRS[i]:
            scale *= 1.5 if part == 0 else 3.0
        rates.append(rates_ref[i] * scale)

    for h in range(2):

        def chunk(index, carry, h=h):
            x = pl.multiple_of(8 * index, 8)
            current = [w_ref[h, pl.ds(NX * i + x, 8), :] for i in range(Q)]
            solid = solid_ref[pl.ds(2 * x + h, 8, stride=2), :] == 1
            collided = collide_cells(current, rates)
            for i in range(Q):
                w_ref[h, pl.ds(NX * i + x, 8), :] = jnp.where(
                    solid, current[Q - 1 - i], collided[i]
                )
            return carry

        lax.fori_loop(0, NX // 8, chunk, 0)

    send_y, send_z = 2 * (1 - side_y), 2 * (1 - side_z)
    base, inner = 112 * (1 - side_y), 15 * (1 - side_z)
    lanes = lane_ids(NX)
    tile = 1 - side_y

    def population(index, h):
        return w_ref[h, pl.ds(pl.multiple_of(index * NX, NX), NX), :]

    packed = [jnp.zeros((NX, LANES), F32), jnp.zeros((NX, LANES), F32)]
    for k in range(9):
        value = population(9 * (k // 3) + 3 * send_y + k % 3, tile)
        value = rolled(value, (16 * (k % 8) - base) & 127)
        packed[k // 8] = jnp.where(lanes >> 4 == k % 8, value, packed[k // 8])
    y_ref[0] = packed[0]
    y_ref[1] = packed[1]
    for h in range(2):
        packed_z = jnp.zeros((NX, LANES), F32)
        for k in range(9):
            value = population(9 * (k // 3) + 3 * (k % 3) + send_z, h)
            value = rolled(value, (k - inner) & 127)
            packed_z = jnp.where(lanes & 15 == k, value, packed_z)
        z_ref[h] = packed_z
    packed_e = jnp.zeros((NX, LANES), F32)
    for a in range(3):
        value = population(9 * a + 3 * send_y + send_z, tile)
        value = rolled(value, (a - base - inner) & 127)
        packed_e = jnp.where(lanes == a, value, packed_e)
    e_ref[...] = packed_e


def stream_kernel(
    q_ref, w_ref, y_ref, z_ref, e_ref, rec_ref, pool_ref, base_ref, right_ref, left_ref, pay_ref, t_ref
):
    del q_ref
    side_y, side_z = sides()
    lanes = lane_ids()
    cells_z = lanes & 15
    zeros = jnp.zeros((8, LANES), F32)
    for h in range(2):
        for i in range(Q):
            for row in (0, 8, 32, 40):
                t_ref[h, pl.ds(PITCH * i + row, 8), :] = zeros
        for row in range(PITCH * Q, PITCH * 32, 8):
            t_ref[h, pl.ds(row, 8), :] = zeros
    z_valid = [cells_z <= 14, None, cells_z >= 1]

    def shifted(first, second, b, shift):
        first, second = rolled(first, shift), rolled(second, shift)
        if b == 2:
            return jnp.where(lanes >= 16, first, 0.0), jnp.where(lanes < 16, first, second)
        if b == 0:
            return jnp.where(lanes >= 112, second, first), jnp.where(lanes < 112, second, 0.0)
        return first, second

    for i, (a, b, c) in enumerate(PAIRS):
        shift = (16 * (b - 1) + c - 1) % 128
        for x in range(0, NX, 8):
            both = [w_ref[h, pl.ds(NX * i + x, 8), :] for h in range(2)]
            if shift:
                both = shifted(both[0], both[1], b, shift)
            for h in range(2):
                value = both[h]
                if z_valid[c] is not None:
                    value = jnp.where(z_valid[c], value, 0.0)
                t_ref[h, pl.ds(PITCH * i + FIRST + x + a - 1, 8), :] = value

    halo_y, halo_z = 2 * side_y, 2 * side_z
    base, inner = 112 * (1 - side_y), 15 * (1 - side_z)
    tile = 1 - side_y

    def add(h, index, a, x, value):
        rows = pl.ds(PITCH * index + FIRST + x + a - 1, 8)
        t_ref[h, rows, :] = t_ref[h, rows, :] + value

    row_mask = lanes >> 4 == base >> 4
    column_mask = cells_z == inner
    for x in range(0, NX, 8):
        for k in range(9):
            a, c = k // 3, k % 3
            value = rolled(y_ref[k // 8, pl.ds(x, 8), :], (base - 16 * (k % 8) + c - 1) & 127)
            mask = row_mask if z_valid[c] is None else row_mask & z_valid[c]
            add(tile, 9 * a + 3 * halo_y + c, a, x, jnp.where(mask, value, 0.0))
        for k in range(9):
            a, b = k // 3, k % 3
            shift = (inner - k + 16 * (b - 1)) & 127
            both = shifted(z_ref[0, pl.ds(x, 8), :], z_ref[1, pl.ds(x, 8), :], b, shift)
            for h in range(2):
                add(h, 9 * a + 3 * b + halo_z, a, x, jnp.where(column_mask, both[h], 0.0))
        for a in range(3):
            value = rolled(e_ref[pl.ds(x, 8), :], (base + inner - a) & 127)
            value = jnp.where(lanes == base + inner, value, 0.0)
            add(tile, 9 * a + 3 * halo_y + halo_z, a, x, value)

    for group in range(4):
        count = min(8, Q - 8 * group)
        start = PITCH * 8 * group
        for h in range(2):
            for x in range(NX):
                base_ref[
                    8 * group : 8 * group + count, 256 * x + LANES * h : 256 * x + LANES * (h + 1)
                ] = t_ref[h, pl.ds(start + FIRST + x, count, stride=PITCH), :]
            right_ref[8 * group : 8 * group + 8, LANES * h : LANES * (h + 1)] = t_ref[
                h, pl.ds(start + FIRST + NX, 8, stride=PITCH), :
            ]
            left_ref[8 * group : 8 * group + 8, LANES * h : LANES * (h + 1)] = t_ref[
                h, pl.ds(start + FIRST - 1, 8, stride=PITCH), :
            ]

    sums = []
    for h in range(2):
        parts = []
        for i in range(Q):
            for s in range(2):
                row = PITCH * i + FIRST + EDGE * s
                parts.append(
                    t_ref[h, pl.ds(row, 8, stride=2), :] + t_ref[h, pl.ds(row + 1, 8, stride=2), :]
                )
        high, low = FIRST + NX, FIRST - 1
        parts.append(t_ref[h, pl.ds(PITCH * 18 + high, 8, stride=PITCH), :])
        last = t_ref[h, pl.ds(PITCH * 24 + high, 8, stride=PITCH), :]
        rows = lax.broadcasted_iota(jnp.int32, (8, LANES), 0)
        parts.append(jnp.where(rows == 2, last, 0.0))
        parts.append(t_ref[h, pl.ds(low, 8, stride=PITCH), :])
        parts.append(t_ref[h, pl.ds(PITCH * 8 + low, 8, stride=PITCH), :])
        sums.append(jnp.concatenate(parts, 0))
    total = len(parts) * 8
    pooled = jnp.zeros((total, LANES), F32)
    for h in range(2):
        for part in split_bf16(sums[h]):
            pooled = pooled + dot(part, pool_ref[0, LANES * h : LANES * (h + 1), :])
    row_a = lax.broadcasted_iota(jnp.int32, (total, LANES), 0) & 7
    lane_a = lax.broadcasted_iota(jnp.int32, (total, LANES), 1) >> 3 & 7
    pooled = jnp.where(row_a == lane_a, pooled, 0.0)
    target = lax.broadcasted_iota(jnp.int32, (ROWS, total), 0)
    block = lax.broadcasted_iota(jnp.int32, (ROWS, total), 1) >> 3
    column, index = target >> 5, target & 31
    wanted = jnp.where(
        index < Q, 2 * index + column, jnp.where(index < Q + 2, 2 * Q + 2 * column + index - Q, -1)
    )
    chosen = (wanted == block).astype(F32).astype(BF16)
    routed = jnp.zeros((ROWS, LANES), F32)
    for part in split_bf16(pooled):
        routed = routed + dot(chosen, part)
    records = rec_ref[...]
    for slot in range(PLANE):
        pay_ref[slot, 0:ROWS, :] = routed.astype(pay_ref.dtype)
        pay_ref[slot, ROWS : 2 * ROWS, :] = records.astype(pay_ref.dtype)


def owner_of(pairs_ref, device):
    return pairs_ref[2 * device] >> 1


def route_kernel(pairs_ref, inverse_ref, in_ref, out_ref):
    place = lax.axis_index("blocks") & (PLANE - 1)
    for plane in range(PLANE):
        device = PLANE * plane + place
        owner = owner_of(pairs_ref, device)
        source = owner & (PLANE - 1)
        before = (owner - 1) & (PLANE - 1)
        after = (owner + 1) & (PLANE - 1)
        holder = owner_of(inverse_ref, device) & (PLANE - 1)
        main = in_ref[source, 0:ROWS, :]
        rows = lax.broadcasted_iota(jnp.int32, (ROWS, LANES), 0)
        from_before = (rows == 27) | (rows == 28)
        from_after = (rows == 59) | (rows == 60)
        main = jnp.where(from_before, in_ref[before, 0:ROWS, :], main)
        main = jnp.where(from_after, in_ref[after, 0:ROWS, :], main)
        out_ref[plane, 0:ROWS, :] = main
        out_ref[plane, ROWS : 2 * ROWS, :] = in_ref[holder, ROWS : 2 * ROWS, :]


def finish_kernel(
    q_ref,
    pairs_ref,
    inverse_ref,
    base_ref,
    right_ref,
    left_ref,
    in_ref,
    rec_ref,
    line_ref,
    ghost_ref,
    coarse_ref,
    cell_ref,
    pop_ref,
    next_ref,
    update_ref,
):
    del q_ref
    me = lax.axis_index("blocks")
    owner = owner_of(pairs_ref, me)
    before = (owner + BLOCKS - 1) & (BLOCKS - 1)
    after = (owner + 1) & (BLOCKS - 1)
    holder = owner_of(inverse_ref, me)

    records = in_ref[holder >> 3, ROWS : 2 * ROWS, :].astype(F32)
    swap = (inverse_ref[2 * me] & 1) == 1
    first = jnp.where(swap, records[32:64], records[0:32])
    second = jnp.where(swap, records[0:32], records[32:64])
    columns = jnp.concatenate([first, second], 0)
    cell_y = cell_ref[0, 0:Q, :]
    cell_z = cell_ref[0, 32 : 32 + Q, :]
    for x in range(EDGE):
        scaled = columns * line_ref[x : x + 1, :]
        ghost = dot(jnp.concatenate(split_bf16(scaled), 1), ghost_ref[0])
        for s in range(2):
            place = EDGE * s + x
            rows = ghost[32 * s : 32 * s + Q]
            value = base_ref[:, 256 * place : 256 * (place + 1)]
            value = value + rows[:, 0:256] * cell_y + rows[:, 256:512] * cell_z
            if place == 0:
                value = value + right_ref[0:Q, :]
            if place == NX - 1:
                value = value + left_ref[0:Q, :]
            next_ref[0, :, 256 * place : 256 * (place + 1)] = value

    main = in_ref[owner >> 3, 0:ROWS, :].astype(F32)
    lower = in_ref[before >> 3, 16:32, :].astype(F32)
    upper = in_ref[after >> 3, 48:64, :].astype(F32)
    rows = lax.broadcasted_iota(jnp.int32, (32, LANES), 0)
    lane_a = lax.broadcasted_iota(jnp.int32, (32, LANES), 1) >> 3 & 7
    from_low = jnp.where(
        rows == 26, jnp.where(lane_a == 2, lower[12:13], 0.0), jnp.where(rows - 18 == lane_a, lower[11:12], 0.0)
    )
    from_high = jnp.where(
        rows == 8, jnp.where(lane_a == 0, upper[12:13], 0.0), jnp.where(rows == lane_a, upper[11:12], 0.0)
    )
    lane_in = lax.broadcasted_iota(jnp.int32, (LANES, LANES), 0)
    lane_out = lax.broadcasted_iota(jnp.int32, (LANES, LANES), 1)
    alike = ((lane_in >> 6 == lane_out >> 6) & (lane_in & 7 == lane_out & 7)).astype(F32).astype(BF16)
    edges = jnp.zeros((2 * 32, LANES), F32)
    for part in split_bf16(jnp.concatenate([from_low, from_high], 0)):
        edges = edges + dot(part, alike)
    column_0 = main[0:32] + jnp.where(lane_a == 0, edges[0:32], 0.0)
    column_1 = main[32:64] + jnp.where(lane_a == HALF - 1, edges[32:64], 0.0)
    own = dot(rec_ref[...].astype(BF16), coarse_ref[0])
    in_y, in_z = pop_ref[0, 0:32, :], pop_ref[0, 32:64, :]
    for t in range(2):
        share = own[32 * t : 32 * t + 32]
        value = jnp.where((pairs_ref[2 * me + t] & 1) == 1, column_1, column_0)
        value = (
            value
            + in_y * share[:, 0:128]
            + in_z * share[:, 128:256]
            - in_y * in_z * share[:, 256:384]
        )
        for i in range(Q):
            update_ref[0, t : t + 1, LANES * i : LANES * (i + 1)] = value[i : i + 1]


VMEM = pl.BlockSpec(memory_space=pltpu.VMEM)
SMEM = pl.BlockSpec(memory_space=pltpu.SMEM)


def whole(*shape):
    return pl.BlockSpec(shape, lambda i, *scalars: (0,) * len(shape))


def by_side(*shape):
    return pl.BlockSpec((1, *shape), lambda i, side, *rest: (side[0],) + (0,) * len(shape))


def params():
    return pltpu.CompilerParams(vmem_limit_bytes=48 * 1024 * 1024)


def swapped(block, bits):
    return lax.ppermute(block, "group", [(i, i ^ bits) for i in range(4)])


def body(populations, solid_mask, relax_rates, coarse_pops, interface_pairs):
    pools, ghosts, coarse, cell_masks, pop_masks = side_tables()
    position = lax.axis_index("group").astype(jnp.int32).reshape(1)
    pairs = interface_pairs[0]
    columns = jnp.arange(2 * BLOCKS, dtype=jnp.int32)
    inverse = jnp.sum(
        jnp.where(pairs[None, :] == columns[:, None], columns[None, :], 0), axis=1, dtype=jnp.int32
    )
    records = jnp.pad(
        coarse_pops.astype(F32).reshape(2, Q, LANES), ((0, 0), (0, 32 - Q), (0, 0))
    ).reshape(ROWS, LANES)

    shape = jax.ShapeDtypeStruct
    collided, edge_y, edge_z, edge_yz = pl.pallas_call(
        collide_kernel,
        out_shape=(
            shape((2, Q * NX, LANES), F32),
            shape((2, NX, LANES), F32),
            shape((2, NX, LANES), F32),
            shape((NX, LANES), F32),
        ),
        in_specs=[VMEM, VMEM, SMEM],
        out_specs=(VMEM,) * 4,
        compiler_params=params(),
        name="collide",
    )(populations, solid_mask.reshape(2 * NX, LANES), relax_rates)

    edge_y = swapped(edge_y, 1)
    edge_z = swapped(edge_z, 2)
    edge_yz = swapped(edge_yz, 3)

    base, right, left, payload = pl.pallas_call(
        stream_kernel,
        out_shape=(
            shape((Q, NX * 256), F32),
            shape((32, 256), F32),
            shape((32, 256), F32),
            shape((PLANE, 2 * ROWS, LANES), F32),
        ),
        grid_spec=pltpu.PrefetchScalarGridSpec(
            num_scalar_prefetch=1,
            grid=(1,),
            in_specs=[
                whole(2, Q * NX, LANES),
                whole(2, NX, LANES),
                whole(2, NX, LANES),
                whole(NX, LANES),
                whole(ROWS, LANES),
                by_side(256, 128),
            ],
            out_specs=(
                whole(Q, NX * 256),
                whole(32, 256),
                whole(32, 256),
                whole(PLANE, 2 * ROWS, LANES),
            ),
            scratch_shapes=[pltpu.VMEM((2, PITCH * 32, LANES), F32)],
        ),
        compiler_params=params(),
        name="stream",
    )(position, collided, edge_y, edge_z, edge_yz, records, jnp.asarray(pools, BF16))

    ring = [(i, (i + 1) % BLOCKS) for i in range(BLOCKS)]
    right = lax.ppermute(right, "blocks", ring)
    left = lax.ppermute(left, "blocks", [(b, a) for a, b in ring])

    near = [[PLANE * i + j for j in range(PLANE)] for i in range(PLANE)]
    far = [[PLANE * j + i for j in range(PLANE)] for i in range(PLANE)]
    payload = lax.all_to_all(payload, "blocks", 0, 0, axis_index_groups=near, tiled=True)
    payload = pl.pallas_call(
        route_kernel,
        out_shape=shape((PLANE, 2 * ROWS, LANES), F32),
        in_specs=[SMEM, SMEM, VMEM],
        out_specs=VMEM,
        compiler_params=params(),
        name="route",
    )(pairs, inverse, payload)
    payload = lax.all_to_all(payload, "blocks", 0, 0, axis_index_groups=far, tiled=True)

    lines = np.tile(np.repeat(interp_table(), HALF, axis=1), (1, 2))
    return pl.pallas_call(
        finish_kernel,
        out_shape=(shape((1, Q, NX * 256), F32), shape((1, 2, Q * LANES), F32)),
        grid_spec=pltpu.PrefetchScalarGridSpec(
            num_scalar_prefetch=3,
            grid=(1,),
            in_specs=[
                whole(Q, NX * 256),
                whole(32, 256),
                whole(32, 256),
                whole(PLANE, 2 * ROWS, LANES),
                whole(ROWS, LANES),
                whole(EDGE, LANES),
                by_side(256, 512),
                by_side(128, 384),
                by_side(64, 256),
                by_side(64, 128),
            ],
            out_specs=(whole(1, Q, NX * 256), whole(1, 2, Q * LANES)),
        ),
        compiler_params=params(),
        name="finish",
    )(
        position,
        pairs,
        inverse,
        base,
        right,
        left,
        payload,
        records,
        jnp.asarray(lines, F32),
        jnp.asarray(ghosts, BF16),
        jnp.asarray(coarse, BF16),
        jnp.asarray(cell_masks, F32),
        jnp.asarray(pop_masks, F32),
    )


def solution(mesh):
    placed = (
        P("group", None, "blocks"),
        P("group", "blocks"),
        P(),
        P("group", "blocks", None),
        P("group", None),
    )
    return jax.shard_map(
        body,
        mesh=mesh,
        in_specs=placed,
        out_specs=(P("group", None, "blocks"), P("group", "blocks", None)),
        check_vma=False,
    )
```

profile of v0, /device:TPU:1, one launch (start us, length us, event | category | flops | bytes accessed | tf_op | source)
XLA Modules:
  0.0 62.3 jit_solution(5260085573228912175)
XLA Ops:
  0.6 0.0 copy-start.5
  0.6 1.7 %copy.17.g_ref = f32[1,27,8192]{2,1,0:T(8,128)S(1)} copy(f32[1,27,8192]{2,0,1:T(1,128)} %param.11) | data formatting | bytes 1769472 | tf_op args[0]
  2.3 0.0 copy-start.8
  2.4 0.0 copy-done.5
  2.4 0.6 %copy-done.8 = f32[27]{0:T(128)S(1)} copy-done((f32[27]{0:T(128)S(1)}, f32[27]{0:T(128)}, u32[]{:S(2)}) %copy-start.8) | copy-done | bytes 132
  3.0 0.0 copy-start.9
  3.0 0.0 copy-start.2
  3.0 1.9 %collide.1 = (f32[2,864,128]{2,1,0:T(8,128)S(1)}, f32[2,32,128]{2,1,0:T(8,128)S(1)}, f32[2,32,128]{2,1,0:T(8,128)S(1)}, f32[32,128]{1,0:T(8,128)S(1)}) custom-call(f32[1,27,8192]{2,1,0:T(8,128)S(1)} %copy.17.g_ref, s32[64,128]{1,0:T(8,128)S(1)} %bitcast.6, f32[27]{0:T(128)S(1)} %copy-done.8), custom_call_target="tpu_custom_call" | custom-call | tf_op jit(solution)/shard_map/collide/pallas_call | solution.py:490
  4.9 3.4 %collective-permute-start.2 = (f32[32,128]{1,0:T(8,128)S(1)}, f32[32,128]{1,0:T(8,128)S(1)}, u32[]{:S(2)}, u32[]{:S(2)}) collective-permute-start(f32[32,128]{1,0:T(8,128)S(1)} %get-tuple-element.13), channel_id=1, source_target_pairs={{0,3},{1,2},{2,1},{3,0},{4,7},{5,6},{6,5},{7,4},{8,11},{9,10},{10,... | collective-permute-start | bytes 49160 | tf_op jit(solution)/shard_map/ppermute | solution.py:474
  8.3 0.0 collective-permute-start
  8.3 1.3 %collective-permute-start.1 = (f32[2,32,128]{2,1,0:T(8,128)S(1)}, f32[2,32,128]{2,1,0:T(8,128)S(1)}, u32[]{:S(2)}, u32[]{:S(2)}) collective-permute-start(f32[2,32,128]{2,1,0:T(8,128)S(1)} %get-tuple-element.12), channel_id=1, source_target_pairs={{0,2},{1,3},{2,0},{3,1},{4,6},{5,7},{6,4},{7,5},{8,10},{9,11},{10,... | collective-permute-start | bytes 98312 | tf_op jit(solution)/shard_map/ppermute | solution.py:474
  9.6 0.0 copy-done.9
  9.7 0.0 collective-permute-done.2.e_ref
  9.7 1.4 %collective-permute-done.y_ref = f32[2,32,128]{2,1,0:T(8,128)S(1)} collective-permute-done((f32[2,32,128]{2,1,0:T(8,128)S(1)}, f32[2,32,128]{2,1,0:T(8,128)S(1)}, u32[]{:S(2)}, u32[]{:S(2)}) %collective-permute-start) | collective-permute-done | bytes 32800 | tf_op jit(solution)/shard_map/ppermute | solution.py:474
  11.1 1.5 %collective-permute-done.1.z_ref = f32[2,32,128]{2,1,0:T(8,128)S(1)} collective-permute-done((f32[2,32,128]{2,1,0:T(8,128)S(1)}, f32[2,32,128]{2,1,0:T(8,128)S(1)}, u32[]{:S(2)}, u32[]{:S(2)}) %collective-permute-start.1) | collective-permute-done | bytes 32800 | tf_op jit(solution)/shard_map/ppermute | solution.py:474
  12.6 0.0 copy-done.2
  12.6 2.2 %stream.1 = (f32[27,8192]{1,0:T(8,128)S(1)}, f32[32,256]{1,0:T(8,128)}, f32[32,256]{1,0:T(8,128)S(1)}, f32[8,128,128]{2,1,0:T(8,128)}) custom-call(s32[1]{0:T(128)} %bitcast.q_ref, f32[2,864,128]{2,1,0:T(8,128)S(1)} %get-tuple-element.10.w_ref, f32[2,32,128]{2,1,0:T(8,128)S(1)} %collective-permute-done.y_ref, ...), custom_call_target="tpu_custom_call" | custom-call | tf_op jit(solution)/shard_map/stream/pallas_call | solution.py:508
  14.8 6.8 %all-to-all-start = ((f32[8,128,128]{2,1,0:T(8,128)}), f32[8,128,128]{2,1,0:T(8,128)S(1)}, u32[]{:S(2)}, u32[]{:S(2)}) async-start(f32[8,128,128]{2,1,0:T(8,128)} %get-tuple-element.17), calls=%async_computation | async-start | bytes 1048576 | tf_op jit(solution)/shard_map/all_to_all | solution.py:545
  21.6 0.0 copy-start.7
  21.6 0.7 %copy-done.7 = s32[1,128]{1,0:T(1,128)S(1)} copy-done((s32[1,128]{1,0:T(1,128)S(1)}, s32[1,128]{1,0:T(1,128)}, u32[]{:S(2)}) %copy-start.7) | copy-done | bytes 536
  22.3 0.1 select_reduce_fusion.inverse_ref
  22.4 0.0 copy-start
  22.4 8.7 %all-to-all-done.in_ref = f32[8,128,128]{2,1,0:T(8,128)S(1)} async-done(((f32[8,128,128]{2,1,0:T(8,128)}), f32[8,128,128]{2,1,0:T(8,128)S(1)}, u32[]{:S(2)}, u32[]{:S(2)}) %all-to-all-start) | async-done | bytes 524320 | tf_op jit(solution)/shard_map/all_to_all | solution.py:545
  31.1 1.4 %route.1 = f32[8,128,128]{2,1,0:T(8,128)} custom-call(s32[128]{0:T(128)S(1)} %bitcast.8, s32[128]{0:T(128)S(1)} %select_reduce_fusion.inverse_ref, f32[8,128,128]{2,1,0:T(8,128)S(1)} %all-to-all-done.in_ref), custom_call_target="tpu_custom_call" | custom-call | tf_op jit(solution)/shard_map/route/pallas_call | solution.py:546
  32.5 0.0 copy-start.1
  32.5 0.0 copy-start.3
  32.5 0.0 copy-start.4
  32.5 0.0 copy-start.6
  32.5 8.3 %all-to-all-start.1 = ((f32[8,128,128]{2,1,0:T(8,128)}), f32[8,128,128]{2,1,0:T(8,128)S(1)}, u32[]{:S(2)}, u32[]{:S(2)}) async-start(f32[8,128,128]{2,1,0:T(8,128)} %route.1), calls=%async_computation.1 | async-start | bytes 1048576 | tf_op jit(solution)/shard_map/all_to_all | solution.py:554
  40.8 1.3 %collective-permute-start.3 = (f32[32,256]{1,0:T(8,128)}, f32[32,256]{1,0:T(8,128)S(1)}, u32[]{:S(2)}, u32[]{:S(2)}) collective-permute-start(f32[32,256]{1,0:T(8,128)} %get-tuple-element.15), channel_id=1, source_target_pairs={{0,4},{4,8},{8,12},{12,16},{16,20},{20,24},{24,28},{28,32},{32,36}... | collective-permute-start | bytes 98312 | tf_op jit(solution)/shard_map/ppermute | solution.py:540
  42.1 0.0 collective-permute-start.4
  42.2 1.3 %collective-permute-done.3.right_ref = f32[32,256]{1,0:T(8,128)S(1)} collective-permute-done((f32[32,256]{1,0:T(8,128)}, f32[32,256]{1,0:T(8,128)S(1)}, u32[]{:S(2)}, u32[]{:S(2)}) %collective-permute-start.3) | collective-permute-done | bytes 32800 | tf_op jit(solution)/shard_map/ppermute | solution.py:540
  43.5 2.3 %collective-permute-done.4.left_ref = f32[32,256]{1,0:T(8,128)S(1)} collective-permute-done((f32[32,256]{1,0:T(8,128)S(1)}, f32[32,256]{1,0:T(8,128)S(1)}, u32[]{:S(2)}, u32[]{:S(2)}) %collective-permute-start.4) | collective-permute-done | bytes 32800 | tf_op jit(solution)/shard_map/ppermute | solution.py:541
  45.8 12.6 %all-to-all-done.1.in_ref = f32[8,128,128]{2,1,0:T(8,128)S(1)} async-done(((f32[8,128,128]{2,1,0:T(8,128)}), f32[8,128,128]{2,1,0:T(8,128)S(1)}, u32[]{:S(2)}, u32[]{:S(2)}) %all-to-all-start.1) | async-done | bytes 524320 | tf_op jit(solution)/shard_map/all_to_all | solution.py:554
  58.4 0.0 copy-done
  58.4 0.0 copy-done.1
  58.4 0.0 copy-done.3
  58.4 0.0 copy-done.4
  58.4 0.0 copy-done.6
  58.4 2.1 %finish.1 = (f32[1,27,8192]{2,1,0:T(8,128)S(1)}, f32[1,2,3456]{2,1,0:T(2,128)}) custom-call(s32[1]{0:T(128)} %bitcast.q_ref, s32[128]{0:T(128)S(1)} %bitcast.9, s32[128]{0:T(128)S(1)} %select_reduce_fusion.inverse_ref, f32[27,8192]{1,0:T(8,128)S(1)} %get-tuple-element.14.base_ref, f32[32,256]{1,0:T(8,128)S(1)} %collective-permute-done.3.right_ref, ...), custom_call_target="tpu_custom_call" | custom-call | tf_op jit(solution)/shard_map/finish/pallas_call | solution.py:557
  60.5 1.8 %copy.18 = f32[1,27,8192]{2,0,1:T(1,128)} copy(f32[1,27,8192]{2,1,0:T(8,128)S(1)} %get-tuple-element.22) | data formatting | bytes 1769472 | tf_op jit(solution)/shard_map/finish/pallas_call | solution.py:557
  (3 shorter events, 0.1 us)
Async XLA Ops:
  0.6 1.7 %copy-start.5 = (s32[1,8192]{1,0:T(1,128)S(1)}, s32[1,8192]{1,0:T(1,128)}, u32[]{:S(2)}) copy-start(s32[1,8192]{1,0:T(1,128)} %param.12) | copy-start | bytes 98308
  2.3 0.7 %copy-start.8 = (f32[27]{0:T(128)S(1)}, f32[27]{0:T(128)}, u32[]{:S(2)}) copy-start(f32[27]{0:T(128)} %rates_ref.1) | copy-start | bytes 328
  3.0 6.6 %copy-start.9 = (bf16[1,2,3456]{2,1,0:T(2,128)(2,1)S(1)}, bf16[1,2,3456]{2,1,0:T(2,128)(2,1)}, u32[]{:S(2)}) copy-start(bf16[1,2,3456]{2,1,0:T(2,128)(2,1)} %param.14) | copy-start | bytes 41476
  3.0 9.6 %copy-start.2 = (bf16[4,256,128]{2,1,0:T(8,128)(2,1)S(1)}, bf16[4,256,128]{2,1,0:T(8,128)(2,1)}, u32[]{:S(2)}) copy-start(bf16[4,256,128]{2,1,0:T(8,128)(2,1)} %constant.21.clone.pool_ref) | copy-start | bytes 786436
  4.9 4.7 %collective-permute-start.2 = (f32[32,128]{1,0:T(8,128)S(1)}, f32[32,128]{1,0:T(8,128)S(1)}, u32[]{:S(2)}, u32[]{:S(2)}) collective-permute-start(f32[32,128]{1,0:T(8,128)S(1)} %get-tuple-element.13), channel_id=1, source_target_pairs={{0,3},{1,2},{2,1},{3,0},{4,7},{5,6},{6,5},{7,4},{8,11},{9,10},{10,... | collective-permute-start | bytes 49160 | tf_op jit(solution)/shard_map/ppermute | solution.py:474
  8.3 2.8 %collective-permute-start = (f32[2,32,128]{2,1,0:T(8,128)S(1)}, f32[2,32,128]{2,1,0:T(8,128)S(1)}, u32[]{:S(2)}, u32[]{:S(2)}) collective-permute-start(f32[2,32,128]{2,1,0:T(8,128)S(1)} %get-tuple-element.11), channel_id=1, source_target_pairs={{0,1},{1,0},{2,3},{3,2},{4,5},{5,4},{6,7},{7,6},{8,9},{9,8},{10,11... | collective-permute-start | bytes 98312 | tf_op jit(solution)/shard_map/ppermute | solution.py:474
  8.3 4.3 %collective-permute-start.1 = (f32[2,32,128]{2,1,0:T(8,128)S(1)}, f32[2,32,128]{2,1,0:T(8,128)S(1)}, u32[]{:S(2)}, u32[]{:S(2)}) collective-permute-start(f32[2,32,128]{2,1,0:T(8,128)S(1)} %get-tuple-element.12), channel_id=1, source_target_pairs={{0,2},{1,3},{2,0},{3,1},{4,6},{5,7},{6,4},{7,5},{8,10},{9,11},{10,... | collective-permute-start | bytes 98312 | tf_op jit(solution)/shard_map/ppermute | solution.py:474
  14.8 16.3 %all-to-all-start = ((f32[8,128,128]{2,1,0:T(8,128)}), f32[8,128,128]{2,1,0:T(8,128)S(1)}, u32[]{:S(2)}, u32[]{:S(2)}) async-start(f32[8,128,128]{2,1,0:T(8,128)} %get-tuple-element.17), calls=%async_computation | async-start | bytes 1048576 | tf_op jit(solution)/shard_map/all_to_all | solution.py:545
  21.6 0.7 %copy-start.7 = (s32[1,128]{1,0:T(1,128)S(1)}, s32[1,128]{1,0:T(1,128)}, u32[]{:S(2)}) copy-start(s32[1,128]{1,0:T(1,128)} %param.15) | copy-start | bytes 1540
  22.4 36.0 %copy-start = (bf16[4,256,512]{2,1,0:T(8,128)(2,1)S(1)}, bf16[4,256,512]{2,1,0:T(8,128)(2,1)}, u32[]{:S(2)}) copy-start(bf16[4,256,512]{2,1,0:T(8,128)(2,1)} %constant.23.clone.ghost_ref) | copy-start | bytes 3145732
  32.5 25.9 %copy-start.1 = (bf16[4,128,384]{2,1,0:T(8,128)(2,1)S(1)}, bf16[4,128,384]{2,1,0:T(8,128)(2,1)}, u32[]{:S(2)}) copy-start(bf16[4,128,384]{2,1,0:T(8,128)(2,1)} %constant.24.clone.coarse_ref) | copy-start | bytes 1179652
  32.5 25.9 %copy-start.3 = (f32[4,64,256]{2,1,0:T(8,128)S(1)}, f32[4,64,256]{2,1,0:T(8,128)}, u32[]{:S(2)}) copy-start(f32[4,64,256]{2,1,0:T(8,128)} %constant.25.clone.cell_ref) | copy-start | bytes 786436
  32.5 25.9 %copy-start.4 = (f32[4,64,128]{2,1,0:T(8,128)S(1)}, f32[4,64,128]{2,1,0:T(8,128)}, u32[]{:S(2)}) copy-start(f32[4,64,128]{2,1,0:T(8,128)} %constant.26.clone.pop_ref) | copy-start | bytes 393220
  32.5 25.9 %copy-start.6 = (f32[16,128]{1,0:T(8,128)S(1)}, f32[16,128]{1,0:T(8,128)}, u32[]{:S(2)}) copy-start(f32[16,128]{1,0:T(8,128)} %constant.22.clone.line_ref) | copy-start | bytes 24580
  32.5 25.9 %all-to-all-start.1 = ((f32[8,128,128]{2,1,0:T(8,128)}), f32[8,128,128]{2,1,0:T(8,128)S(1)}, u32[]{:S(2)}, u32[]{:S(2)}) async-start(f32[8,128,128]{2,1,0:T(8,128)} %route.1), calls=%async_computation.1 | async-start | bytes 1048576 | tf_op jit(solution)/shard_map/all_to_all | solution.py:554
  40.8 2.7 %collective-permute-start.3 = (f32[32,256]{1,0:T(8,128)}, f32[32,256]{1,0:T(8,128)S(1)}, u32[]{:S(2)}, u32[]{:S(2)}) collective-permute-start(f32[32,256]{1,0:T(8,128)} %get-tuple-element.15), channel_id=1, source_target_pairs={{0,4},{4,8},{8,12},{12,16},{16,20},{20,24},{24,28},{28,32},{32,36}... | collective-permute-start | bytes 98312 | tf_op jit(solution)/shard_map/ppermute | solution.py:540
  42.1 3.6 %collective-permute-start.4 = (f32[32,256]{1,0:T(8,128)S(1)}, f32[32,256]{1,0:T(8,128)S(1)}, u32[]{:S(2)}, u32[]{:S(2)}) collective-permute-start(f32[32,256]{1,0:T(8,128)S(1)} %get-tuple-element.16), channel_id=1, source_target_pairs={{4,0},{8,4},{12,8},{16,12},{20,16},{24,20},{28,24},{32,28},{36,32}... | collective-permute-start | bytes 98312 | tf_op jit(solution)/shard_map/ppermute | solution.py:541
where the time goes:
time: 62.6 us; the launch traced here: 62.3 us
  waiting for transfers between devices  27.9 us (45%)
  starting transfers between devices  21.1 us (34%)
  Pallas kernels  7.58 us (12%)
  local copies, waits for them, and re-layouts  4.89 us (8%)
  between operations  0.73 us (1%)
    all_to_all x1, waiting for transfers between devices, body(): lax.all_to_all(payload, 'blocks', 0, 0, axis_index_groups=far, tiled=True)  12.6 us
    all_to_all x1, waiting for transfers between devices, body(): lax.all_to_all(payload, 'blocks', 0, 0, axis_index_groups=near, tiled=True)  8.71 us
    all_to_all x1, starting transfers between devices, body(): lax.all_to_all(payload, 'blocks', 0, 0, axis_index_groups=far, tiled=True)  8.33 us
    all_to_all x1, starting transfers between devices, body(): lax.all_to_all(payload, 'blocks', 0, 0, axis_index_groups=near, tiled=True)  6.77 us
    ppermute x3, starting transfers between devices, swapped(): return lax.ppermute(block, 'group', [(i, i ^ bits) for i in range(4)])  4.68 us
    unnamed x21, local copies, waits for them, and re-layouts  3.03 us
    ppermute x3, waiting for transfers between devices, swapped(): return lax.ppermute(block, 'group', [(i, i ^ bits) for i in range(4)])  2.93 us
    ppermute x1, waiting for transfers between devices, body(): left = lax.ppermute(left, 'blocks', [(b, a) for a, b in ring])  2.29 us
  transfers between devices with their start and end apart: 7, of which 6 were waited for; matrix products, arithmetic and copies ran while one was open for 0% of the time, Pallas kernels for 0%

commit v1 on v0

v1 whole, which is shorter than its diff:
```python
import jax
import jax.numpy as jnp
import numpy as np
from jax import lax
from jax.experimental import pallas as pl
from jax.experimental.pallas import tpu as pltpu
from jax.sharding import PartitionSpec as P

Q = 27
EDGE = 16
HALF = 8
NX = 32
SPAN = 2 * NX
PITCH = SPAN + 16
FIRST = 8
LANES = 128
PLANE = 8
BLOCKS = PLANE * PLANE
LOW, HIGH, SHARED, CENTRE, RECORDS, ROWS = 54, 55, 56, 57, 58, 112
PAIRS = [(i // 9, i // 3 % 3, i % 3) for i in range(Q)]
F32 = jnp.float32
BF16 = jnp.bfloat16


def interp_table():
    fine = np.arange(EDGE)[:, None]
    coarse = np.arange(HALF)[None, :]
    raw = np.maximum(0.0, 1.0 - np.abs((fine - 0.5) / 2.0 - coarse))
    return raw / raw.sum(axis=1, keepdims=True)


def share_table(pool, in_y, in_z, out_y, out_z):
    layer = np.zeros((Q, 2, 8, 8))
    for i, (a, b, c) in enumerate(PAIRS):
        valid = np.ones((16, 16))
        if b == in_y:
            valid[out_y, :] = 0.0
        if c == in_z:
            valid[:, out_z] = 0.0
        layer[i] = (valid.reshape(256) @ pool).reshape(2, 8, 8)
    share = np.zeros((64, 2, 8, 8))
    for i, (a, b, c) in enumerate(PAIRS):
        for column in range(2):
            share[27 * column + i] = 2.0 * layer[i]
        if a == 2:
            share[i, :, 0, :] = layer[i, :, 0, :]
            row, at = (LOW, i - 18) if i < 26 else (SHARED, 7)
            share[row, :, at, :] = layer[i, :, 0, :]
        if a == 0:
            share[27 + i, :, 7, :] = layer[i, :, 0, :]
            row, at = (HIGH, i) if i < 8 else (SHARED, 0)
            share[row, :, at, :] = layer[i, :, 0, :]
    return share.reshape(64, 128)


def side_tables():
    interp = interp_table()
    pair = interp[0::2] + interp[1::2]
    pools, shares, ghosts, coarse, pop_masks = [], [], [], [], []
    for q in range(4):
        side_y, side_z = q % 2, q // 2
        out_y, out_z = 15 * side_y, 15 * side_z
        next_y = 1 if side_y == 0 else 14
        next_z = 1 if side_z == 0 else 14
        in_y, in_z = 2 * (1 - side_y), 2 * (1 - side_z)
        pool = np.zeros((16, 16, 2, 8, 8))
        for s in range(16):
            pool[out_y, s, 0, :, s // 2] = 0.125
            pool[next_y, s, 0, :, s // 2] = 0.125
            pool[s, out_z, 1, :, s // 2] = 0.125
            pool[s, next_z, 1, :, s // 2] = 0.125
        pool = pool.reshape(256, 128)
        pools.append(pool)
        shares.append(share_table(pool, in_y, in_z, out_y, out_z))
        ghost = np.zeros((2, 8, 8, 2, 16, 16))
        for s in range(16):
            ghost[0, :, :, 0, out_y, s] = interp[s][None, :]
            ghost[1, :, :, 1, s, out_z] = interp[s][None, :]
        ghost = ghost.reshape(128, 512)
        ghosts.append(np.concatenate([ghost, ghost], 0))
        part = np.zeros((2, 8, 8, 3, 2, 8, 8))
        pair_y, pair_z = out_y // 2, out_z // 2
        for a in range(8):
            for b in range(8):
                part[0, :, :, 0, 0, a, b] = np.outer(pair[a], pair[b])
                part[1, :, :, 1, 1, a, b] = np.outer(pair[a], pair[b])
            part[0, :, :, 0, 1, a, pair_y] = np.outer(pair[a], interp[out_z] + interp[next_z])
            part[1, :, :, 1, 0, a, pair_z] = np.outer(pair[a], interp[out_y] + interp[next_y])
            part[1, :, :, 2, 0, a, pair_z] = np.outer(pair[a], interp[out_y])
            part[1, :, :, 2, 1, a, pair_y] = np.outer(pair[a], interp[out_y])
        coarse.append(0.125 * part.reshape(128, 384))
        pops = np.zeros((2, 32, 128))
        for i, (a, b, c) in enumerate(PAIRS):
            pops[0, i] = float(b == in_y)
            pops[1, i] = float(c == in_z)
        pop_masks.append(pops.reshape(64, 128))
    return [np.stack(table) for table in (pools, shares, ghosts, coarse, pop_masks)]


def sides():
    position = lax.axis_index("group")
    return position & 1, position >> 1


def geometry():
    side_y, side_z = sides()
    return 1 - side_y, 112 * (1 - side_y), 15 * (1 - side_z)


def ids(shape, dim):
    return lax.broadcasted_iota(jnp.int32, shape, dim)


def rolled(value, shift):
    return pltpu.roll(value, shift, 1)


def split_bf16(value):
    high = value.astype(BF16)
    return high, (value - high.astype(F32)).astype(BF16)


def dot(left, right):
    return jnp.dot(left, right, preferred_element_type=F32)


def along(table, axis, line):
    out = {}
    for first in range(3):
        for second in range(3):
            keys = []
            for third in range(3):
                key = [first, second]
                key.insert(axis, third)
                keys.append(tuple(key))
            values = line(*[table[key] for key in keys])
            for key, value in zip(keys, values):
                out[key] = value
    return out


def line_moments(low, mid, high):
    both = low + high
    return both + 4.0 * mid, high - low, both


def line_inverse(zeroth, first, second):
    return second - first, zeroth - 0.5 * second, first + second


def collide_cells(current, rates):
    table = {PAIRS[i]: current[i] for i in range(Q)}
    moments = table
    for axis in range(3):
        moments = along(moments, axis, line_moments)
    density = moments[0, 0, 0]
    inverse = 1.0 / density
    flow = [moments[1, 0, 0], moments[0, 1, 0], moments[0, 0, 1]]
    speed = [part * inverse for part in flow]
    carried = [density * part for part in speed]
    square = [carried[axis] * speed[axis] for axis in range(3)]
    third = density * (1.0 / 3.0)
    relaxed = {}
    for index, key in enumerate(PAIRS):
        ones = [axis for axis in range(3) if key[axis] == 1]
        twos = [axis for axis in range(3) if key[axis] == 2]
        scale = (1.0 / 3.0) ** len(twos)
        if len(ones) == 0:
            if len(twos) == 0:
                balance = density
            elif len(twos) == 1:
                balance = third + square[twos[0]]
            elif len(twos) == 2:
                balance = (third + square[twos[0]] + square[twos[1]]) * (1.0 / 3.0)
            else:
                balance = (third + square[0] + square[1] + square[2]) * (1.0 / 9.0)
        elif len(ones) == 1:
            balance = carried[ones[0]] * scale if twos else carried[ones[0]]
        elif len(ones) == 2:
            balance = carried[ones[0]] * speed[ones[1]]
            balance = balance * scale if twos else balance
        else:
            balance = None
        rest = moments[key] if balance is None else moments[key] - balance
        relaxed[key] = rates[index] * rest
    change = relaxed
    for axis in range(3):
        change = along(change, axis, line_inverse)
    return [current[i] - change[PAIRS[i]] for i in range(Q)]


def collide_kernel(g_ref, solid_ref, rates_ref, w_ref, y_ref, z_ref):
    side_y, side_z = sides()
    rates = []
    for i in range(Q):
        scale = 1.0 / 216.0
        for part in PAIRS[i]:
            scale *= 1.5 if part == 0 else 3.0
        rates.append(rates_ref[i] * scale)

    def chunk(index, carry):
        row = pl.multiple_of(8 * index, 8)
        current = [g_ref[pl.ds(SPAN * i + row, 8), :] for i in range(Q)]
        solid = solid_ref[pl.ds(row, 8), :] == 1
        collided = collide_cells(current, rates)
        for i in range(Q):
            w_ref[pl.ds(SPAN * i + row, 8), :] = jnp.where(solid, current[Q - 1 - i], collided[i])
        return carry

    lax.fori_loop(0, SPAN // 8, chunk, 0)

    send_y, send_z = 2 * (1 - side_y), 2 * (1 - side_z)
    tile, base, inner = geometry()
    lanes = ids((NX, LANES), 1)
    packed = [jnp.zeros((NX, LANES), F32), jnp.zeros((NX, LANES), F32)]
    for k in range(9):
        index = 9 * (k // 3) + 3 * send_y + k % 3
        value = w_ref[pl.ds(index * SPAN + tile, NX, stride=2), :]
        value = rolled(value, (16 * (k % 8) - base) & 127)
        packed[k // 8] = jnp.where(lanes >> 4 == k % 8, value, packed[k // 8])
    y_ref[0] = packed[0]
    y_ref[1] = packed[1]
    lanes = ids((SPAN, LANES), 1)
    packed_z = jnp.zeros((SPAN, LANES), F32)
    for k in range(9):
        index = 9 * (k // 3) + 3 * (k % 3) + send_z
        value = w_ref[pl.ds(pl.multiple_of(index * SPAN, SPAN), SPAN), :]
        packed_z = jnp.where(lanes & 15 == k, rolled(value, (k - inner) & 127), packed_z)
    z_ref[...] = packed_z


def moved(value, b, shift):
    value = rolled(value, shift)
    if b == 1:
        return value
    rows, lanes = ids(value.shape, 0), ids(value.shape, 1)
    if b == 2:
        other = pltpu.roll(value, 1, 0)
        return jnp.where(lanes >= 16, value, jnp.where(rows & 1 == 1, other, 0.0))
    other = pltpu.roll(value, value.shape[0] - 1, 0)
    return jnp.where(lanes < 112, value, jnp.where(rows & 1 == 0, other, 0.0))


def z_inside(lanes, c):
    return lanes & 15 <= 14 if c == 0 else lanes & 15 >= 1


def stream_kernel(w_ref, t_ref, e_ref):
    lanes = ids((8, LANES), 1)
    zeros = jnp.zeros((8, LANES), F32)
    for i, (a, b, c) in enumerate(PAIRS):
        for row in (0, 8, SPAN, SPAN + 8):
            t_ref[pl.ds(PITCH * i + row, 8), :] = zeros
        shift = (16 * (b - 1) + c - 1) % 128
        for row in range(0, SPAN, 8):
            value = w_ref[pl.ds(SPAN * i + row, 8), :]
            if shift:
                value = moved(value, b, shift)
            if c != 1:
                value = jnp.where(z_inside(lanes, c), value, 0.0)
            t_ref[pl.ds(PITCH * i + FIRST + row + 2 * (a - 1), 8), :] = value

    side_y, side_z = sides()
    tile, base, inner = geometry()
    lanes = ids((NX, LANES), 1)
    packed = jnp.zeros((NX, LANES), F32)
    for a in range(3):
        index = 9 * a + 6 * (1 - side_y) + 2 * (1 - side_z)
        value = w_ref[pl.ds(index * SPAN + tile, NX, stride=2), :]
        packed = jnp.where(lanes == a, rolled(value, (a - base - inner) & 127), packed)
    e_ref[...] = packed


def halo_kernel(
    q_ref, t_ref, y_ref, z_ref, e_ref, rec_ref, pool_ref, share_ref,
    out_ref, right_ref, left_ref, pay_ref, edge_ref,
):
    del q_ref, t_ref
    side_y, side_z = sides()
    halo_y, halo_z = 2 * side_y, 2 * side_z
    tile, base, inner = geometry()
    edge_ref[...] = e_ref[...]

    lanes = ids((NX, LANES), 1)
    row_mask = lanes >> 4 == base >> 4
    for k in range(9):
        a, c = k // 3, k % 3
        value = rolled(y_ref[k // 8], (base - 16 * (k % 8) + c - 1) & 127)
        mask = row_mask if c == 1 else row_mask & z_inside(lanes, c)
        index = 9 * a + 3 * halo_y + c
        rows = pl.ds(PITCH * index + FIRST + 2 * (a - 1) + tile, NX, stride=2)
        out_ref[rows, :] = out_ref[rows, :] + jnp.where(mask, value, 0.0)
    lanes = ids((8, LANES), 1)
    for k in range(9):
        a, b = k // 3, k % 3
        shift = (inner - k + 16 * (b - 1)) & 127
        index = 9 * a + 3 * b + halo_z
        for row in range(0, SPAN, 8):
            value = moved(z_ref[pl.ds(row, 8), :], b, shift)
            rows = pl.ds(PITCH * index + FIRST + row + 2 * (a - 1), 8)
            out_ref[rows, :] = out_ref[rows, :] + jnp.where(lanes & 15 == inner, value, 0.0)

    for k in range(9):
        right_ref[8 * k : 8 * k + 8, :] = out_ref[pl.ds(PITCH * (18 + k) + FIRST + SPAN, 8), :]
        left_ref[8 * k : 8 * k + 8, :] = out_ref[pl.ds(PITCH * k, 8), :]

    row_8 = ids((8, LANES), 0)
    total = 8 * (2 * Q + 4)
    pooled = jnp.zeros((total, LANES), F32)
    for h in range(2):
        parts = []
        for i in range(Q):
            for s in range(2):
                row = PITCH * i + FIRST + NX * s + h
                parts.append(
                    out_ref[pl.ds(row, 8, stride=4), :] + out_ref[pl.ds(row + 2, 8, stride=4), :]
                )
        over, under = FIRST + SPAN + h, FIRST - 2 + h
        parts.append(out_ref[pl.ds(PITCH * 18 + over, 8, stride=PITCH), :])
        last = out_ref[pl.ds(PITCH * 19 + over, 8, stride=PITCH), :]
        parts.append(jnp.where(row_8 == 7, last, 0.0))
        parts.append(out_ref[pl.ds(under, 8, stride=PITCH), :])
        parts.append(out_ref[pl.ds(PITCH * 8 + under, 8, stride=PITCH), :])
        for part in split_bf16(jnp.concatenate(parts, 0)):
            pooled = pooled + dot(part, pool_ref[0, LANES * h : LANES * (h + 1), :])
    pooled = jnp.where(ids((total, LANES), 0) & 7 == ids((total, LANES), 1) >> 3 & 7, pooled, 0.0)
    target, block = ids((64, total), 0), ids((64, total), 1) >> 3
    second = (target >= Q).astype(jnp.int32)
    wanted = jnp.where(target < LOW, 2 * (target - Q * second) + second, -1)
    wanted = jnp.where(target == LOW, 54, jnp.where(target == HIGH, 56, wanted))
    chosen = (wanted == block) | ((target == SHARED) & ((block == 55) | (block == 57)))
    chosen = chosen.astype(F32).astype(BF16)
    routed = jnp.zeros((64, LANES), F32)
    for part in split_bf16(pooled):
        routed = routed + dot(chosen, part)

    share = share_ref[0]
    rows, lane_a = ids((64, LANES), 0), ids((64, LANES), 1) >> 3 & 7
    inside = rows < LOW
    held = jnp.sum(jnp.where(inside, routed, 0.0), axis=0, keepdims=True)
    held = jnp.sum(held, axis=1, keepdims=True)
    parts = jnp.sum(jnp.where(inside, share, 0.0), axis=0, keepdims=True)
    parts = jnp.sum(parts, axis=1, keepdims=True)
    centre = (held / parts).astype(BF16).astype(F32)
    routed = routed - centre * share
    is_centre = (rows == CENTRE) | ((rows == SHARED) & ((lane_a == 1) | (lane_a == 6)))
    routed = jnp.where(is_centre, centre, routed)
    payload = jnp.concatenate([routed[0:RECORDS], rec_ref[...]], 0).astype(BF16)
    for slot in range(PLANE):
        pay_ref[slot] = payload


def owner_of(pairs_ref, device):
    return pairs_ref[2 * device] >> 1


def route_kernel(
    pairs_ref, inverse_ref, in_ref, e_ref, right_in, left_in, out_ref, right_ref, left_ref
):
    place = lax.axis_index("blocks") & (PLANE - 1)
    rows, lane_a = ids((16, LANES), 0) + 48, ids((16, LANES), 1) >> 3 & 7
    from_low = (rows == LOW) | ((rows == SHARED) & (lane_a >= 4))
    from_high = (rows == HIGH) | ((rows == SHARED) & (lane_a < 4))
    for plane in range(PLANE):
        device = PLANE * plane + place
        owner = owner_of(pairs_ref, device)
        source = owner & (PLANE - 1)
        before = (owner - 1) & (PLANE - 1)
        after = (owner + 1) & (PLANE - 1)
        holder = owner_of(inverse_ref, device) & (PLANE - 1)
        out_ref[plane, 0:48] = in_ref[source, 0:48]
        mixed = in_ref[source, 48:64].astype(F32)
        mixed = jnp.where(rows >= RECORDS, in_ref[holder, 48:64].astype(F32), mixed)
        mixed = jnp.where(from_low, in_ref[before, 48:64].astype(F32), mixed)
        mixed = jnp.where(from_high, in_ref[after, 48:64].astype(F32), mixed)
        out_ref[plane, 48:64] = mixed.astype(BF16)
        out_ref[plane, 64:ROWS] = in_ref[holder, 64:ROWS]

    side_y, side_z = sides()
    tile, base, inner = geometry()
    right_ref[...] = right_in[...]
    left_ref[...] = left_in[...]
    corner = 8 * (6 * side_y + 2 * side_z)
    lanes = ids((1, LANES), 1)
    for ref, layer, a, row in ((right_ref, NX - 1, 2, 0), (left_ref, 0, 0, 6)):
        value = rolled(e_ref[layer : layer + 1, :], (base + inner - a) & 127)
        at = pl.ds(corner + row + tile, 1)
        ref[at, :] = ref[at, :] + jnp.where(lanes == base + inner, value, 0.0)


def finish_kernel(
    q_ref, pairs_ref, inverse_ref,
    t_ref, e_ref, right_ref, left_ref, in_ref, rec_ref, line_ref, share_ref, ghost_ref, coarse_ref, pop_ref,
    next_ref, update_ref,
    p_ref,
):
    del q_ref
    me = lax.axis_index("blocks")
    owner = owner_of(pairs_ref, me)
    before = (owner + BLOCKS - 1) & (BLOCKS - 1)
    after = (owner + 1) & (BLOCKS - 1)
    holder = owner_of(inverse_ref, me)
    side_y, side_z = sides()
    tile, base, inner = geometry()

    records = in_ref[holder >> 3].astype(F32)[RECORDS:ROWS]
    swap = (inverse_ref[2 * me] & 1) == 1
    p_ref[0:Q] = jnp.where(swap, records[Q:], records[:Q])
    p_ref[32 : 32 + Q] = jnp.where(swap, records[:Q], records[Q:])
    lines = line_ref[...]
    lanes = ids((NX, LANES), 1)
    for a in range(3):
        for b in range(3):
            scaled = []
            for c in range(3):
                i = 9 * a + 3 * b + c
                for s in range(2):
                    scaled.append(lines * p_ref[32 * s + i : 32 * s + i + 1, :])
            scaled = jnp.concatenate(scaled, 0)
            ghost = dot(jnp.concatenate(split_bf16(scaled), 1), ghost_ref[0])
            in_y = b == 2 * (1 - side_y)
            for c in range(3):
                i = 9 * a + 3 * b + c
                in_z = c == 2 * (1 - side_z)
                for h in range(2):
                    rows_y = ghost[NX * c : NX * (c + 1), LANES * h : LANES * (h + 1)]
                    rows_z = ghost[NX * c : NX * (c + 1), 256 + LANES * h : 256 + LANES * (h + 1)]
                    value = t_ref[pl.ds(PITCH * i + FIRST + h, NX, stride=2), :]
                    if c != 1:
                        value = value + jnp.where(in_z, rows_z, 0.0)
                    if b != 1:
                        outer = (lanes >> 4 == 7 * side_y) & (h == side_y) & in_y
                        value = jnp.where(outer, rows_y, value)
                    next_ref[pl.ds(SPAN * i + h, NX, stride=2), :] = value
    for k in range(9):
        rows = pl.ds(SPAN * (18 + k), 8)
        next_ref[rows, :] = next_ref[rows, :] + right_ref[8 * k : 8 * k + 8, :]
        rows = pl.ds(SPAN * k + SPAN - 8, 8)
        next_ref[rows, :] = next_ref[rows, :] + left_ref[8 * k : 8 * k + 8, :]
    for a in range(3):
        index = 9 * a + 6 * side_y + 2 * side_z
        low, high = (0, NX - (a - 1)) if a >= 1 else (1, NX)
        value = rolled(e_ref[low:high, :], (base + inner - a) & 127)
        value = jnp.where(lanes[low:high] == base + inner, value, 0.0)
        rows = pl.ds(SPAN * index + 2 * (low + a - 1) + tile, high - low, stride=2)
        next_ref[rows, :] = next_ref[rows, :] + value

    main = in_ref[owner >> 3].astype(F32)
    lower = in_ref[before >> 3, 48:64].astype(F32)
    upper = in_ref[after >> 3, 48:64].astype(F32)
    share = share_ref[0]
    main = main[0:LOW] + main[CENTRE : CENTRE + 1] * share[0:LOW]
    shared = SHARED - 48
    lane_1 = ids((1, LANES), 1)
    low_centre = jnp.sum(jnp.where(lane_1 == 48, lower[shared : shared + 1], 0.0), axis=1, keepdims=True)
    high_centre = jnp.sum(jnp.where(lane_1 == 8, upper[shared : shared + 1], 0.0), axis=1, keepdims=True)
    lower = lower + low_centre * share[48:64]
    upper = upper + high_centre * share[48:64]
    rows, lane_a = ids((32, LANES), 0), ids((32, LANES), 1) >> 3 & 7
    from_low = jnp.where(
        rows == 26,
        jnp.where(lane_a == 7, lower[shared : shared + 1], 0.0),
        jnp.where(rows - 18 == lane_a, lower[LOW - 48 : LOW - 47], 0.0),
    )
    from_high = jnp.where(
        rows == 8,
        jnp.where(lane_a == 0, upper[shared : shared + 1], 0.0),
        jnp.where(rows == lane_a, upper[HIGH - 48 : HIGH - 47], 0.0),
    )
    lane_in, lane_out = ids((LANES, LANES), 0), ids((LANES, LANES), 1)
    alike = (lane_in >> 6 == lane_out >> 6) & (lane_in & 7 == lane_out & 7)
    alike = alike.astype(F32).astype(BF16)
    edges = jnp.zeros((2 * 32, LANES), F32)
    for part in split_bf16(jnp.concatenate([from_low, from_high], 0)):
        edges = edges + dot(part, alike)
    column_0 = main[0:Q] + jnp.where(lane_a == 0, edges[0:32], 0.0)[0:Q]
    column_1 = main[Q : 2 * Q] + jnp.where(lane_a == HALF - 1, edges[32:64], 0.0)[0:Q]
    own = dot(rec_ref[...].astype(BF16), coarse_ref[0])
    in_y, in_z = pop_ref[0, 0:Q, :], pop_ref[0, 32 : 32 + Q, :]
    for t in range(2):
        part = own[Q * t : Q * t + Q]
        value = jnp.where((pairs_ref[2 * me + t] & 1) == 1, column_1, column_0)
        value = value + in_y * part[:, 0:128] + in_z * part[:, 128:256] - in_y * in_z * part[:, 256:384]
        for i in range(Q):
            update_ref[0, t : t + 1, LANES * i : LANES * (i + 1)] = value[i : i + 1]


VMEM = pl.BlockSpec(memory_space=pltpu.VMEM)
SMEM = pl.BlockSpec(memory_space=pltpu.SMEM)


def whole(*shape):
    return pl.BlockSpec(shape, lambda i, *scalars: (0,) * len(shape))


def by_side(*shape):
    return pl.BlockSpec((1, *shape), lambda i, side, *rest: (side[0],) + (0,) * len(shape))


def params():
    return pltpu.CompilerParams(vmem_limit_bytes=32 * 1024 * 1024)


def cost(flops, moved_bytes):
    return pl.CostEstimate(flops=flops, bytes_accessed=moved_bytes, transcendentals=0)


def swapped(block, bits):
    return lax.ppermute(block, "group", [(i, i ^ bits) for i in range(4)])


def body(populations, solid_mask, relax_rates, coarse_pops, interface_pairs):
    pools, shares, ghosts, coarse, pop_masks = side_tables()
    position = lax.axis_index("group").astype(jnp.int32).reshape(1)
    pairs = interface_pairs[0]
    columns = jnp.arange(2 * BLOCKS, dtype=jnp.int32)
    inverse = jnp.sum(
        jnp.where(pairs[None, :] == columns[:, None], columns[None, :], 0), axis=1, dtype=jnp.int32
    )
    records = coarse_pops.reshape(2 * Q, LANES).astype(F32)
    shares = jnp.asarray(shares, F32)

    shape = jax.ShapeDtypeStruct
    collided, edge_y, edge_z = pl.pallas_call(
        collide_kernel,
        out_shape=(
            shape((Q * SPAN, LANES), F32),
            shape((2, NX, LANES), F32),
            shape((SPAN, LANES), F32),
        ),
        in_specs=[VMEM, VMEM, SMEM],
        out_specs=(VMEM,) * 3,
        compiler_params=params(),
        name="collide",
    )(populations.reshape(Q * SPAN, LANES), solid_mask.reshape(SPAN, LANES), relax_rates)

    edge_y = swapped(edge_y, 1)
    edge_z = swapped(edge_z, 2)
    streamed, edge_yz = pl.pallas_call(
        stream_kernel,
        out_shape=(shape((Q * PITCH, LANES), F32), shape((NX, LANES), F32)),
        in_specs=[VMEM],
        out_specs=(VMEM,) * 2,
        compiler_params=params(),
        cost_estimate=cost(10_000_000, 8_000_000),
        name="stream",
    )(collided)

    streamed, right, left, payload, edge_yz = pl.pallas_call(
        halo_kernel,
        out_shape=(
            shape((Q * PITCH, LANES), F32),
            shape((72, LANES), F32),
            shape((72, LANES), F32),
            shape((PLANE, ROWS, LANES), BF16),
            shape((NX, LANES), F32),
        ),
        grid_spec=pltpu.PrefetchScalarGridSpec(
            num_scalar_prefetch=1,
            grid=(1,),
            in_specs=[VMEM, VMEM, VMEM, VMEM, VMEM, by_side(256, 128), by_side(64, 128)],
            out_specs=(VMEM,) * 5,
        ),
        input_output_aliases={1: 0},
        compiler_params=params(),
        name="halo",
    )(position, streamed, edge_y, edge_z, edge_yz, records, jnp.asarray(pools, BF16), shares)
    edge_yz = swapped(edge_yz, 3)

    near = [[PLANE * i + j for j in range(PLANE)] for i in range(PLANE)]
    far = [[PLANE * j + i for j in range(PLANE)] for i in range(PLANE)]
    payload = lax.all_to_all(payload, "blocks", 0, 0, axis_index_groups=near, tiled=True)
    payload, right, left = pl.pallas_call(
        route_kernel,
        out_shape=(
            shape((PLANE, ROWS, LANES), BF16),
            shape((72, LANES), F32),
            shape((72, LANES), F32),
        ),
        in_specs=[SMEM, SMEM, VMEM, VMEM, VMEM, VMEM],
        out_specs=(VMEM,) * 3,
        compiler_params=params(),
        name="route",
    )(pairs, inverse, payload, edge_yz, right, left)
    payload = lax.all_to_all(payload, "blocks", 0, 0, axis_index_groups=far, tiled=True)
    ring = [(i, (i + 1) % BLOCKS) for i in range(BLOCKS)]
    right = lax.ppermute(right, "blocks", ring)
    left = lax.ppermute(left, "blocks", [(b, a) for a, b in ring])

    lines = np.tile(np.repeat(interp_table(), HALF, axis=1), (1, 2))
    result, update = pl.pallas_call(
        finish_kernel,
        out_shape=(shape((Q * SPAN, LANES), F32), shape((1, 2, Q * LANES), F32)),
        grid_spec=pltpu.PrefetchScalarGridSpec(
            num_scalar_prefetch=3,
            grid=(1,),
            in_specs=[
                VMEM, VMEM, VMEM, VMEM, VMEM, VMEM, VMEM,
                by_side(64, 128), by_side(256, 512), by_side(128, 384), by_side(64, 128),
            ],
            out_specs=(VMEM,) * 2,
            scratch_shapes=[pltpu.VMEM((64, LANES), F32)],
        ),
        compiler_params=params(),
        name="finish",
    )(
        position, pairs, inverse,
        streamed, edge_yz, right, left, payload, records,
        jnp.asarray(lines, F32), shares, jnp.asarray(ghosts, BF16), jnp.asarray(coarse, BF16), jnp.asarray(pop_masks, F32),
    )
    return result.reshape(1, Q, SPAN * LANES), update


def solution(mesh):
    placed = (
        P("group", None, "blocks"),
        P("group", "blocks"),
        P(),
        P("group", "blocks", None),
        P("group", None),
    )
    return jax.shard_map(
        body,
        mesh=mesh,
        in_specs=placed,
        out_specs=(P("group", None, "blocks"), P("group", "blocks", None)),
        check_vma=False,
    )
```

time: 62.6 us -> 47.6 us (0.76)
  the two profiles are of different devices: /device:TPU:1 before, /device:TPU:4 now
where the time goes in v1:
time: 47.6 us; the launch traced here: 47.1 us
  starting transfers between devices  21.1 us (44%)
  waiting for transfers between devices  15.5 us (33%)
  Pallas kernels  6.44 us (14%)
  local copies, waits for them, and re-layouts  3.34 us (7%)
  between operations  0.72 us (2%)
    all_to_all x1, starting transfers between devices, body(): lax.all_to_all(payload, 'blocks', 0, 0, axis_index_groups=far, tiled=True)  8.46 us
    ppermute x3, waiting for transfers between devices, swapped(): return lax.ppermute(block, 'group', [(i, i ^ bits) for i in range(4)])  6.24 us
    ppermute x1, starting transfers between devices, body(): left = lax.ppermute(left, 'blocks', [(b, a) for a, b in ring])  5.06 us
    all_to_all x1, starting transfers between devices, body(): lax.all_to_all(payload, 'blocks', 0, 0, axis_index_groups=near, tiled=True)  4.47 us
    all_to_all x1, waiting for transfers between devices, body(): lax.all_to_all(payload, 'blocks', 0, 0, axis_index_groups=near, tiled=True)  3.45 us
    ppermute x1, waiting for transfers between devices, body(): right = lax.ppermute(right, 'blocks', ring)  3.18 us
    ppermute x3, starting transfers between devices, swapped(): return lax.ppermute(block, 'group', [(i, i ^ bits) for i in range(4)])  3.06 us
    unnamed x20, local copies, waits for them, and re-layouts  2.61 us
  transfers between devices with their start and end apart: 7, of which 6 were waited for; matrix products, arithmetic and copies ran while one was open for 2% of the time, Pallas kernels for 1%

profile of v1, /device:TPU:4, one launch (start us, length us, event | category | flops | bytes accessed | tf_op | source)
XLA Modules:
  0.0 47.1 jit_solution(2315340332969136549)
XLA Ops:
  0.6 0.0 copy-start.1
  0.6 1.2 %copy-done.1 = f32[1,27,8192]{2,0,1:T(1,128)S(1)} copy-done((f32[1,27,8192]{2,0,1:T(1,128)S(1)}, f32[1,27,8192]{2,0,1:T(1,128)}, u32[]{:S(2)}) %copy-start.1) | copy-done | bytes 884760
  1.8 0.0 copy-start.6
  1.8 0.8 %copy-done.6 = s32[1,8192]{1,0:T(1,128)S(1)} copy-done((s32[1,8192]{1,0:T(1,128)S(1)}, s32[1,8192]{1,0:T(1,128)}, u32[]{:S(2)}) %copy-start.6) | copy-done | bytes 32792
  2.6 0.0 copy-start.9
  2.6 0.7 %copy-done.9 = f32[27]{0:T(128)S(1)} copy-done((f32[27]{0:T(128)S(1)}, f32[27]{0:T(128)}, u32[]{:S(2)}) %copy-start.9) | copy-done | bytes 132
  3.2 0.0 copy-start.2
  3.2 0.0 copy-start.4
  3.2 1.3 %collide.1 = (f32[1728,128]{1,0:T(8,128)S(1)}, f32[2,32,128]{2,1,0:T(8,128)S(1)}, f32[64,128]{1,0:T(8,128)S(1)}) custom-call(f32[1728,128]{1,0:T(8,128)S(1)} %bitcast.5, s32[64,128]{1,0:T(8,128)S(1)} %bitcast.6, f32[27]{0:T(128)S(1)} %copy-done.9), custom_call_target="tpu_custom_call" | custom-call | tf_op jit(solution)/shard_map/collide/pallas_call | solution.py:524
  4.5 1.3 %collective-permute-start = (f32[2,32,128]{2,1,0:T(8,128)S(1)}, f32[2,32,128]{2,1,0:T(8,128)S(1)}, u32[]{:S(2)}, u32[]{:S(2)}) collective-permute-start(f32[2,32,128]{2,1,0:T(8,128)S(1)} %get-tuple-element.19), channel_id=1, source_target_pairs={{0,1},{1,0},{2,3},{3,2},{4,5},{5,4},{6,7},{7,6},{8,9},{9,8},{10,11... | collective-permute-start | bytes 98312 | tf_op jit(solution)/shard_map/ppermute | solution.py:509
  5.8 1.1 %collective-permute-start.1 = (f32[64,128]{1,0:T(8,128)S(1)}, f32[64,128]{1,0:T(8,128)S(1)}, u32[]{:S(2)}, u32[]{:S(2)}) collective-permute-start(f32[64,128]{1,0:T(8,128)S(1)} %get-tuple-element.20), channel_id=1, source_target_pairs={{0,2},{1,3},{2,0},{3,1},{4,6},{5,7},{6,4},{7,5},{8,10},{9,11},{10,... | collective-permute-start | bytes 98312 | tf_op jit(solution)/shard_map/ppermute | solution.py:509
  6.9 0.7 %reshape.23.rec_ref = f32[54,128]{1,0:T(8,128)S(1)} reshape(bf16[1,2,3456]{2,1,0:T(2,128)(2,1)} %param.14) | data formatting | bytes 41472 | tf_op jit(solution)/shard_map/convert_element_type | solution.py:520
  7.6 0.3 stream.1
  7.9 0.0 copy-start.8
  7.9 0.5 %collective-permute-done.y_ref = f32[2,32,128]{2,1,0:T(8,128)S(1)} collective-permute-done((f32[2,32,128]{2,1,0:T(8,128)S(1)}, f32[2,32,128]{2,1,0:T(8,128)S(1)}, u32[]{:S(2)}, u32[]{:S(2)}) %collective-permute-start) | collective-permute-done | bytes 32800 | tf_op jit(solution)/shard_map/ppermute | solution.py:509
  8.5 2.7 %collective-permute-done.1.z_ref = f32[64,128]{1,0:T(8,128)S(1)} collective-permute-done((f32[64,128]{1,0:T(8,128)S(1)}, f32[64,128]{1,0:T(8,128)S(1)}, u32[]{:S(2)}, u32[]{:S(2)}) %collective-permute-start.1) | collective-permute-done | bytes 32800 | tf_op jit(solution)/shard_map/ppermute | solution.py:509
  11.2 0.0 copy-done.2
  11.2 0.0 copy-done.4
  11.2 0.0 copy-start
  11.2 0.0 copy-start.3
  11.2 0.0 copy-start.5
  11.2 0.0 copy-start.7
  11.2 1.6 %halo.1 = (f32[2160,128]{1,0:T(8,128)S(1)}, f32[72,128]{1,0:T(8,128)S(1)}, f32[72,128]{1,0:T(8,128)S(1)}, bf16[8,112,128]{2,1,0:T(8,128)(2,1)}, f32[32,128]{1,0:T(8,128)S(1)}) custom-call(s32[1]{0:T(128)} %bitcast.q_ref, f32[2160,128]{1,0:T(8,128)S(1)} %get-tuple-element.18.t_ref, ...), custom_call_target="tpu_custom_call", output_to_operand_aliasing={{0}: (1, {})} | custom-call | tf_op jit(solution)/shard_map/halo/pallas_call | solution.py:549
  12.9 4.5 %all-to-all-start = ((bf16[8,112,128]{2,1,0:T(8,128)(2,1)}), bf16[8,112,128]{2,1,0:T(8,128)(2,1)S(1)}, u32[]{:S(2)}, u32[]{:S(2)}) async-start(bf16[8,112,128]{2,1,0:T(8,128)(2,1)} %get-tuple-element.24), calls=%async_computation | async-start | bytes 458752 | tf_op jit(solution)/shard_map/all_to_all | solution.py:572
  17.3 0.6 %collective-permute-start.2 = (f32[32,128]{1,0:T(8,128)S(1)}, f32[32,128]{1,0:T(8,128)S(1)}, u32[]{:S(2)}, u32[]{:S(2)}) collective-permute-start(f32[32,128]{1,0:T(8,128)S(1)} %get-tuple-element.23), channel_id=1, source_target_pairs={{0,3},{1,2},{2,1},{3,0},{4,7},{5,6},{6,5},{7,4},{8,11},{9,10},{10,... | collective-permute-start | bytes 49160 | tf_op jit(solution)/shard_map/ppermute | solution.py:509
  18.0 0.0 copy-done.8
  18.0 0.1 select_reduce_fusion.inverse_ref
  18.1 3.0 %collective-permute-done.2.e_ref = f32[32,128]{1,0:T(8,128)S(1)} collective-permute-done((f32[32,128]{1,0:T(8,128)S(1)}, f32[32,128]{1,0:T(8,128)S(1)}, u32[]{:S(2)}, u32[]{:S(2)}) %collective-permute-start.2) | collective-permute-done | bytes 16416 | tf_op jit(solution)/shard_map/ppermute | solution.py:509
  21.1 3.4 %all-to-all-done.in_ref = bf16[8,112,128]{2,1,0:T(8,128)(2,1)S(1)} async-done(((bf16[8,112,128]{2,1,0:T(8,128)(2,1)}), bf16[8,112,128]{2,1,0:T(8,128)(2,1)S(1)}, u32[]{:S(2)}, u32[]{:S(2)}) %all-to-all-start) | async-done | bytes 229408 | tf_op jit(solution)/shard_map/all_to_all | solution.py:572
  24.5 1.3 %route.1 = (bf16[8,112,128]{2,1,0:T(8,128)(2,1)}, f32[72,128]{1,0:T(8,128)S(1)}, f32[72,128]{1,0:T(8,128)S(1)}) custom-call(s32[128]{0:T(128)S(1)} %bitcast.8, s32[128]{0:T(128)S(1)} %select_reduce_fusion.inverse_ref, bf16[8,112,128]{2,1,0:T(8,128)(2,1)S(1)} %all-to-all-done.in_ref, f32[32,128]{1,0:T(8,128)S(1)} %collective-permute-done.2.e_ref, ...), custom_call_target="tpu_custom_call" | custom-call | tf_op jit(solution)/shard_map/route/pallas_call | solution.py:573
  25.8 8.5 %all-to-all-start.1 = ((bf16[8,112,128]{2,1,0:T(8,128)(2,1)}), bf16[8,112,128]{2,1,0:T(8,128)(2,1)S(1)}, u32[]{:S(2)}, u32[]{:S(2)}) async-start(bf16[8,112,128]{2,1,0:T(8,128)(2,1)} %get-tuple-element.29), calls=%async_computation.1 | async-start | bytes 458752 | tf_op jit(solution)/shard_map/all_to_all | solution.py:585
  34.3 0.0 collective-permute-start.3
  34.3 5.1 %collective-permute-start.4 = (f32[72,128]{1,0:T(8,128)S(1)}, f32[72,128]{1,0:T(8,128)S(1)}, u32[]{:S(2)}, u32[]{:S(2)}) collective-permute-start(f32[72,128]{1,0:T(8,128)S(1)} %get-tuple-element.28), channel_id=1, source_target_pairs={{4,0},{8,4},{12,8},{16,12},{20,16},{24,20},{28,24},{32,28},{36,32}... | collective-permute-start | bytes 110600 | tf_op jit(solution)/shard_map/ppermute | solution.py:588
  39.3 3.2 %collective-permute-done.3.right_ref = f32[72,128]{1,0:T(8,128)S(1)} collective-permute-done((f32[72,128]{1,0:T(8,128)S(1)}, f32[72,128]{1,0:T(8,128)S(1)}, u32[]{:S(2)}, u32[]{:S(2)}) %collective-permute-start.3) | collective-permute-done | bytes 36896 | tf_op jit(solution)/shard_map/ppermute | solution.py:587
  42.5 0.0 collective-permute-done.4.left_ref
  42.5 2.6 %all-to-all-done.1.in_ref = bf16[8,112,128]{2,1,0:T(8,128)(2,1)S(1)} async-done(((bf16[8,112,128]{2,1,0:T(8,128)(2,1)}), bf16[8,112,128]{2,1,0:T(8,128)(2,1)S(1)}, u32[]{:S(2)}, u32[]{:S(2)}) %all-to-all-start.1) | async-done | bytes 229408 | tf_op jit(solution)/shard_map/all_to_all | solution.py:585
  45.1 0.0 copy-done
  45.1 0.0 copy-done.3
  45.1 0.0 copy-done.5
  45.1 0.0 copy-done.7
  45.1 2.0 %finish.1 = (f32[1728,128]{1,0:T(8,128)}, f32[1,2,3456]{2,1,0:T(2,128)}) custom-call(s32[1]{0:T(128)} %bitcast.q_ref, s32[128]{0:T(128)S(1)} %bitcast.9, s32[128]{0:T(128)S(1)} %select_reduce_fusion.inverse_ref, f32[2160,128]{1,0:T(8,128)S(1)} %get-tuple-element.22.t_ref, f32[32,128]{1,0:T(8,128)S(1)} %collective-permute-done.2.e_ref, ...), custom_call_target="tpu_custom_call" | custom-call | tf_op jit(solution)/shard_map/finish/pallas_call | solution.py:591
Async XLA Ops:
  0.6 1.2 %copy-start.1 = (f32[1,27,8192]{2,0,1:T(1,128)S(1)}, f32[1,27,8192]{2,0,1:T(1,128)}, u32[]{:S(2)}) copy-start(f32[1,27,8192]{2,0,1:T(1,128)} %param.11) | copy-start | bytes 2654212
  1.8 0.8 %copy-start.6 = (s32[1,8192]{1,0:T(1,128)S(1)}, s32[1,8192]{1,0:T(1,128)}, u32[]{:S(2)}) copy-start(s32[1,8192]{1,0:T(1,128)} %param.12) | copy-start | bytes 98308
  2.6 0.7 %copy-start.9 = (f32[27]{0:T(128)S(1)}, f32[27]{0:T(128)}, u32[]{:S(2)}) copy-start(f32[27]{0:T(128)} %rates_ref.1) | copy-start | bytes 328
  3.2 8.0 %copy-start.2 = (f32[4,64,128]{2,1,0:T(8,128)S(1)}, f32[4,64,128]{2,1,0:T(8,128)}, u32[]{:S(2)}) copy-start(f32[4,64,128]{2,1,0:T(8,128)} %constant.18.clone.share_ref) | copy-start | bytes 393220
  3.2 8.0 %copy-start.4 = (bf16[4,256,128]{2,1,0:T(8,128)(2,1)S(1)}, bf16[4,256,128]{2,1,0:T(8,128)(2,1)}, u32[]{:S(2)}) copy-start(bf16[4,256,128]{2,1,0:T(8,128)(2,1)} %constant.19.clone.pool_ref) | copy-start | bytes 786436
  4.5 4.0 %collective-permute-start = (f32[2,32,128]{2,1,0:T(8,128)S(1)}, f32[2,32,128]{2,1,0:T(8,128)S(1)}, u32[]{:S(2)}, u32[]{:S(2)}) collective-permute-start(f32[2,32,128]{2,1,0:T(8,128)S(1)} %get-tuple-element.19), channel_id=1, source_target_pairs={{0,1},{1,0},{2,3},{3,2},{4,5},{5,4},{6,7},{7,6},{8,9},{9,8},{10,11... | collective-permute-start | bytes 98312 | tf_op jit(solution)/shard_map/ppermute | solution.py:509
  5.8 5.4 %collective-permute-start.1 = (f32[64,128]{1,0:T(8,128)S(1)}, f32[64,128]{1,0:T(8,128)S(1)}, u32[]{:S(2)}, u32[]{:S(2)}) collective-permute-start(f32[64,128]{1,0:T(8,128)S(1)} %get-tuple-element.20), channel_id=1, source_target_pairs={{0,2},{1,3},{2,0},{3,1},{4,6},{5,7},{6,4},{7,5},{8,10},{9,11},{10,... | collective-permute-start | bytes 98312 | tf_op jit(solution)/shard_map/ppermute | solution.py:509
  7.9 10.0 %copy-start.8 = (s32[1,128]{1,0:T(1,128)S(1)}, s32[1,128]{1,0:T(1,128)}, u32[]{:S(2)}) copy-start(s32[1,128]{1,0:T(1,128)} %param.15) | copy-start | bytes 1540
  11.2 33.9 %copy-start = (bf16[4,256,512]{2,1,0:T(8,128)(2,1)S(1)}, bf16[4,256,512]{2,1,0:T(8,128)(2,1)}, u32[]{:S(2)}) copy-start(bf16[4,256,512]{2,1,0:T(8,128)(2,1)} %constant.21.clone.ghost_ref) | copy-start | bytes 3145732
  11.2 33.9 %copy-start.3 = (bf16[4,128,384]{2,1,0:T(8,128)(2,1)S(1)}, bf16[4,128,384]{2,1,0:T(8,128)(2,1)}, u32[]{:S(2)}) copy-start(bf16[4,128,384]{2,1,0:T(8,128)(2,1)} %constant.22.clone.coarse_ref) | copy-start | bytes 1179652
  11.2 33.9 %copy-start.5 = (f32[4,64,128]{2,1,0:T(8,128)S(1)}, f32[4,64,128]{2,1,0:T(8,128)}, u32[]{:S(2)}) copy-start(f32[4,64,128]{2,1,0:T(8,128)} %constant.23.clone.pop_ref) | copy-start | bytes 393220
  11.2 33.9 %copy-start.7 = (f32[16,128]{1,0:T(8,128)S(1)}, f32[16,128]{1,0:T(8,128)}, u32[]{:S(2)}) copy-start(f32[16,128]{1,0:T(8,128)} %constant.20.clone.line_ref) | copy-start | bytes 24580
  12.9 11.7 %all-to-all-start = ((bf16[8,112,128]{2,1,0:T(8,128)(2,1)}), bf16[8,112,128]{2,1,0:T(8,128)(2,1)S(1)}, u32[]{:S(2)}, u32[]{:S(2)}) async-start(bf16[8,112,128]{2,1,0:T(8,128)(2,1)} %get-tuple-element.24), calls=%async_computation | async-start | bytes 458752 | tf_op jit(solution)/shard_map/all_to_all | solution.py:572
  17.3 3.7 %collective-permute-start.2 = (f32[32,128]{1,0:T(8,128)S(1)}, f32[32,128]{1,0:T(8,128)S(1)}, u32[]{:S(2)}, u32[]{:S(2)}) collective-permute-start(f32[32,128]{1,0:T(8,128)S(1)} %get-tuple-element.23), channel_id=1, source_target_pairs={{0,3},{1,2},{2,1},{3,0},{4,7},{5,6},{6,5},{7,4},{8,11},{9,10},{10,... | collective-permute-start | bytes 49160 | tf_op jit(solution)/shard_map/ppermute | solution.py:509
  25.8 19.3 %all-to-all-start.1 = ((bf16[8,112,128]{2,1,0:T(8,128)(2,1)}), bf16[8,112,128]{2,1,0:T(8,128)(2,1)S(1)}, u32[]{:S(2)}, u32[]{:S(2)}) async-start(bf16[8,112,128]{2,1,0:T(8,128)(2,1)} %get-tuple-element.29), calls=%async_computation.1 | async-start | bytes 458752 | tf_op jit(solution)/shard_map/all_to_all | solution.py:585
  34.3 8.2 %collective-permute-start.3 = (f32[72,128]{1,0:T(8,128)S(1)}, f32[72,128]{1,0:T(8,128)S(1)}, u32[]{:S(2)}, u32[]{:S(2)}) collective-permute-start(f32[72,128]{1,0:T(8,128)S(1)} %get-tuple-element.27), channel_id=1, source_target_pairs={{0,4},{4,8},{8,12},{12,16},{16,20},{20,24},{24,28},{28,32},{32,36}... | collective-permute-start | bytes 110600 | tf_op jit(solution)/shard_map/ppermute | solution.py:587
  34.3 8.2 %collective-permute-start.4 = (f32[72,128]{1,0:T(8,128)S(1)}, f32[72,128]{1,0:T(8,128)S(1)}, u32[]{:S(2)}, u32[]{:S(2)}) collective-permute-start(f32[72,128]{1,0:T(8,128)S(1)} %get-tuple-element.28), channel_id=1, source_target_pairs={{4,0},{8,4},{12,8},{16,12},{20,16},{24,20},{28,24},{32,28},{36,32}... | collective-permute-start | bytes 110600 | tf_op jit(solution)/shard_map/ppermute | solution.py:588

commit v2 on v1

v2 whole, which is shorter than its diff:
```python
import jax
import jax.numpy as jnp
from jax import lax
from jax.experimental import pallas as pl
from jax.experimental.pallas import tpu as pltpu
from jax.sharding import PartitionSpec as P

Q = 27
EDGE = 16
HALF = 8
NX = 32
SPAN = 2 * NX
PITCH = SPAN + 16
FIRST = 8
LANES = 128
PLANE = 8
BLOCKS = PLANE * PLANE
LOW, HIGH, SHARED, CENTRE, RECORDS, ROWS = 54, 55, 56, 57, 62, 80
MIXED = 48
PAIRS = [(i // 9, i // 3 % 3, i % 3) for i in range(Q)]
F32 = jnp.float32
BF16 = jnp.bfloat16


def sides():
    position = lax.axis_index("group")
    return position & 1, position >> 1


def geometry():
    side_y, side_z = sides()
    return 1 - side_y, 112 * (1 - side_y), 15 * (1 - side_z)


def ids(shape, dim):
    return lax.broadcasted_iota(jnp.int32, shape, dim)


def rolled(value, shift):
    return pltpu.roll(value, shift, 1)


def split_bf16(value):
    high = value.astype(BF16)
    return high, (value - high.astype(F32)).astype(BF16)


def dot(left, right):
    return jnp.dot(left, right, preferred_element_type=F32)


def record_ids(shape, dim):
    value = ids(shape, dim) & 127
    return value >> 6, value >> 3 & 7, value & 7


def digits(index):
    third, ninth = index * 11 >> 5, index * 57 >> 9
    return ninth, third - 3 * ninth, index - 3 * third


def interp(fine, coarse):
    weight = 1.0 - jnp.abs(0.5 * fine.astype(F32) - 0.25 - coarse.astype(F32))
    end = (fine == 0) | (fine == EDGE - 1)
    return jnp.where(weight > 0.0, jnp.where(end, 1.0, weight), 0.0)


def pool_table():
    side_y, side_z = sides()
    shape = (256, LANES)
    cell = ids(shape, 0)
    pair_y, pair_z = cell >> 5, cell >> 1 & 7
    face, a, b = record_ids(shape, 1)
    on_y = (pair_y == 7 * side_y) & (pair_z == b)
    on_z = (pair_z == 7 * side_z) & (pair_y == b)
    return jnp.where(((face == 0) & on_y) | ((face == 1) & on_z), 0.125, 0.0).astype(BF16)


def share_table():
    side_y, side_z = sides()
    shape = (64, LANES)
    row = ids(shape, 0)
    face, a, b = record_ids(shape, 1)
    column = (row >= Q).astype(jnp.int32)
    index = jnp.where(row < LOW, row - Q * column, jnp.where(row == LOW, 18 + a, a))
    index = jnp.where(row == SHARED, jnp.where(a == 7, 26, 8), index)
    by_x, by_y, by_z = digits(index)
    in_y, in_z = by_y == 2 * (1 - side_y), by_z == 2 * (1 - side_z)
    half_y = in_y & ((face == 0) | (b == 7 * side_y))
    half_z = in_z & ((face == 1) | (b == 7 * side_z))
    low = (by_x == 2) & (column == 0) & (a == 0)
    high = (by_x == 0) & (column == 1) & (a == HALF - 1)
    half_x = (row >= LOW) | low | high
    share = jnp.where(half_y, 0.5, 1.0) * jnp.where(half_z, 0.5, 1.0) * jnp.where(half_x, 0.5, 1.0)
    held = (row <= HIGH) | ((row == SHARED) & ((a == 0) | (a == 7)))
    return jnp.where(held, share, 0.0)


def ghost_table():
    side_y, side_z = sides()
    shape = (LANES, LANES)
    face, a, b = record_ids(shape, 0)
    lanes = ids(shape, 1)
    y, z = lanes >> 4, lanes & 15
    parts = [jnp.where((face == 0) & (y == 7 * side_y), interp(z, b), 0.0)]
    for h in range(2):
        parts.append(jnp.where((face == 1) & (z == 15 * side_z), interp(y + HALF * h, b), 0.0))
    return jnp.concatenate(parts, 1).astype(BF16)


def part_table():
    side_y, side_z = sides()
    shape = (LANES, LANES)
    face, a, b = record_ids(shape, 0)
    to_face, to_a, to_b = record_ids(shape, 1)
    along_x = 0.125 * (interp(2 * to_a, a) + interp(2 * to_a + 1, a))
    across = along_x * (interp(2 * to_b, b) + interp(2 * to_b + 1, b))
    zero = jnp.zeros(shape, jnp.int32)
    out_y, out_z = zero + 15 * side_y, zero + 15 * side_z
    next_y, next_z = zero + 1 + 13 * side_y, zero + 1 + 13 * side_z
    edge_y, edge_z = to_b == 7 * side_y, to_b == 7 * side_z
    line_y = along_x * interp(out_y, b)
    both_y = line_y + along_x * interp(next_y, b)
    both_z = along_x * (interp(out_z, b) + interp(next_z, b))
    in_y = jnp.where(to_face == 0, across, jnp.where(edge_y, both_z, 0.0))
    in_z = jnp.where(to_face == 1, across, jnp.where(edge_z, both_y, 0.0))
    ends = ((to_face == 0) & edge_z) | ((to_face == 1) & edge_y)
    shared = jnp.where(ends, line_y, 0.0)
    parts = [jnp.where(face == 0, in_y, 0.0), jnp.where(face == 1, in_z, 0.0), jnp.where(face == 1, shared, 0.0)]
    return jnp.concatenate(parts, 1).astype(BF16)


def along(table, axis, line):
    out = {}
    for first in range(3):
        for second in range(3):
            keys = []
            for third in range(3):
                key = [first, second]
                key.insert(axis, third)
                keys.append(tuple(key))
            values = line(*[table[key] for key in keys])
            for key, value in zip(keys, values):
                out[key] = value
    return out


def line_moments(low, mid, high):
    both = low + high
    return both + 4.0 * mid, high - low, both


def line_inverse(zeroth, first, second):
    return second - first, zeroth - 0.5 * second, first + second


def collide_cells(current, rates):
    table = {PAIRS[i]: current[i] for i in range(Q)}
    moments = table
    for axis in range(3):
        moments = along(moments, axis, line_moments)
    density = moments[0, 0, 0]
    inverse = 1.0 / density
    flow = [moments[1, 0, 0], moments[0, 1, 0], moments[0, 0, 1]]
    speed = [part * inverse for part in flow]
    carried = [density * part for part in speed]
    square = [carried[axis] * speed[axis] for axis in range(3)]
    third = density * (1.0 / 3.0)
    relaxed = {}
    for index, key in enumerate(PAIRS):
        ones = [axis for axis in range(3) if key[axis] == 1]
        twos = [axis for axis in range(3) if key[axis] == 2]
        scale = (1.0 / 3.0) ** len(twos)
        if len(ones) == 0:
            if len(twos) == 0:
                balance = density
            elif len(twos) == 1:
                balance = third + square[twos[0]]
            elif len(twos) == 2:
                balance = (third + square[twos[0]] + square[twos[1]]) * (1.0 / 3.0)
            else:
                balance = (third + square[0] + square[1] + square[2]) * (1.0 / 9.0)
        elif len(ones) == 1:
            balance = carried[ones[0]] * scale if twos else carried[ones[0]]
        elif len(ones) == 2:
            balance = carried[ones[0]] * speed[ones[1]]
            balance = balance * scale if twos else balance
        else:
            balance = None
        rest = moments[key] if balance is None else moments[key] - balance
        relaxed[key] = rates[index] * rest
    change = relaxed
    for axis in range(3):
        change = along(change, axis, line_inverse)
    return [current[i] - change[PAIRS[i]] for i in range(Q)]


def collide_kernel(
    g_hbm, solid_hbm, rates_hbm, w_hbm, y_ref, z_ref, g_ref, w_ref, solid_ref, rates_ref, sems
):
    pieces = 4
    size = SPAN // pieces
    copies = [
        pltpu.make_async_copy(rates_hbm, rates_ref, sems.at[pieces]),
        pltpu.make_async_copy(solid_hbm, solid_ref, sems.at[pieces + 1]),
    ]
    for piece in range(pieces):
        rows = pl.ds(size * piece, size)
        copies.append(
            pltpu.make_async_copy(g_hbm.at[:, rows, :], g_ref.at[:, rows, :], sems.at[piece])
        )
    for copy in copies:
        copy.start()
    side_y, side_z = sides()
    copies[0].wait()
    rates = []
    for i in range(Q):
        scale = 1.0 / 216.0
        for part in PAIRS[i]:
            scale *= 1.5 if part == 0 else 3.0
        rates.append(rates_ref[i] * scale)
    copies[1].wait()

    def chunk(index, carry):
        row = pl.multiple_of(8 * index, 8)
        current = [g_ref[i, pl.ds(row, 8), :] for i in range(Q)]
        solid = solid_ref[pl.ds(row, 8), :] == 1
        collided = collide_cells(current, rates)
        for i in range(Q):
            w_ref[i, pl.ds(row, 8), :] = jnp.where(solid, current[Q - 1 - i], collided[i])
        return carry

    for piece in range(pieces):
        copies[2 + piece].wait()
        lax.fori_loop(size // 8 * piece, size // 8 * (piece + 1), chunk, 0)
        rows = pl.ds(size * piece, size)
        copy = pltpu.make_async_copy(
            w_ref.at[:, rows, :], w_hbm.at[:, rows, :], sems.at[pieces + 2 + piece]
        )
        copy.start()
        copies.append(copy)

    send_y, send_z = 2 * (1 - side_y), 2 * (1 - side_z)
    tile, base, inner = geometry()
    lanes = ids((NX, LANES), 1)
    packed = [jnp.zeros((NX, LANES), F32), jnp.zeros((NX, LANES), F32)]
    for k in range(9):
        index = 9 * (k // 3) + 3 * send_y + k % 3
        value = w_ref[index, pl.ds(tile, NX, stride=2), :]
        value = rolled(value, (16 * (k % 8) - base) & 127)
        packed[k // 8] = jnp.where(lanes >> 4 == k % 8, value, packed[k // 8])
    y_ref[0] = packed[0]
    y_ref[1] = packed[1]
    lanes = ids((SPAN, LANES), 1)
    packed_z = jnp.zeros((SPAN, LANES), F32)
    for k in range(9):
        index = 9 * (k // 3) + 3 * (k % 3) + send_z
        value = w_ref[index]
        packed_z = jnp.where(lanes & 15 == k, rolled(value, (k - inner) & 127), packed_z)
    z_ref[...] = packed_z
    for copy in copies[2 + pieces :]:
        copy.wait()


def moved(value, b, shift):
    value = rolled(value, shift)
    if b == 1:
        return value
    rows, lanes = ids(value.shape, 0), ids(value.shape, 1)
    if b == 2:
        other = pltpu.roll(value, 1, 0)
        return jnp.where(lanes >= 16, value, jnp.where(rows & 1 == 1, other, 0.0))
    other = pltpu.roll(value, value.shape[0] - 1, 0)
    return jnp.where(lanes < 112, value, jnp.where(rows & 1 == 0, other, 0.0))


def z_inside(lanes, c):
    return lanes & 15 <= 14 if c == 0 else lanes & 15 >= 1


def stream_kernel(w_ref, coarse_ref, t_ref, e_ref, pool_ref, share_ref, rec_ref, p_ref):
    lanes = ids((8, LANES), 1)
    zeros = jnp.zeros((8, LANES), F32)
    for i, (a, b, c) in enumerate(PAIRS):
        for row in (0, 8, SPAN, SPAN + 8):
            t_ref[pl.ds(PITCH * i + row, 8), :] = zeros
        shift = (16 * (b - 1) + c - 1) % 128
        for row in range(0, SPAN, 8):
            value = w_ref[i, pl.ds(row, 8), :]
            if shift:
                value = moved(value, b, shift)
            if c != 1:
                value = jnp.where(z_inside(lanes, c), value, 0.0)
            t_ref[pl.ds(PITCH * i + FIRST + row + 2 * (a - 1), 8), :] = value

    side_y, side_z = sides()
    tile, base, inner = geometry()
    lanes = ids((NX, LANES), 1)
    packed = jnp.zeros((NX, LANES), F32)
    for a in range(3):
        index = 9 * a + 6 * (1 - side_y) + 2 * (1 - side_z)
        value = w_ref[index, pl.ds(tile, NX, stride=2), :]
        packed = jnp.where(lanes == a, rolled(value, (a - base - inner) & 127), packed)
    e_ref[...] = packed

    p_ref[...] = jnp.zeros((64, LANES), F32)
    records = coarse_ref[0].astype(F32)
    for t in range(2):
        for i in range(Q):
            p_ref[32 * t + i : 32 * t + i + 1, :] = records[t : t + 1, LANES * i : LANES * (i + 1)]
    in_y, in_z = 2 * (1 - side_y), 2 * (1 - side_z)
    first = ids((1, LANES), 1) < 64
    rec_ref[...] = jnp.zeros((32, LANES), F32)
    for t in range(2):
        for k in range(9):
            for_y = p_ref[pl.ds(32 * t + 9 * (k // 3) + 3 * in_y + k % 3, 1), :]
            for_z = p_ref[pl.ds(32 * t + 9 * (k // 3) + 3 * (k % 3) + in_z, 1), :]
            row = RECORDS - MIXED + 9 * t + k
            rec_ref[row : row + 1, :] = jnp.where(first, for_y, for_z)

    pool_ref[...] = pool_table()
    share_ref[...] = share_table()


def halo_kernel(
    t_ref, y_ref, z_ref, e_ref, rec_ref, pool_ref, share_ref, p_ref,
    out_ref, right_ref, left_ref, pay_ref, edge_ref, kept_ref,
):
    del t_ref
    kept_ref[...] = p_ref[...]
    side_y, side_z = sides()
    halo_y, halo_z = 2 * side_y, 2 * side_z
    tile, base, inner = geometry()
    edge_ref[...] = e_ref[...]

    lanes = ids((NX, LANES), 1)
    row_mask = lanes >> 4 == base >> 4
    for k in range(9):
        a, c = k // 3, k % 3
        value = rolled(y_ref[k // 8], (base - 16 * (k % 8) + c - 1) & 127)
        mask = row_mask if c == 1 else row_mask & z_inside(lanes, c)
        index = 9 * a + 3 * halo_y + c
        rows = pl.ds(PITCH * index + FIRST + 2 * (a - 1) + tile, NX, stride=2)
        out_ref[rows, :] = out_ref[rows, :] + jnp.where(mask, value, 0.0)
    lanes = ids((8, LANES), 1)
    for k in range(9):
        a, b = k // 3, k % 3
        shift = (inner - k + 16 * (b - 1)) & 127
        index = 9 * a + 3 * b + halo_z
        for row in range(0, SPAN, 8):
            value = moved(z_ref[pl.ds(row, 8), :], b, shift)
            rows = pl.ds(PITCH * index + FIRST + row + 2 * (a - 1), 8)
            out_ref[rows, :] = out_ref[rows, :] + jnp.where(lanes & 15 == inner, value, 0.0)

    for k in range(9):
        right_ref[8 * k : 8 * k + 8, :] = out_ref[pl.ds(PITCH * (18 + k) + FIRST + SPAN, 8), :]
        left_ref[8 * k : 8 * k + 8, :] = out_ref[pl.ds(PITCH * k, 8), :]

    row_8 = ids((8, LANES), 0)
    total = 8 * (2 * Q + 4)
    pooled = jnp.zeros((total, LANES), F32)
    for h in range(2):
        parts = []
        for i in range(Q):
            for s in range(2):
                row = PITCH * i + FIRST + NX * s + h
                parts.append(
                    out_ref[pl.ds(row, 8, stride=4), :] + out_ref[pl.ds(row + 2, 8, stride=4), :]
                )
        over, under = FIRST + SPAN + h, FIRST - 2 + h
        parts.append(out_ref[pl.ds(PITCH * 18 + over, 8, stride=PITCH), :])
        last = out_ref[pl.ds(PITCH * 19 + over, 8, stride=PITCH), :]
        parts.append(jnp.where(row_8 == 7, last, 0.0))
        parts.append(out_ref[pl.ds(under, 8, stride=PITCH), :])
        parts.append(out_ref[pl.ds(PITCH * 8 + under, 8, stride=PITCH), :])
        for part in split_bf16(jnp.concatenate(parts, 0)):
            pooled = pooled + dot(part, pool_ref[LANES * h : LANES * (h + 1), :])
    pooled = jnp.where(ids((total, LANES), 0) & 7 == ids((total, LANES), 1) >> 3 & 7, pooled, 0.0)
    target, block = ids((64, total), 0), ids((64, total), 1) >> 3
    second = (target >= Q).astype(jnp.int32)
    wanted = jnp.where(target < LOW, 2 * (target - Q * second) + second, -1)
    wanted = jnp.where(target == LOW, 54, jnp.where(target == HIGH, 56, wanted))
    chosen = (wanted == block) | ((target == SHARED) & ((block == 55) | (block == 57)))
    chosen = chosen.astype(F32).astype(BF16)
    routed = jnp.zeros((64, LANES), F32)
    for part in split_bf16(pooled):
        routed = routed + dot(chosen, part)

    share = share_ref[...]
    rows, lane_a = ids((64, LANES), 0), ids((64, LANES), 1) >> 3 & 7
    inside = rows < LOW
    held = jnp.sum(jnp.where(inside, routed, 0.0), axis=0, keepdims=True)
    held = jnp.sum(held, axis=1, keepdims=True)
    parts = jnp.sum(jnp.where(inside, share, 0.0), axis=0, keepdims=True)
    parts = jnp.sum(parts, axis=1, keepdims=True)
    centre = (held / parts).astype(BF16).astype(F32)
    routed = routed - centre * share
    is_centre = (rows == CENTRE) | ((rows == SHARED) & ((lane_a == 1) | (lane_a == 6)))
    routed = jnp.where(is_centre, centre, routed)
    payload = jnp.where(rows[MIXED:64] >= RECORDS, rec_ref[0:16], routed[MIXED:64])
    payload = jnp.concatenate([routed[0:MIXED], payload, rec_ref[16:32]], 0).astype(BF16)
    for slot in range(PLANE):
        pay_ref[slot] = payload


def tables_kernel(p_ref, pairs_ref, ghost_ref, line_ref, own_ref, route_ref):
    side_y, side_z = sides()
    ghost = ghost_table()
    ghost_ref[0:LANES] = ghost
    ghost_ref[LANES : 2 * LANES] = ghost
    shape = (EDGE, LANES)
    line_ref[...] = interp(ids(shape, 0), record_ids(shape, 1)[1])

    part = dot(p_ref[...].astype(BF16), part_table())
    _, by_y, by_z = digits(ids((32, LANES), 0))
    in_y, in_z = by_y == 2 * (1 - side_y), by_z == 2 * (1 - side_z)
    for t in range(2):
        rows = part[32 * t : 32 * t + 32]
        value = jnp.where(in_y, rows[:, 0:128], 0.0) + jnp.where(in_z, rows[:, 128:256], 0.0)
        own_ref[32 * t : 32 * t + 32] = value - jnp.where(in_y & in_z, rows[:, 256:384], 0.0)

    me = lax.axis_index("blocks")
    pairs = jnp.broadcast_to(pairs_ref[...], (8, LANES))
    lanes = ids((8, LANES), 1)
    devices = PLANE * ids((8, LANES), 0) + (me & (PLANE - 1))

    def total(mask, value):
        value = jnp.where(mask, value.astype(F32), 0.0)
        return jnp.broadcast_to(jnp.sum(value, axis=1, keepdims=True), (8, LANES)).astype(jnp.int32)

    route_ref[0:8] = total(lanes == 2 * devices, pairs >> 1)
    route_ref[8:16] = total(pairs == 2 * devices, lanes >> 1)
    rows = ids((8, LANES), 0)
    mine = total(lanes == 2 * me, pairs)
    held = total(pairs == 2 * me, lanes)
    route_ref[16:24] = jnp.where(
        rows == 0, mine >> 1, jnp.where(rows == 1, held >> 1, jnp.where(rows == 2, held & 1, mine & 1))
    )


def pick(route, mask, in_ref, rows):
    chosen = None
    for member in range(PLANE):
        value = in_ref[member, rows].astype(F32)
        chosen = value if chosen is None else jnp.where((route & mask) == member, value, chosen)
    return chosen


def route_kernel(route_ref, in_ref, e_ref, right_in, left_in, out_ref, right_ref, left_ref):
    rows, lane_a = ids((16, LANES), 0) + MIXED, ids((16, LANES), 1) >> 3 & 7
    from_low = (rows == LOW) | ((rows == SHARED) & (lane_a >= 4))
    from_high = (rows == HIGH) | ((rows == SHARED) & (lane_a < 4))
    from_holder = rows >= RECORDS
    for plane in range(PLANE):
        owner = route_ref[plane : plane + 1, :]
        holder = route_ref[8 + plane : 9 + plane, :]
        mixed = jnp.where(from_holder, holder, owner)
        mixed = jnp.where(from_low, owner - 1, jnp.where(from_high, owner + 1, mixed))
        for start in range(0, ROWS, 16):
            route = owner if start < MIXED else mixed if start == MIXED else holder
            route = jnp.broadcast_to(route, (16, LANES))
            value = pick(route, PLANE - 1, in_ref, slice(start, start + 16))
            out_ref[plane, start : start + 16] = value.astype(BF16)

    side_y, side_z = sides()
    tile, base, inner = geometry()
    right_ref[...] = right_in[...]
    left_ref[...] = left_in[...]
    corner = 8 * (6 * side_y + 2 * side_z)
    lanes = ids((1, LANES), 1)
    for ref, layer, a, row in ((right_ref, NX - 1, 2, 0), (left_ref, 0, 0, 6)):
        value = rolled(e_ref[layer : layer + 1, :], (base + inner - a) & 127)
        at = pl.ds(corner + row + tile, 1)
        ref[at, :] = ref[at, :] + jnp.where(lanes == base + inner, value, 0.0)


def finish_kernel(
    t_ref, e_ref, right_ref, left_ref, in_ref, route_ref, own_ref, line_ref, share_ref, ghost_ref,
    next_ref, update_ref,
    p_ref,
):
    side_y, side_z = sides()
    tile, base, inner = geometry()
    in_y, in_z = 2 * (1 - side_y), 2 * (1 - side_z)
    for i in range(Q):
        next_ref[SPAN * i : SPAN * (i + 1), :] = t_ref[PITCH * i + FIRST : PITCH * i + FIRST + SPAN, :]

    holder = jnp.broadcast_to(route_ref[17:18, :], (32, LANES)) >> 3
    p_ref[...] = pick(holder, PLANE - 1, in_ref, slice(MIXED, ROWS))
    swap = route_ref[18:19, :] == 1
    lines = line_ref[...]
    scaled = []
    for k in range(9):
        row = RECORDS - MIXED + k
        first, second = p_ref[row : row + 1, :], p_ref[row + 9 : row + 10, :]
        scaled.append(lines * jnp.where(swap, second, first))
        scaled.append(lines * jnp.where(swap, first, second))
    scaled = jnp.concatenate(scaled, 0)
    ghost = dot(jnp.concatenate(split_bf16(scaled), 1), ghost_ref[...])
    for k in range(9):
        index = 9 * (k // 3) + 3 * (k % 3) + in_z
        for h in range(2):
            rows = pl.ds(SPAN * index + h, NX, stride=2)
            part = ghost[NX * k : NX * (k + 1), LANES * (h + 1) : LANES * (h + 2)]
            next_ref[rows, :] = next_ref[rows, :] + part
    lanes = ids((NX, LANES), 1)
    outer = lanes >> 4 == 7 * side_y
    for k in range(9):
        index = 9 * (k // 3) + 3 * in_y + k % 3
        rows = pl.ds(SPAN * index + side_y, NX, stride=2)
        next_ref[rows, :] = jnp.where(outer, ghost[NX * k : NX * (k + 1), 0:LANES], next_ref[rows, :])
    for k in range(9):
        rows = pl.ds(SPAN * (18 + k), 8)
        next_ref[rows, :] = next_ref[rows, :] + right_ref[8 * k : 8 * k + 8, :]
        rows = pl.ds(SPAN * k + SPAN - 8, 8)
        next_ref[rows, :] = next_ref[rows, :] + left_ref[8 * k : 8 * k + 8, :]
    for a in range(3):
        index = 9 * a + 6 * side_y + 2 * side_z
        low, high = (0, NX - (a - 1)) if a >= 1 else (1, NX)
        value = rolled(e_ref[low:high, :], (base + inner - a) & 127)
        value = jnp.where(lanes[low:high] == base + inner, value, 0.0)
        rows = pl.ds(SPAN * index + 2 * (low + a - 1) + tile, high - low, stride=2)
        next_ref[rows, :] = next_ref[rows, :] + value

    owner = route_ref[16:17, :]
    main = pick(jnp.broadcast_to(owner, (64, LANES)) >> 3, PLANE - 1, in_ref, slice(0, 64))
    owner = jnp.broadcast_to(owner, (16, LANES))
    lower = pick((owner + BLOCKS - 1) >> 3, PLANE - 1, in_ref, slice(MIXED, 64))
    upper = pick((owner + 1) >> 3, PLANE - 1, in_ref, slice(MIXED, 64))
    share = share_ref[...]
    main = main[0:LOW] + main[CENTRE : CENTRE + 1] * share[0:LOW]
    shared = SHARED - 48
    lane_1 = ids((1, LANES), 1)
    low_centre = jnp.sum(jnp.where(lane_1 == 48, lower[shared : shared + 1], 0.0), axis=1, keepdims=True)
    high_centre = jnp.sum(jnp.where(lane_1 == 8, upper[shared : shared + 1], 0.0), axis=1, keepdims=True)
    lower = lower + low_centre * share[48:64]
    upper = upper + high_centre * share[48:64]
    rows, lane_a = ids((32, LANES), 0), ids((32, LANES), 1) >> 3 & 7
    from_low = jnp.where(
        rows == 26,
        jnp.where(lane_a == 7, lower[shared : shared + 1], 0.0),
        jnp.where(rows - 18 == lane_a, lower[LOW - 48 : LOW - 47], 0.0),
    )
    from_high = jnp.where(
        rows == 8,
        jnp.where(lane_a == 0, upper[shared : shared + 1], 0.0),
        jnp.where(rows == lane_a, upper[HIGH - 48 : HIGH - 47], 0.0),
    )
    lane_in, lane_out = ids((LANES, LANES), 0), ids((LANES, LANES), 1)
    alike = (lane_in >> 6 == lane_out >> 6) & (lane_in & 7 == lane_out & 7)
    alike = alike.astype(F32).astype(BF16)
    edges = jnp.zeros((2 * 32, LANES), F32)
    for part in split_bf16(jnp.concatenate([from_low, from_high], 0)):
        edges = edges + dot(part, alike)
    column_0 = main[0:Q] + jnp.where(lane_a == 0, edges[0:32], 0.0)[0:Q]
    column_1 = main[Q : 2 * Q] + jnp.where(lane_a == HALF - 1, edges[32:64], 0.0)[0:Q]
    crossed = jnp.broadcast_to(route_ref[19:20, :], (Q, LANES)) == 1
    for t in range(2):
        here, there = (column_0, column_1) if t == 0 else (column_1, column_0)
        value = jnp.where(crossed, there, here) + own_ref[32 * t : 32 * t + Q, :]
        for i in range(Q):
            update_ref[0, t : t + 1, LANES * i : LANES * (i + 1)] = value[i : i + 1]


VMEM = pl.BlockSpec(memory_space=pltpu.VMEM)
HBM = pl.BlockSpec(memory_space=pltpu.HBM)


def call(kernel, name, results, inputs, outputs=None, scratch=(), cost=None, aliases=None, limit=32):
    return pl.pallas_call(
        kernel,
        out_shape=tuple(jax.ShapeDtypeStruct(*result) for result in results),
        in_specs=inputs,
        out_specs=outputs or (VMEM,) * len(results),
        scratch_shapes=scratch,
        input_output_aliases=aliases or {},
        compiler_params=pltpu.CompilerParams(vmem_limit_bytes=limit * 1024 * 1024),
        cost_estimate=cost,
        name=name,
    )


def swapped(block, bits):
    return lax.ppermute(block, "group", [(i, i ^ bits) for i in range(4)])


def body(populations, solid_mask, relax_rates, coarse_pops, interface_pairs):
    collided, edge_y, edge_z = call(
        collide_kernel,
        "collide",
        [((Q, SPAN, LANES), F32), ((2, NX, LANES), F32), ((SPAN, LANES), F32)],
        [HBM] * 3,
        (HBM, VMEM, VMEM),
        [
            pltpu.VMEM((Q, SPAN, LANES), F32),
            pltpu.VMEM((Q, SPAN, LANES), F32),
            pltpu.VMEM((SPAN, LANES), jnp.int32),
            pltpu.SMEM((Q,), F32),
            pltpu.SemaphoreType.DMA((10,)),
        ],
        limit=60,
    )(populations.reshape(Q, SPAN, LANES), solid_mask.reshape(SPAN, LANES), relax_rates)

    edge_y = swapped(edge_y, 1)
    edge_z = swapped(edge_z, 2)
    streamed, edge_yz, pool, share, chosen, records = call(
        stream_kernel,
        "stream",
        [
            ((Q * PITCH, LANES), F32),
            ((NX, LANES), F32),
            ((256, LANES), BF16),
            ((64, LANES), F32),
            ((32, LANES), F32),
            ((64, LANES), F32),
        ],
        [VMEM] * 2,
        cost=pl.CostEstimate(flops=10_000_000, bytes_accessed=8_000_000, transcendentals=0),
    )(collided, coarse_pops)

    streamed, right, left, payload, edge_yz, records = call(
        halo_kernel,
        "halo",
        [
            ((Q * PITCH, LANES), F32),
            ((72, LANES), F32),
            ((72, LANES), F32),
            ((PLANE, ROWS, LANES), BF16),
            ((NX, LANES), F32),
            ((64, LANES), F32),
        ],
        [VMEM] * 8,
        aliases={0: 0},
    )(streamed, edge_y, edge_z, edge_yz, chosen, pool, share, records)
    edge_yz = swapped(edge_yz, 3)

    near = [[PLANE * i + j for j in range(PLANE)] for i in range(PLANE)]
    far = [[PLANE * j + i for j in range(PLANE)] for i in range(PLANE)]
    payload = lax.all_to_all(payload, "blocks", 0, 0, axis_index_groups=near, tiled=True)
    ghost, line, own, route = call(
        tables_kernel,
        "tables",
        [((256, 384), BF16), ((EDGE, LANES), F32), ((64, LANES), F32), ((24, LANES), jnp.int32)],
        [VMEM] * 2,
        cost=pl.CostEstimate(flops=1_000_000, bytes_accessed=4_000_000, transcendentals=0),
    )(records, interface_pairs)
    payload, right, left = call(
        route_kernel,
        "route",
        [((PLANE, ROWS, LANES), BF16), ((72, LANES), F32), ((72, LANES), F32)],
        [VMEM] * 5,
    )(route, payload, edge_yz, right, left)
    payload = lax.all_to_all(payload, "blocks", 0, 0, axis_index_groups=far, tiled=True)
    ring = [(i, (i + 1) % BLOCKS) for i in range(BLOCKS)]
    right = lax.ppermute(right, "blocks", ring)
    left = lax.ppermute(left, "blocks", [(b, a) for a, b in ring])

    result, update = call(
        finish_kernel,
        "finish",
        [((Q * SPAN, LANES), F32), ((1, 2, Q * LANES), F32)],
        [VMEM] * 10,
        scratch=[pltpu.VMEM((32, LANES), F32)],
    )(streamed, edge_yz, right, left, payload, route, own, line, share, ghost)
    return result.reshape(1, Q, SPAN * LANES), update


def solution(mesh):
    placed = (
        P("group", None, "blocks"),
        P("group", "blocks"),
        P(),
        P("group", "blocks", None),
        P("group", None),
    )
    return jax.shard_map(
        body,
        mesh=mesh,
        in_specs=placed,
        out_specs=(P("group", None, "blocks"), P("group", "blocks", None)),
        check_vma=False,
    )
```

time: 47.6 us -> 43.5 us (0.914)
  waiting for transfers between devices: 15.5 us -> 12.1 us
  local copies, waits for them, and re-layouts: 3.34 us -> 1.88 us
  Pallas kernels: 6.44 us -> 7.37 us
    ppermute x3, waiting for transfers between devices: 6.24 us -> 4.93 us  [swapped(): return lax.ppermute(block, 'group', [(i, i ^ bits) for i in range(4)])]
    pallas_call x5 -> x6, Pallas kernels: 6.44 us -> 7.37 us  [the longest x1 2.92 us: body(): call(collide_kernel, 'collide', [((Q, SPAN, LANES), F32), ((2, NX, LANES)...]
    all_to_all x1, waiting for transfers between devices: 2.6 us -> 1.72 us  [body(): lax.all_to_all(payload, 'blocks', 0, 0, axis_index_groups=far, tiled=True)]
    convert_element_type x1 -> x0, local copies, waits for them, and re-layouts: 0.73 us -> none  [body(): records = coarse_pops.reshape(2 * Q, LANES).astype(F32)]
    unnamed x20 -> x6, local copies, waits for them, and re-layouts: 2.61 us -> 1.88 us
    all_to_all x1, waiting for transfers between devices: 3.45 us -> 2.75 us  [body(): lax.all_to_all(payload, 'blocks', 0, 0, axis_index_groups=near, tiled=True)]
  transfers between devices with their start and end apart: 7 -> 7, of which waited for: 6 -> 5; matrix products, arithmetic and copies ran while one was open for 2% -> 0% of each run, Pallas kernels for 1% -> 2%
where the time goes in v2:
time: 43.5 us; the launch traced here: 43.1 us
  starting transfers between devices  21 us (48%)
  waiting for transfers between devices  12.1 us (28%)
  Pallas kernels  7.37 us (17%)
  local copies, waits for them, and re-layouts  1.88 us (4%)
  between operations  0.67 us (2%)
    all_to_all x1, starting transfers between devices, body(): lax.all_to_all(payload, 'blocks', 0, 0, axis_index_groups=far, tiled=True)  8.47 us
    ppermute x1, starting transfers between devices, body(): left = lax.ppermute(left, 'blocks', [(b, a) for a, b in ring])  5.06 us
    ppermute x3, waiting for transfers between devices, swapped(): return lax.ppermute(block, 'group', [(i, i ^ bits) for i in range(4)])  4.93 us
    all_to_all x1, starting transfers between devices, body(): lax.all_to_all(payload, 'blocks', 0, 0, axis_index_groups=near, tiled=True)  4.47 us
    ppermute x3, starting transfers between devices, swapped(): return lax.ppermute(block, 'group', [(i, i ^ bits) for i in range(4)])  3.04 us
    pallas_call x1, Pallas kernels, body(): call(collide_kernel, 'collide', [((Q, SPAN, LANES), F32), ((2, NX, LANES)...  2.92 us
    all_to_all x1, waiting for transfers between devices, body(): lax.all_to_all(payload, 'blocks', 0, 0, axis_index_groups=near, tiled=True)  2.75 us
    ppermute x1, waiting for transfers between devices, body(): right = lax.ppermute(right, 'blocks', ring)  2.74 us
  transfers between devices with their start and end apart: 7, of which 5 were waited for; matrix products, arithmetic and copies ran while one was open for 0% of the time, Pallas kernels for 2%

profile of v2, /device:TPU:4, one launch (start us, length us, event | category | flops | bytes accessed | tf_op | source)
XLA Modules:
  0.0 43.1 jit_solution(13251932703172189965)
XLA Ops:
  0.6 2.9 %collide.1 = (f32[27,64,128]{2,1,0:T(8,128)}, f32[2,32,128]{2,1,0:T(8,128)}, f32[64,128]{1,0:T(8,128)}) custom-call(f32[27,64,128]{2,1,0:T(8,128)} %bitcast.3, s32[64,128]{1,0:T(8,128)} %bitcast.4, f32[27]{0:T(128)} %rates_hbm.1), custom_call_target="tpu_custom_call" | custom-call | tf_op jit(solution)/shard_map/collide/pallas_call | solution.py:588
  3.6 1.3 %collective-permute-start = (f32[2,32,128]{2,1,0:T(8,128)}, f32[2,32,128]{2,1,0:T(8,128)S(1)}, u32[]{:S(2)}, u32[]{:S(2)}) collective-permute-start(f32[2,32,128]{2,1,0:T(8,128)} %get-tuple-element.28), channel_id=1, source_target_pairs={{0,1},{1,0},{2,3},{3,2},{4,5},{5,4},{6,7},{7,6},{8,9},{9,8},{10,11... | collective-permute-start | bytes 98312 | tf_op jit(solution)/shard_map/ppermute | solution.py:584
  4.8 1.1 %collective-permute-start.1 = (f32[64,128]{1,0:T(8,128)}, f32[64,128]{1,0:T(8,128)S(1)}, u32[]{:S(2)}, u32[]{:S(2)}) collective-permute-start(f32[64,128]{1,0:T(8,128)} %get-tuple-element.29), channel_id=1, source_target_pairs={{0,2},{1,3},{2,0},{3,1},{4,6},{5,7},{6,4},{7,5},{8,10},{9,11},{10,... | collective-permute-start | bytes 98312 | tf_op jit(solution)/shard_map/ppermute | solution.py:584
  6.0 0.0 copy-start
  6.0 1.2 %copy-done = f32[27,64,128]{2,1,0:T(8,128)S(1)} copy-done((f32[27,64,128]{2,1,0:T(8,128)S(1)}, f32[27,64,128]{2,1,0:T(8,128)}, u32[]{:S(2)}) %copy-start) | copy-done | bytes 884760
  7.2 0.0 copy-start.1
  7.2 0.7 %copy-done.1 = bf16[1,2,3456]{2,1,0:T(2,128)(2,1)S(1)} copy-done((bf16[1,2,3456]{2,1,0:T(2,128)(2,1)S(1)}, bf16[1,2,3456]{2,1,0:T(2,128)(2,1)}, u32[]{:S(2)}) %copy-start.1) | copy-done | bytes 13848
  7.9 0.0 copy-start.2
  7.9 0.4 stream.1
  8.3 0.0 collective-permute-done.y_ref
  8.3 2.2 %collective-permute-done.1.z_ref = f32[64,128]{1,0:T(8,128)S(1)} collective-permute-done((f32[64,128]{1,0:T(8,128)}, f32[64,128]{1,0:T(8,128)S(1)}, u32[]{:S(2)}, u32[]{:S(2)}) %collective-permute-start.1) | collective-permute-done | bytes 32800 | tf_op jit(solution)/shard_map/ppermute | solution.py:584
  10.5 1.6 %halo.1 = (f32[2160,128]{1,0:T(8,128)S(1)}, f32[72,128]{1,0:T(8,128)S(1)}, f32[72,128]{1,0:T(8,128)S(1)}, bf16[8,80,128]{2,1,0:T(8,128)(2,1)}, f32[32,128]{1,0:T(8,128)S(1)}, /*index=5*/f32[64,128]{1,0:T(8,128)S(1)}) custom-call(f32[2160,128]{1,0:T(8,128)S(1)} %get-tuple-element.27.t_ref, ...), custom_call_target="tpu_custom_call", output_to_operand_aliasing={{0}: (0, {})} | custom-call | tf_op jit(solution)/shard_map/halo/pallas_call | solution.py:621
  12.1 4.5 %all-to-all-start = ((bf16[8,80,128]{2,1,0:T(8,128)(2,1)}), bf16[8,80,128]{2,1,0:T(8,128)(2,1)S(1)}, u32[]{:S(2)}, u32[]{:S(2)}) async-start(bf16[8,80,128]{2,1,0:T(8,128)(2,1)} %get-tuple-element.39), calls=%async_computation | async-start | bytes 327680 | tf_op jit(solution)/shard_map/all_to_all | solution.py:639
  16.5 0.6 %collective-permute-start.2 = (f32[32,128]{1,0:T(8,128)S(1)}, f32[32,128]{1,0:T(8,128)S(1)}, u32[]{:S(2)}, u32[]{:S(2)}) collective-permute-start(f32[32,128]{1,0:T(8,128)S(1)} %get-tuple-element.36), channel_id=1, source_target_pairs={{0,3},{1,2},{2,1},{3,0},{4,7},{5,6},{6,5},{7,4},{8,11},{9,10},{10,... | collective-permute-start | bytes 49160 | tf_op jit(solution)/shard_map/ppermute | solution.py:584
  17.2 0.0 copy-done.2
  17.2 0.4 tables.1
  17.5 2.7 %collective-permute-done.2.e_ref = f32[32,128]{1,0:T(8,128)S(1)} collective-permute-done((f32[32,128]{1,0:T(8,128)S(1)}, f32[32,128]{1,0:T(8,128)S(1)}, u32[]{:S(2)}, u32[]{:S(2)}) %collective-permute-start.2) | collective-permute-done | bytes 16416 | tf_op jit(solution)/shard_map/ppermute | solution.py:584
  20.3 2.7 %all-to-all-done.in_ref = bf16[8,80,128]{2,1,0:T(8,128)(2,1)S(1)} async-done(((bf16[8,80,128]{2,1,0:T(8,128)(2,1)}), bf16[8,80,128]{2,1,0:T(8,128)(2,1)S(1)}, u32[]{:S(2)}, u32[]{:S(2)}) %all-to-all-start) | async-done | bytes 163872 | tf_op jit(solution)/shard_map/all_to_all | solution.py:639
  23.0 0.8 %route.1 = (bf16[8,80,128]{2,1,0:T(8,128)(2,1)}, f32[72,128]{1,0:T(8,128)S(1)}, f32[72,128]{1,0:T(8,128)S(1)}) custom-call(s32[24,128]{1,0:T(8,128)S(1)} %get-tuple-element.38.route_ref, bf16[8,80,128]{2,1,0:T(8,128)(2,1)S(1)} %all-to-all-done.in_ref, f32[32,128]{1,0:T(8,128)S(1)} %collective-permute-done.2.e_ref, f32[72,128]{1,0:T(8,128)S(1)} %get-tuple-element.40.right_in, ...), custom_call_target="tpu_custom_call" | custom-call | tf_op jit(solution)/shard_map/route/pallas_call | solution.py:647
  23.9 8.5 %all-to-all-start.1 = ((bf16[8,80,128]{2,1,0:T(8,128)(2,1)}), bf16[8,80,128]{2,1,0:T(8,128)(2,1)S(1)}, u32[]{:S(2)}, u32[]{:S(2)}) async-start(bf16[8,80,128]{2,1,0:T(8,128)(2,1)} %get-tuple-element.44), calls=%async_computation.1 | async-start | bytes 327680 | tf_op jit(solution)/shard_map/all_to_all | solution.py:653
  32.3 0.0 collective-permute-start.3
  32.3 5.1 %collective-permute-start.4 = (f32[72,128]{1,0:T(8,128)S(1)}, f32[72,128]{1,0:T(8,128)S(1)}, u32[]{:S(2)}, u32[]{:S(2)}) collective-permute-start(f32[72,128]{1,0:T(8,128)S(1)} %get-tuple-element.43), channel_id=1, source_target_pairs={{4,0},{8,4},{12,8},{16,12},{20,16},{24,20},{28,24},{32,28},{36,32}... | collective-permute-start | bytes 110600 | tf_op jit(solution)/shard_map/ppermute | solution.py:656
  37.4 2.7 %collective-permute-done.3.right_ref = f32[72,128]{1,0:T(8,128)S(1)} collective-permute-done((f32[72,128]{1,0:T(8,128)S(1)}, f32[72,128]{1,0:T(8,128)S(1)}, u32[]{:S(2)}, u32[]{:S(2)}) %collective-permute-start.3) | collective-permute-done | bytes 36896 | tf_op jit(solution)/shard_map/ppermute | solution.py:655
  40.1 0.0 collective-permute-done.4.left_ref
  40.2 1.7 %all-to-all-done.1.in_ref = bf16[8,80,128]{2,1,0:T(8,128)(2,1)S(1)} async-done(((bf16[8,80,128]{2,1,0:T(8,128)(2,1)}), bf16[8,80,128]{2,1,0:T(8,128)(2,1)S(1)}, u32[]{:S(2)}, u32[]{:S(2)}) %all-to-all-start.1) | async-done | bytes 163872 | tf_op jit(solution)/shard_map/all_to_all | solution.py:653
  41.9 1.2 %finish.1 = (f32[1728,128]{1,0:T(8,128)}, f32[1,2,3456]{2,1,0:T(2,128)}) custom-call(f32[2160,128]{1,0:T(8,128)S(1)} %get-tuple-element.35.t_ref, f32[32,128]{1,0:T(8,128)S(1)} %collective-permute-done.2.e_ref, f32[72,128]{1,0:T(8,128)S(1)} %collective-permute-done.3.right_ref, f32[72,128]{1,0:T(8,128)S(1)} %collective-permute-done.4.left_ref, ...), custom_call_target="tpu_custom_call" | custom-call | tf_op jit(solution)/shard_map/finish/pallas_call | solution.py:658
Async XLA Ops:
  3.6 4.7 %collective-permute-start = (f32[2,32,128]{2,1,0:T(8,128)}, f32[2,32,128]{2,1,0:T(8,128)S(1)}, u32[]{:S(2)}, u32[]{:S(2)}) collective-permute-start(f32[2,32,128]{2,1,0:T(8,128)} %get-tuple-element.28), channel_id=1, source_target_pairs={{0,1},{1,0},{2,3},{3,2},{4,5},{5,4},{6,7},{7,6},{8,9},{9,8},{10,11... | collective-permute-start | bytes 98312 | tf_op jit(solution)/shard_map/ppermute | solution.py:584
  4.8 5.6 %collective-permute-start.1 = (f32[64,128]{1,0:T(8,128)}, f32[64,128]{1,0:T(8,128)S(1)}, u32[]{:S(2)}, u32[]{:S(2)}) collective-permute-start(f32[64,128]{1,0:T(8,128)} %get-tuple-element.29), channel_id=1, source_target_pairs={{0,2},{1,3},{2,0},{3,1},{4,6},{5,7},{6,4},{7,5},{8,10},{9,11},{10,... | collective-permute-start | bytes 98312 | tf_op jit(solution)/shard_map/ppermute | solution.py:584
  6.0 1.2 %copy-start = (f32[27,64,128]{2,1,0:T(8,128)S(1)}, f32[27,64,128]{2,1,0:T(8,128)}, u32[]{:S(2)}) copy-start(f32[27,64,128]{2,1,0:T(8,128)} %get-tuple-element.26.w_ref) | copy-start | bytes 2654212
  7.2 0.7 %copy-start.1 = (bf16[1,2,3456]{2,1,0:T(2,128)(2,1)S(1)}, bf16[1,2,3456]{2,1,0:T(2,128)(2,1)}, u32[]{:S(2)}) copy-start(bf16[1,2,3456]{2,1,0:T(2,128)(2,1)} %coarse_ref.1) | copy-start | bytes 41476
  7.9 9.3 %copy-start.2 = (s32[1,128]{1,0:T(1,128)S(1)}, s32[1,128]{1,0:T(1,128)}, u32[]{:S(2)}) copy-start(s32[1,128]{1,0:T(1,128)} %pairs_ref.1) | copy-start | bytes 1540
  12.1 11.0 %all-to-all-start = ((bf16[8,80,128]{2,1,0:T(8,128)(2,1)}), bf16[8,80,128]{2,1,0:T(8,128)(2,1)S(1)}, u32[]{:S(2)}, u32[]{:S(2)}) async-start(bf16[8,80,128]{2,1,0:T(8,128)(2,1)} %get-tuple-element.39), calls=%async_computation | async-start | bytes 327680 | tf_op jit(solution)/shard_map/all_to_all | solution.py:639
  16.5 3.7 %collective-permute-start.2 = (f32[32,128]{1,0:T(8,128)S(1)}, f32[32,128]{1,0:T(8,128)S(1)}, u32[]{:S(2)}, u32[]{:S(2)}) collective-permute-start(f32[32,128]{1,0:T(8,128)S(1)} %get-tuple-element.36), channel_id=1, source_target_pairs={{0,3},{1,2},{2,1},{3,0},{4,7},{5,6},{6,5},{7,4},{8,11},{9,10},{10,... | collective-permute-start | bytes 49160 | tf_op jit(solution)/shard_map/ppermute | solution.py:584
  23.9 18.0 %all-to-all-start.1 = ((bf16[8,80,128]{2,1,0:T(8,128)(2,1)}), bf16[8,80,128]{2,1,0:T(8,128)(2,1)S(1)}, u32[]{:S(2)}, u32[]{:S(2)}) async-start(bf16[8,80,128]{2,1,0:T(8,128)(2,1)} %get-tuple-element.44), calls=%async_computation.1 | async-start | bytes 327680 | tf_op jit(solution)/shard_map/all_to_all | solution.py:653
  32.3 7.8 %collective-permute-start.3 = (f32[72,128]{1,0:T(8,128)S(1)}, f32[72,128]{1,0:T(8,128)S(1)}, u32[]{:S(2)}, u32[]{:S(2)}) collective-permute-start(f32[72,128]{1,0:T(8,128)S(1)} %get-tuple-element.42), channel_id=1, source_target_pairs={{0,4},{4,8},{8,12},{12,16},{16,20},{20,24},{24,28},{28,32},{32,36}... | collective-permute-start | bytes 110600 | tf_op jit(solution)/shard_map/ppermute | solution.py:655
  32.3 7.8 %collective-permute-start.4 = (f32[72,128]{1,0:T(8,128)S(1)}, f32[72,128]{1,0:T(8,128)S(1)}, u32[]{:S(2)}, u32[]{:S(2)}) collective-permute-start(f32[72,128]{1,0:T(8,128)S(1)} %get-tuple-element.43), channel_id=1, source_target_pairs={{4,0},{8,4},{12,8},{16,12},{20,16},{24,20},{28,24},{32,28},{36,32}... | collective-permute-start | bytes 110600 | tf_op jit(solution)/shard_map/ppermute | solution.py:656

commit v3 on v2

--- a/solution.py
+++ b/solution.py
@@ -15,8 +15,11 @@
 LANES = 128
 PLANE = 8
 BLOCKS = PLANE * PLANE
-LOW, HIGH, SHARED, CENTRE, RECORDS, ROWS = 54, 55, 56, 57, 62, 80
+LOW, HIGH, LAST_LOW, LAST_HIGH, CENTRE, RECORDS, ROWS = 54, 55, 56, 57, 58, 62, 80
+TILE = 16
 MIXED = 48
+POOLED = 8 * (2 * Q + 4)
+ENDS = 32
 PAIRS = [(i // 9, i // 3 % 3, i % 3) for i in range(Q)]
 F32 = jnp.float32
 BF16 = jnp.bfloat16
@@ -83,7 +86,7 @@
     face, a, b = record_ids(shape, 1)
     column = (row >= Q).astype(jnp.int32)
     index = jnp.where(row < LOW, row - Q * column, jnp.where(row == LOW, 18 + a, a))
-    index = jnp.where(row == SHARED, jnp.where(a == 7, 26, 8), index)
+    index = jnp.where(row == LAST_LOW, 26, jnp.where(row == LAST_HIGH, 8, index))
     by_x, by_y, by_z = digits(index)
     in_y, in_z = by_y == 2 * (1 - side_y), by_z == 2 * (1 - side_z)
     half_y = in_y & ((face == 0) | (b == 7 * side_y))
@@ -92,8 +95,18 @@
     high = (by_x == 0) & (column == 1) & (a == HALF - 1)
     half_x = (row >= LOW) | low | high
     share = jnp.where(half_y, 0.5, 1.0) * jnp.where(half_z, 0.5, 1.0) * jnp.where(half_x, 0.5, 1.0)
-    held = (row <= HIGH) | ((row == SHARED) & ((a == 0) | (a == 7)))
+    held = (row <= HIGH) | ((row == LAST_LOW) & (a == 7)) | ((row == LAST_HIGH) & (a == 0))
     return jnp.where(held, share, 0.0)
+
+
+def chosen_table():
+    shape = (64, POOLED)
+    target, block = ids(shape, 0), ids(shape, 1) >> 3
+    second = (target >= Q).astype(jnp.int32)
+    wanted = jnp.where(target < LOW, 2 * (target - Q * second) + second, -1)
+    wanted = jnp.where(target == LOW, 54, jnp.where(target == HIGH, 56, wanted))
+    wanted = jnp.where(target == LAST_LOW, 55, jnp.where(target == LAST_HIGH, 57, wanted))
+    return (wanted == block).astype(F32).astype(BF16)
 
 
 def ghost_table():
@@ -196,7 +209,7 @@
 
 
 def collide_kernel(
-    g_hbm, solid_hbm, rates_hbm, w_hbm, y_ref, z_ref, g_ref, w_ref, solid_ref, rates_ref, sems
+    g_hbm, solid_hbm, rates_hbm, w_ref, y_ref, z_ref, g_ref, solid_ref, rates_ref, sems
 ):
     pieces = 4
     size = SPAN // pieces
@@ -233,12 +246,6 @@
     for piece in range(pieces):
         copies[2 + piece].wait()
         lax.fori_loop(size // 8 * piece, size // 8 * (piece + 1), chunk, 0)
-        rows = pl.ds(size * piece, size)
-        copy = pltpu.make_async_copy(
-            w_ref.at[:, rows, :], w_hbm.at[:, rows, :], sems.at[pieces + 2 + piece]
-        )
-        copy.start()
-        copies.append(copy)
 
     send_y, send_z = 2 * (1 - side_y), 2 * (1 - side_z)
     tile, base, inner = geometry()
@@ -249,17 +256,15 @@
         value = w_ref[index, pl.ds(tile, NX, stride=2), :]
         value = rolled(value, (16 * (k % 8) - base) & 127)
         packed[k // 8] = jnp.where(lanes >> 4 == k % 8, value, packed[k // 8])
-    y_ref[0] = packed[0]
-    y_ref[1] = packed[1]
+    y_ref[0] = (packed[0] - 1.0).astype(BF16)
+    y_ref[1] = (packed[1] - 1.0).astype(BF16)
     lanes = ids((SPAN, LANES), 1)
     packed_z = jnp.zeros((SPAN, LANES), F32)
     for k in range(9):
         index = 9 * (k // 3) + 3 * (k % 3) + send_z
         value = w_ref[index]
         packed_z = jnp.where(lanes & 15 == k, rolled(value, (k - inner) & 127), packed_z)
-    z_ref[...] = packed_z
-    for copy in copies[2 + pieces :]:
-        copy.wait()
+    z_ref[...] = (packed_z - 1.0).astype(BF16)
 
 
 def moved(value, b, shift):
@@ -278,7 +283,11 @@
     return lanes & 15 <= 14 if c == 0 else lanes & 15 >= 1
 
 
-def stream_kernel(w_ref, coarse_ref, t_ref, e_ref, pool_ref, share_ref, rec_ref, p_ref):
+def stream_kernel(
+    w_ref, coarse_hbm, t_ref, e_ref, pool_ref, share_ref, rec_ref, p_ref, chosen_ref, coarse_ref, sem
+):
+    copy = pltpu.make_async_copy(coarse_hbm, coarse_ref, sem)
+    copy.start()
     lanes = ids((8, LANES), 1)
     zeros = jnp.zeros((8, LANES), F32)
     for i, (a, b, c) in enumerate(PAIRS):
@@ -304,6 +313,7 @@
     e_ref[...] = packed
 
     p_ref[...] = jnp.zeros((64, LANES), F32)
+    copy.wait()
     records = coarse_ref[0].astype(F32)
     for t in range(2):
         for i in range(Q):
@@ -320,45 +330,46 @@
 
     pool_ref[...] = pool_table()
     share_ref[...] = share_table()
+    chosen_ref[...] = chosen_table()
 
 
 def halo_kernel(
-    t_ref, y_ref, z_ref, e_ref, rec_ref, pool_ref, share_ref, p_ref,
-    out_ref, right_ref, left_ref, pay_ref, edge_ref, kept_ref,
+    t_ref, y_ref, z_ref, e_ref, rec_ref, pool_ref, share_ref, p_ref, chosen_ref,
+    out_ref, right_ref, left_ref, pay_ref, kept_ref,
 ):
     del t_ref
     kept_ref[...] = p_ref[...]
     side_y, side_z = sides()
     halo_y, halo_z = 2 * side_y, 2 * side_z
     tile, base, inner = geometry()
-    edge_ref[...] = e_ref[...]
 
     lanes = ids((NX, LANES), 1)
     row_mask = lanes >> 4 == base >> 4
     for k in range(9):
         a, c = k // 3, k % 3
-        value = rolled(y_ref[k // 8], (base - 16 * (k % 8) + c - 1) & 127)
+        value = rolled(y_ref[k // 8].astype(F32) + 1.0, (base - 16 * (k % 8) + c - 1) & 127)
         mask = row_mask if c == 1 else row_mask & z_inside(lanes, c)
         index = 9 * a + 3 * halo_y + c
         rows = pl.ds(PITCH * index + FIRST + 2 * (a - 1) + tile, NX, stride=2)
         out_ref[rows, :] = out_ref[rows, :] + jnp.where(mask, value, 0.0)
-    lanes = ids((8, LANES), 1)
+    lanes = ids((TILE, LANES), 1)
     for k in range(9):
         a, b = k // 3, k % 3
         shift = (inner - k + 16 * (b - 1)) & 127
         index = 9 * a + 3 * b + halo_z
-        for row in range(0, SPAN, 8):
-            value = moved(z_ref[pl.ds(row, 8), :], b, shift)
-            rows = pl.ds(PITCH * index + FIRST + row + 2 * (a - 1), 8)
+        for row in range(0, SPAN, TILE):
+            value = moved(z_ref[row : row + TILE].astype(F32) + 1.0, b, shift)
+            rows = pl.ds(PITCH * index + FIRST + row + 2 * (a - 1), TILE)
             out_ref[rows, :] = out_ref[rows, :] + jnp.where(lanes & 15 == inner, value, 0.0)
 
     for k in range(9):
-        right_ref[8 * k : 8 * k + 8, :] = out_ref[pl.ds(PITCH * (18 + k) + FIRST + SPAN, 8), :]
-        left_ref[8 * k : 8 * k + 8, :] = out_ref[pl.ds(PITCH * k, 8), :]
+        right_ref[2 * k : 2 * k + 2, :] = out_ref[pl.ds(PITCH * (18 + k) + FIRST + SPAN, 2), :]
+        left_ref[2 * k : 2 * k + 2, :] = out_ref[pl.ds(PITCH * k + FIRST - 2, 2), :]
+    right_ref[24:ENDS, :] = e_ref[NX - 8 : NX, :]
+    left_ref[24:ENDS, :] = e_ref[0:8, :]
 
     row_8 = ids((8, LANES), 0)
-    total = 8 * (2 * Q + 4)
-    pooled = jnp.zeros((total, LANES), F32)
+    tiles = []
     for h in range(2):
         parts = []
         for i in range(Q):
@@ -373,18 +384,14 @@
         parts.append(jnp.where(row_8 == 7, last, 0.0))
         parts.append(out_ref[pl.ds(under, 8, stride=PITCH), :])
         parts.append(out_ref[pl.ds(PITCH * 8 + under, 8, stride=PITCH), :])
-        for part in split_bf16(jnp.concatenate(parts, 0)):
-            pooled = pooled + dot(part, pool_ref[LANES * h : LANES * (h + 1), :])
-    pooled = jnp.where(ids((total, LANES), 0) & 7 == ids((total, LANES), 1) >> 3 & 7, pooled, 0.0)
-    target, block = ids((64, total), 0), ids((64, total), 1) >> 3
-    second = (target >= Q).astype(jnp.int32)
-    wanted = jnp.where(target < LOW, 2 * (target - Q * second) + second, -1)
-    wanted = jnp.where(target == LOW, 54, jnp.where(target == HIGH, 56, wanted))
-    chosen = (wanted == block) | ((target == SHARED) & ((block == 55) | (block == 57)))
-    chosen = chosen.astype(F32).astype(BF16)
-    routed = jnp.zeros((64, LANES), F32)
-    for part in split_bf16(pooled):
-        routed = routed + dot(chosen, part)
+        tiles.append(jnp.concatenate(parts, 0))
+    pool = pool_ref[...]
+    high, low = split_bf16(jnp.concatenate(tiles, 1))
+    pooled = dot(high, pool) + dot(low, pool)
+    pooled = jnp.where(ids((POOLED, LANES), 0) & 7 == ids((POOLED, LANES), 1) >> 3 & 7, pooled, 0.0)
+    chosen = chosen_ref[...]
+    high, low = split_bf16(pooled)
+    routed = dot(chosen, high) + dot(chosen, low)
 
     share = share_ref[...]
     rows, lane_a = ids((64, LANES), 0), ids((64, LANES), 1) >> 3 & 7
@@ -395,7 +402,7 @@
     parts = jnp.sum(parts, axis=1, keepdims=True)
     centre = (held / parts).astype(BF16).astype(F32)
     routed = routed - centre * share
-    is_centre = (rows == CENTRE) | ((rows == SHARED) & ((lane_a == 1) | (lane_a == 6)))
+    is_centre = (rows == CENTRE) | ((rows == LAST_LOW) & (lane_a == 6)) | ((rows == LAST_HIGH) & (lane_a == 1))
     routed = jnp.where(is_centre, centre, routed)
     payload = jnp.where(rows[MIXED:64] >= RECORDS, rec_ref[0:16], routed[MIXED:64])
     payload = jnp.concatenate([routed[0:MIXED], payload, rec_ref[16:32]], 0).astype(BF16)
@@ -403,7 +410,7 @@
         pay_ref[slot] = payload
 
 
-def tables_kernel(p_ref, pairs_ref, ghost_ref, line_ref, own_ref, route_ref):
+def tables_kernel(p_ref, pairs_ref, ghost_ref, line_ref, own_ref, route_ref, last_ref, flag_ref):
     side_y, side_z = sides()
     ghost = ghost_table()
     ghost_ref[0:LANES] = ghost
@@ -420,132 +427,131 @@
         own_ref[32 * t : 32 * t + 32] = value - jnp.where(in_y & in_z, rows[:, 256:384], 0.0)
 
     me = lax.axis_index("blocks")
-    pairs = jnp.broadcast_to(pairs_ref[...], (8, LANES))
-    lanes = ids((8, LANES), 1)
-    devices = PLANE * ids((8, LANES), 0) + (me & (PLANE - 1))
+    pairs = pairs_ref[...]
+    rows, lanes = ids((LANES, LANES), 0), ids((LANES, LANES), 1)
 
     def total(mask, value):
         value = jnp.where(mask, value.astype(F32), 0.0)
-        return jnp.broadcast_to(jnp.sum(value, axis=1, keepdims=True), (8, LANES)).astype(jnp.int32)
-
-    route_ref[0:8] = total(lanes == 2 * devices, pairs >> 1)
-    route_ref[8:16] = total(pairs == 2 * devices, lanes >> 1)
-    rows = ids((8, LANES), 0)
-    mine = total(lanes == 2 * me, pairs)
-    held = total(pairs == 2 * me, lanes)
-    route_ref[16:24] = jnp.where(
-        rows == 0, mine >> 1, jnp.where(rows == 1, held >> 1, jnp.where(rows == 2, held & 1, mine & 1))
-    )
-
-
-def pick(route, mask, in_ref, rows):
-    chosen = None
-    for member in range(PLANE):
-        value = in_ref[member, rows].astype(F32)
-        chosen = value if chosen is None else jnp.where((route & mask) == member, value, chosen)
-    return chosen
-
-
-def route_kernel(route_ref, in_ref, e_ref, right_in, left_in, out_ref, right_ref, left_ref):
-    rows, lane_a = ids((16, LANES), 0) + MIXED, ids((16, LANES), 1) >> 3 & 7
-    from_low = (rows == LOW) | ((rows == SHARED) & (lane_a >= 4))
-    from_high = (rows == HIGH) | ((rows == SHARED) & (lane_a < 4))
-    from_holder = rows >= RECORDS
-    for plane in range(PLANE):
-        owner = route_ref[plane : plane + 1, :]
-        holder = route_ref[8 + plane : 9 + plane, :]
-        mixed = jnp.where(from_holder, holder, owner)
-        mixed = jnp.where(from_low, owner - 1, jnp.where(from_high, owner + 1, mixed))
-        for start in range(0, ROWS, 16):
-            route = owner if start < MIXED else mixed if start == MIXED else holder
-            route = jnp.broadcast_to(route, (16, LANES))
-            value = pick(route, PLANE - 1, in_ref, slice(start, start + 16))
-            out_ref[plane, start : start + 16] = value.astype(BF16)
-
+        value = jnp.sum(value, axis=1, keepdims=True)
+        return jnp.broadcast_to(value, mask.shape).astype(jnp.int32)
+
+    def matrices(ref, owner, holder, source, rows, lanes):
+        place = rows & (TILE - 1)
+        low = (place == LOW - MIXED) | (place == LAST_LOW - MIXED)
+        high = (place == HIGH - MIXED) | (place == LAST_HIGH - MIXED)
+        mixed = jnp.where(low, owner - 1, jnp.where(high, owner + 1, owner))
+        mixed = jnp.where(place >= RECORDS - MIXED, holder, mixed)
+        for kind, route in enumerate((owner, mixed, holder)):
+            chosen = (source(route) == lanes >> 4) & (place == lanes & (TILE - 1))
+            ref[kind] = chosen.astype(F32).astype(BF16)
+
+    device = PLANE * (rows >> 4) + (me & (PLANE - 1))
+    pairs = jnp.broadcast_to(pairs, (LANES, LANES))
+    owner = total(lanes == 2 * device, pairs >> 1)
+    holder = total(pairs == 2 * device, lanes >> 1)
+    matrices(route_ref, owner, holder, lambda route: route & (PLANE - 1), rows, lanes)
+    rows, lanes, pairs = rows[0:TILE], lanes[0:TILE], pairs[0:TILE]
+    serves = total(lanes == 2 * me, pairs)
+    record = total(pairs == 2 * me, lanes)
+    matrices(last_ref, serves >> 1, record >> 1, lambda route: (route & (BLOCKS - 1)) >> 3, rows, lanes)
+    flag_ref[...] = jnp.where(rows[0:8] == 0, record[0:8] & 1, serves[0:8] & 1)
+
+
+def passed_on(matrix_ref, in_ref):
+    for start in range(0, ROWS, TILE):
+        kind = 0 if start < MIXED else 1 if start == MIXED else 2
+        tile = [in_ref[member, start : start + TILE] for member in range(PLANE)]
+        yield start, dot(matrix_ref[kind], jnp.concatenate(tile, 0))
+
+
+def route_kernel(route_ref, in_ref, e_ref, right_ref, left_ref, out_ref, edge_ref):
+    for start, rows in passed_on(route_ref, in_ref):
+        rows = rows.astype(BF16)
+        for plane in range(PLANE):
+            out_ref[plane, start : start + TILE] = rows[TILE * plane : TILE * (plane + 1)]
+    edge_ref[0:NX, :] = e_ref[...]
+    edge_ref[NX : NX + 8, :] = right_ref[24:ENDS, :]
+    edge_ref[NX + 8 : NX + 16, :] = left_ref[24:ENDS, :]
+
+
+def merge_kernel(t_ref, e_ref, right_ref, left_ref, next_ref):
     side_y, side_z = sides()
     tile, base, inner = geometry()
-    right_ref[...] = right_in[...]
-    left_ref[...] = left_in[...]
-    corner = 8 * (6 * side_y + 2 * side_z)
-    lanes = ids((1, LANES), 1)
-    for ref, layer, a, row in ((right_ref, NX - 1, 2, 0), (left_ref, 0, 0, 6)):
-        value = rolled(e_ref[layer : layer + 1, :], (base + inner - a) & 127)
-        at = pl.ds(corner + row + tile, 1)
-        ref[at, :] = ref[at, :] + jnp.where(lanes == base + inner, value, 0.0)
+    for i in range(Q):
+        next_ref[i] = t_ref[PITCH * i + FIRST : PITCH * i + FIRST + SPAN, :]
+    for k in range(9):
+        next_ref[18 + k, 0:2] = next_ref[18 + k, 0:2] + right_ref[2 * k : 2 * k + 2, :]
+        next_ref[k, SPAN - 2 : SPAN] = next_ref[k, SPAN - 2 : SPAN] + left_ref[2 * k : 2 * k + 2, :]
+    rows, lanes = ids((NX, LANES), 0), ids((NX, LANES), 1)
+    corner = e_ref[0:NX, :]
+    low = jnp.where(rows == 0, e_ref[NX + 7 : NX + 8, :], pltpu.roll(corner, 1, 0))
+    high = jnp.where(rows == NX - 1, e_ref[NX + 8 : NX + 9, :], pltpu.roll(corner, NX - 1, 0))
+    for a, value in ((0, high), (1, corner), (2, low)):
+        index = 9 * a + 6 * side_y + 2 * side_z
+        value = rolled(value, (base + inner - a) & 127)
+        at = pl.ds(tile, NX, stride=2)
+        next_ref[index, at, :] = next_ref[index, at, :] + jnp.where(lanes == base + inner, value, 0.0)
 
 
 def finish_kernel(
-    t_ref, e_ref, right_ref, left_ref, in_ref, route_ref, own_ref, line_ref, share_ref, ghost_ref,
-    next_ref, update_ref,
-    p_ref,
+    base_ref, in_ref, last_ref, flag_ref, own_ref, line_ref, share_ref, ghost_ref,
+    value_ref, next_hbm, update_hbm,
+    update_ref, sems,
 ):
-    side_y, side_z = sides()
-    tile, base, inner = geometry()
+    del base_ref
+    side_y, side_z = sides()
     in_y, in_z = 2 * (1 - side_y), 2 * (1 - side_z)
-    for i in range(Q):
-        next_ref[SPAN * i : SPAN * (i + 1), :] = t_ref[PITCH * i + FIRST : PITCH * i + FIRST + SPAN, :]
-
-    holder = jnp.broadcast_to(route_ref[17:18, :], (32, LANES)) >> 3
-    p_ref[...] = pick(holder, PLANE - 1, in_ref, slice(MIXED, ROWS))
-    swap = route_ref[18:19, :] == 1
+    copies = []
+
+    def send(source, target):
+        copy = pltpu.make_async_copy(source, target, sems.at[len(copies)])
+        copy.start()
+        copies.append(copy)
+
+    rows = jnp.concatenate([tile for _, tile in passed_on(last_ref, in_ref)], 0)
+    swap = flag_ref[0:1, :] == 1
     lines = line_ref[...]
     scaled = []
     for k in range(9):
-        row = RECORDS - MIXED + k
-        first, second = p_ref[row : row + 1, :], p_ref[row + 9 : row + 10, :]
+        row = RECORDS + k
+        first, second = rows[row : row + 1], rows[row + 9 : row + 10]
         scaled.append(lines * jnp.where(swap, second, first))
         scaled.append(lines * jnp.where(swap, first, second))
     scaled = jnp.concatenate(scaled, 0)
     ghost = dot(jnp.concatenate(split_bf16(scaled), 1), ghost_ref[...])
-    for k in range(9):
-        index = 9 * (k // 3) + 3 * (k % 3) + in_z
-        for h in range(2):
-            rows = pl.ds(SPAN * index + h, NX, stride=2)
-            part = ghost[NX * k : NX * (k + 1), LANES * (h + 1) : LANES * (h + 2)]
-            next_ref[rows, :] = next_ref[rows, :] + part
     lanes = ids((NX, LANES), 1)
     outer = lanes >> 4 == 7 * side_y
-    for k in range(9):
-        index = 9 * (k // 3) + 3 * in_y + k % 3
-        rows = pl.ds(SPAN * index + side_y, NX, stride=2)
-        next_ref[rows, :] = jnp.where(outer, ghost[NX * k : NX * (k + 1), 0:LANES], next_ref[rows, :])
-    for k in range(9):
-        rows = pl.ds(SPAN * (18 + k), 8)
-        next_ref[rows, :] = next_ref[rows, :] + right_ref[8 * k : 8 * k + 8, :]
-        rows = pl.ds(SPAN * k + SPAN - 8, 8)
-        next_ref[rows, :] = next_ref[rows, :] + left_ref[8 * k : 8 * k + 8, :]
     for a in range(3):
-        index = 9 * a + 6 * side_y + 2 * side_z
-        low, high = (0, NX - (a - 1)) if a >= 1 else (1, NX)
-        value = rolled(e_ref[low:high, :], (base + inner - a) & 127)
-        value = jnp.where(lanes[low:high] == base + inner, value, 0.0)
-        rows = pl.ds(SPAN * index + 2 * (low + a - 1) + tile, high - low, stride=2)
-        next_ref[rows, :] = next_ref[rows, :] + value
-
-    owner = route_ref[16:17, :]
-    main = pick(jnp.broadcast_to(owner, (64, LANES)) >> 3, PLANE - 1, in_ref, slice(0, 64))
-    owner = jnp.broadcast_to(owner, (16, LANES))
-    lower = pick((owner + BLOCKS - 1) >> 3, PLANE - 1, in_ref, slice(MIXED, 64))
-    upper = pick((owner + 1) >> 3, PLANE - 1, in_ref, slice(MIXED, 64))
+        for b in range(3):
+            k = 3 * a + b
+            for h in range(2):
+                at = pl.ds(h, NX, stride=2)
+                part = ghost[NX * k : NX * (k + 1), LANES * (h + 1) : LANES * (h + 2)]
+                value_ref[9 * a + 3 * b + in_z, at, :] = value_ref[9 * a + 3 * b + in_z, at, :] + part
+        for c in range(3):
+            k = 3 * a + c
+            at = pl.ds(side_y, NX, stride=2)
+            part = ghost[NX * k : NX * (k + 1), 0:LANES]
+            value = value_ref[9 * a + 3 * in_y + c, at, :]
+            value_ref[9 * a + 3 * in_y + c, at, :] = jnp.where(outer, part, value)
+        send(value_ref.at[pl.ds(9 * a, 9)], next_hbm.at[pl.ds(9 * a, 9)])
+
     share = share_ref[...]
-    main = main[0:LOW] + main[CENTRE : CENTRE + 1] * share[0:LOW]
-    shared = SHARED - 48
     lane_1 = ids((1, LANES), 1)
-    low_centre = jnp.sum(jnp.where(lane_1 == 48, lower[shared : shared + 1], 0.0), axis=1, keepdims=True)
-    high_centre = jnp.sum(jnp.where(lane_1 == 8, upper[shared : shared + 1], 0.0), axis=1, keepdims=True)
-    lower = lower + low_centre * share[48:64]
-    upper = upper + high_centre * share[48:64]
-    rows, lane_a = ids((32, LANES), 0), ids((32, LANES), 1) >> 3 & 7
-    from_low = jnp.where(
-        rows == 26,
-        jnp.where(lane_a == 7, lower[shared : shared + 1], 0.0),
-        jnp.where(rows - 18 == lane_a, lower[LOW - 48 : LOW - 47], 0.0),
+    low_centre = jnp.sum(jnp.where(lane_1 == 48, rows[LAST_LOW : LAST_LOW + 1], 0.0), axis=1, keepdims=True)
+    high_centre = jnp.sum(jnp.where(lane_1 == 8, rows[LAST_HIGH : LAST_HIGH + 1], 0.0), axis=1, keepdims=True)
+    main = rows[0:LOW] + rows[CENTRE : CENTRE + 1] * share[0:LOW]
+    low, high, last_low, last_high = (
+        rows[row : row + 1] + centre * share[row : row + 1]
+        for row, centre in (
+            (LOW, low_centre), (HIGH, high_centre), (LAST_LOW, low_centre), (LAST_HIGH, high_centre)
+        )
     )
-    from_high = jnp.where(
-        rows == 8,
-        jnp.where(lane_a == 0, upper[shared : shared + 1], 0.0),
-        jnp.where(rows == lane_a, upper[HIGH - 48 : HIGH - 47], 0.0),
-    )
+    row, lane_a = ids((32, LANES), 0), ids((32, LANES), 1) >> 3 & 7
+    from_low = jnp.where(row - 18 == lane_a, low, 0.0)
+    from_low = jnp.where(row == 26, jnp.where(lane_a == 7, last_low, 0.0), from_low)
+    from_high = jnp.where(row == lane_a, high, 0.0)
+    from_high = jnp.where(row == 8, jnp.where(lane_a == 0, last_high, 0.0), from_high)
     lane_in, lane_out = ids((LANES, LANES), 0), ids((LANES, LANES), 1)
     alike = (lane_in >> 6 == lane_out >> 6) & (lane_in & 7 == lane_out & 7)
     alike = alike.astype(F32).astype(BF16)
@@ -554,12 +560,15 @@
         edges = edges + dot(part, alike)
     column_0 = main[0:Q] + jnp.where(lane_a == 0, edges[0:32], 0.0)[0:Q]
     column_1 = main[Q : 2 * Q] + jnp.where(lane_a == HALF - 1, edges[32:64], 0.0)[0:Q]
-    crossed = jnp.broadcast_to(route_ref[19:20, :], (Q, LANES)) == 1
+    crossed = jnp.broadcast_to(flag_ref[1:2, :], (Q, LANES)) == 1
     for t in range(2):
         here, there = (column_0, column_1) if t == 0 else (column_1, column_0)
         value = jnp.where(crossed, there, here) + own_ref[32 * t : 32 * t + Q, :]
         for i in range(Q):
             update_ref[0, t : t + 1, LANES * i : LANES * (i + 1)] = value[i : i + 1]
+    send(update_ref, update_hbm)
+    for copy in copies:
+        copy.wait()
 
 
 VMEM = pl.BlockSpec(memory_space=pltpu.VMEM)
@@ -580,6 +589,10 @@
     )
 
 
+def in_hbm(value):
+    return pltpu.with_memory_space_constraint(value, pltpu.HBM)
+
+
 def swapped(block, bits):
     return lax.ppermute(block, "group", [(i, i ^ bits) for i in range(4)])
 
@@ -588,22 +601,23 @@
     collided, edge_y, edge_z = call(
         collide_kernel,
         "collide",
-        [((Q, SPAN, LANES), F32), ((2, NX, LANES), F32), ((SPAN, LANES), F32)],
+        [((Q, SPAN, LANES), F32), ((2, NX, LANES), BF16), ((SPAN, LANES), BF16)],
         [HBM] * 3,
-        (HBM, VMEM, VMEM),
-        [
-            pltpu.VMEM((Q, SPAN, LANES), F32),
+        scratch=[
             pltpu.VMEM((Q, SPAN, LANES), F32),
             pltpu.VMEM((SPAN, LANES), jnp.int32),
             pltpu.SMEM((Q,), F32),
-            pltpu.SemaphoreType.DMA((10,)),
+            pltpu.SemaphoreType.DMA((6,)),
         ],
-        limit=60,
-    )(populations.reshape(Q, SPAN, LANES), solid_mask.reshape(SPAN, LANES), relax_rates)
-
+    )(
+        in_hbm(populations.reshape(Q, SPAN, LANES)),
+        in_hbm(solid_mask.reshape(SPAN, LANES)),
+        in_hbm(relax_rates),
+    )
+
+    edge_z = swapped(edge_z, 2)
     edge_y = swapped(edge_y, 1)
-    edge_z = swapped(edge_z, 2)
-    streamed, edge_yz, pool, share, chosen, records = call(
+    streamed, edge_yz, pool, share, halves, records, chosen = call(
         stream_kernel,
         "stream",
         [
@@ -613,55 +627,71 @@
             ((64, LANES), F32),
             ((32, LANES), F32),
             ((64, LANES), F32),
+            ((64, POOLED), BF16),
         ],
-        [VMEM] * 2,
+        [VMEM, HBM],
+        scratch=[pltpu.VMEM((1, 2, Q * LANES), BF16), pltpu.SemaphoreType.DMA(())],
         cost=pl.CostEstimate(flops=10_000_000, bytes_accessed=8_000_000, transcendentals=0),
-    )(collided, coarse_pops)
-
-    streamed, right, left, payload, edge_yz, records = call(
+    )(collided, in_hbm(coarse_pops))
+
+    streamed, right, left, payload, records = call(
         halo_kernel,
         "halo",
         [
             ((Q * PITCH, LANES), F32),
-            ((72, LANES), F32),
-            ((72, LANES), F32),
+            ((ENDS, LANES), F32),
+            ((ENDS, LANES), F32),
             ((PLANE, ROWS, LANES), BF16),
-            ((NX, LANES), F32),
             ((64, LANES), F32),
         ],
-        [VMEM] * 8,
+        [VMEM] * 9,
         aliases={0: 0},
-    )(streamed, edge_y, edge_z, edge_yz, chosen, pool, share, records)
-    edge_yz = swapped(edge_yz, 3)
+    )(streamed, edge_y, edge_z, edge_yz, halves, pool, share, records, chosen)
 
     near = [[PLANE * i + j for j in range(PLANE)] for i in range(PLANE)]
     far = [[PLANE * j + i for j in range(PLANE)] for i in range(PLANE)]
     payload = lax.all_to_all(payload, "blocks", 0, 0, axis_index_groups=near, tiled=True)
-    ghost, line, own, route = call(
+    ring = [(i, (i + 1) % BLOCKS) for i in range(BLOCKS)]
+    right = lax.ppermute(right, "blocks", ring)
+    left = lax.ppermute(left, "blocks", [(b, a) for a, b in ring])
+    ghost, line, own, route, last, flags = call(
         tables_kernel,
         "tables",
-        [((256, 384), BF16), ((EDGE, LANES), F32), ((64, LANES), F32), ((24, LANES), jnp.int32)],
+        [
+            ((256, 384), BF16),
+            ((EDGE, LANES), F32),
+            ((64, LANES), F32),
+            ((3, LANES, LANES), BF16),
+            ((3, TILE, LANES), BF16),
+            ((8, LANES), jnp.int32),
+        ],
         [VMEM] * 2,
         cost=pl.CostEstimate(flops=1_000_000, bytes_accessed=4_000_000, transcendentals=0),
     )(records, interface_pairs)
-    payload, right, left = call(
+    payload, edge_yz = call(
         route_kernel,
         "route",
-        [((PLANE, ROWS, LANES), BF16), ((72, LANES), F32), ((72, LANES), F32)],
+        [((PLANE, ROWS, LANES), BF16), ((NX + 16, LANES), F32)],
         [VMEM] * 5,
     )(route, payload, edge_yz, right, left)
     payload = lax.all_to_all(payload, "blocks", 0, 0, axis_index_groups=far, tiled=True)
-    ring = [(i, (i + 1) % BLOCKS) for i in range(BLOCKS)]
-    right = lax.ppermute(right, "blocks", ring)
-    left = lax.ppermute(left, "blocks", [(b, a) for a, b in ring])
-
-    result, update = call(
+    edge_yz = swapped(edge_yz, 3)
+    merged = call(
+        merge_kernel,
+        "merge",
+        [((Q, SPAN, LANES), F32)],
+        [VMEM] * 4,
+        cost=pl.CostEstimate(flops=1_000_000, bytes_accessed=4_000_000, transcendentals=0),
+    )(streamed, edge_yz, right, left)[0]
+    _, result, update = call(
         finish_kernel,
         "finish",
-        [((Q * SPAN, LANES), F32), ((1, 2, Q * LANES), F32)],
-        [VMEM] * 10,
-        scratch=[pltpu.VMEM((32, LANES), F32)],
-    )(streamed, edge_yz, right, left, payload, route, own, line, share, ghost)
+        [((Q, SPAN, LANES), F32), ((Q, SPAN, LANES), F32), ((1, 2, Q * LANES), F32)],
+        [VMEM] * 8,
+        (VMEM, HBM, HBM),
+        [pltpu.VMEM((1, 2, Q * LANES), F32), pltpu.SemaphoreType.DMA((4,))],
+        aliases={0: 0},
+    )(merged, payload, last, flags, own, line, share, ghost)
     return result.reshape(1, Q, SPAN * LANES), update
 
 

time: 43.5 us -> 42.3 us (0.972)
  the two profiles are of different devices: /device:TPU:4 before, /device:TPU:25 now
where the time goes in v3:
time: 42.3 us; the launch traced here: 41.5 us
  starting transfers between devices  21.4 us (51%)
  waiting for transfers between devices  12.6 us (30%)
  Pallas kernels  6.93 us (16%)
  between operations  0.67 us (2%)
    all_to_all x1, starting transfers between devices, body(): lax.all_to_all(payload, 'blocks', 0, 0, axis_index_groups=far, tiled=True)  8.04 us
    all_to_all x1, starting transfers between devices, body(): lax.all_to_all(payload, 'blocks', 0, 0, axis_index_groups=near, tiled=True)  6.43 us
    ppermute x3, starting transfers between devices, swapped(): return lax.ppermute(block, 'group', [(i, i ^ bits) for i in range(4)])  5.56 us
    all_to_all x1, waiting for transfers between devices, body(): lax.all_to_all(payload, 'blocks', 0, 0, axis_index_groups=far, tiled=True)  4.82 us
    ppermute x1, waiting for transfers between devices, body(): left = lax.ppermute(left, 'blocks', [(b, a) for a, b in ring])  4.4 us
    ppermute x3, waiting for transfers between devices, swapped(): return lax.ppermute(block, 'group', [(i, i ^ bits) for i in range(4)])  2.88 us
    pallas_call x1, Pallas kernels, body(): call(collide_kernel, 'collide', [((Q, SPAN, LANES), F32), ((2, NX, LANES)...  1.72 us
    pallas_call x1, Pallas kernels, body(): call(halo_kernel, 'halo', [((Q * PITCH, LANES), F32), ((ENDS, LANES), F32...  1.47 us
  transfers between devices with their start and end apart: 7, of which 5 were waited for; matrix products, arithmetic and copies ran while one was open for 0% of the time, Pallas kernels for 4%

profile of v3, /device:TPU:25, one launch (start us, length us, event | category | flops | bytes accessed | tf_op | source)
XLA Modules:
  0.0 41.5 jit_solution(8229022895714920028)
XLA Ops:
  0.6 1.7 %collide.1 = (f32[27,64,128]{2,1,0:T(8,128)S(1)}, bf16[2,32,128]{2,1,0:T(8,128)(2,1)S(1)}, bf16[64,128]{1,0:T(8,128)(2,1)S(1)}) custom-call(f32[27,64,128]{2,1,0:T(8,128)} %bitcast.3, s32[64,128]{1,0:T(8,128)} %bitcast.4, f32[27]{0:T(128)} %rates_hbm.1), custom_call_target="tpu_custom_call" | custom-call | tf_op jit(solution)/shard_map/collide/pallas_call | solution.py:601
  2.4 1.3 %collective-permute-start = (bf16[2,32,128]{2,1,0:T(8,128)(2,1)S(1)}, bf16[2,32,128]{2,1,0:T(8,128)(2,1)S(1)}, u32[]{:S(2)}, u32[]{:S(2)}) collective-permute-start(bf16[2,32,128]{2,1,0:T(8,128)(2,1)S(1)} %get-tuple-element.29), channel_id=1, source_target_pairs={{0,1},{1,0},{2,3},{3,2},{4,5},{5,4},{6,7},{7,6},{8,9},{9,8},{10,11... | collective-permute-start | bytes 49160 | tf_op jit(solution)/shard_map/ppermute | solution.py:597
  3.7 2.5 %collective-permute-start.1 = (bf16[64,128]{1,0:T(8,128)(2,1)S(1)}, bf16[64,128]{1,0:T(8,128)(2,1)S(1)}, u32[]{:S(2)}, u32[]{:S(2)}) collective-permute-start(bf16[64,128]{1,0:T(8,128)(2,1)S(1)} %get-tuple-element.30), channel_id=1, source_target_pairs={{0,2},{1,3},{2,0},{3,1},{4,6},{5,7},{6,4},{7,5},{8,10},{9,11},{10,... | collective-permute-start | bytes 49160 | tf_op jit(solution)/shard_map/ppermute | solution.py:597
  6.1 0.0 copy-start
  6.1 1.1 %stream.1 = (f32[2160,128]{1,0:T(8,128)S(1)}, f32[32,128]{1,0:T(8,128)S(1)}, bf16[256,128]{1,0:T(8,128)(2,1)S(1)}, f32[64,128]{1,0:T(8,128)S(1)}, f32[32,128]{1,...) custom-call(f32[27,64,128]{2,1,0:T(8,128)S(1)} %get-tuple-element.27.w_ref, bf16[1,2,3456]{2,1,0:T(2,128)(2,1)} %coarse_hbm.1), custom_call_target="tpu_custom_call" | custom-call | flops 10000000 | bytes 8000000 | tf_op jit(solution)/shard_map/stream/pallas_call | solution.py:620
  7.2 0.0 collective-permute-done.y_ref
  7.2 0.5 %collective-permute-done.1.z_ref = bf16[64,128]{1,0:T(8,128)(2,1)S(1)} collective-permute-done((bf16[64,128]{1,0:T(8,128)(2,1)S(1)}, bf16[64,128]{1,0:T(8,128)(2,1)S(1)}, u32[]{:S(2)}, u32[]{:S(2)}) %collective-permute-start.1) | collective-permute-done | bytes 16416 | tf_op jit(solution)/shard_map/ppermute | solution.py:597
  7.7 1.5 %halo.1 = (f32[2160,128]{1,0:T(8,128)S(1)}, f32[32,128]{1,0:T(8,128)S(1)}, f32[32,128]{1,0:T(8,128)S(1)}, bf16[8,80,128]{2,1,0:T(8,128)(2,1)}, f32[64,128]{1,0:T(8,128)S(1)}) custom-call(f32[2160,128]{1,0:T(8,128)S(1)} %get-tuple-element.28.t_ref, bf16[2,32,128]{2,1,0:T(8,128)(2,1)S(1)} %collective-permute-done.y_ref, ...), custom_call_target="tpu_custom_call", output_to_operand_aliasing={{0}: (0, {})} | custom-call | tf_op jit(solution)/shard_map/halo/pallas_call | solution.py:637
  9.2 6.4 %all-to-all-start = ((bf16[8,80,128]{2,1,0:T(8,128)(2,1)}), bf16[8,80,128]{2,1,0:T(8,128)(2,1)S(1)}, u32[]{:S(2)}, u32[]{:S(2)}) async-start(bf16[8,80,128]{2,1,0:T(8,128)(2,1)} %get-tuple-element.40), calls=%async_computation | async-start | bytes 327680 | tf_op jit(solution)/shard_map/all_to_all | solution.py:653
  15.7 1.3 %collective-permute-start.2 = (f32[32,128]{1,0:T(8,128)S(1)}, f32[32,128]{1,0:T(8,128)S(1)}, u32[]{:S(2)}, u32[]{:S(2)}) collective-permute-start(f32[32,128]{1,0:T(8,128)S(1)} %get-tuple-element.41), channel_id=1, source_target_pairs={{0,4},{4,8},{8,12},{12,16},{16,20},{20,24},{24,28},{28,32},{32,36}... | collective-permute-start | bytes 49160 | tf_op jit(solution)/shard_map/ppermute | solution.py:655
  17.0 0.0 collective-permute-start.3
  17.0 0.0 copy-done
  17.0 0.4 tables.1
  17.4 0.5 %collective-permute-done.2.right_ref = f32[32,128]{1,0:T(8,128)S(1)} collective-permute-done((f32[32,128]{1,0:T(8,128)S(1)}, f32[32,128]{1,0:T(8,128)S(1)}, u32[]{:S(2)}, u32[]{:S(2)}) %collective-permute-start.2) | collective-permute-done | bytes 16416 | tf_op jit(solution)/shard_map/ppermute | solution.py:655
  17.8 4.4 %collective-permute-done.3.left_ref = f32[32,128]{1,0:T(8,128)S(1)} collective-permute-done((f32[32,128]{1,0:T(8,128)S(1)}, f32[32,128]{1,0:T(8,128)S(1)}, u32[]{:S(2)}, u32[]{:S(2)}) %collective-permute-start.3) | collective-permute-done | bytes 16416 | tf_op jit(solution)/shard_map/ppermute | solution.py:656
  22.2 0.0 all-to-all-done.in_ref
  22.3 0.9 %route.1 = (bf16[8,80,128]{2,1,0:T(8,128)(2,1)}, f32[48,128]{1,0:T(8,128)S(1)}) custom-call(bf16[3,128,128]{2,1,0:T(8,128)(2,1)S(1)} %get-tuple-element.39.route_ref, bf16[8,80,128]{2,1,0:T(8,128)(2,1)S(1)} %all-to-all-done.in_ref, f32[32,128]{1,0:T(8,128)S(1)} %get-tuple-element.31.e_ref, f32[32,128]{1,0:T(8,128)S(1)} %collective-permute-done.2.right_ref, ...), custom_call_target="tpu_custom_call" | custom-call | tf_op jit(solution)/shard_map/route/pallas_call | solution.py:671
  23.1 8.0 %all-to-all-start.1 = ((bf16[8,80,128]{2,1,0:T(8,128)(2,1)}), bf16[8,80,128]{2,1,0:T(8,128)(2,1)S(1)}, u32[]{:S(2)}, u32[]{:S(2)}) async-start(bf16[8,80,128]{2,1,0:T(8,128)(2,1)} %get-tuple-element.44), calls=%async_computation.1 | async-start | bytes 327680 | tf_op jit(solution)/shard_map/all_to_all | solution.py:677
  31.2 1.8 %collective-permute-start.4 = (f32[48,128]{1,0:T(8,128)S(1)}, f32[48,128]{1,0:T(8,128)S(1)}, u32[]{:S(2)}, u32[]{:S(2)}) collective-permute-start(f32[48,128]{1,0:T(8,128)S(1)} %get-tuple-element.43), channel_id=1, source_target_pairs={{0,3},{1,2},{2,1},{3,0},{4,7},{5,6},{6,5},{7,4},{8,11},{9,10},{10,... | collective-permute-start | bytes 73736 | tf_op jit(solution)/shard_map/ppermute | solution.py:597
  33.0 2.4 %collective-permute-done.4.e_ref = f32[48,128]{1,0:T(8,128)S(1)} collective-permute-done((f32[48,128]{1,0:T(8,128)S(1)}, f32[48,128]{1,0:T(8,128)S(1)}, u32[]{:S(2)}, u32[]{:S(2)}) %collective-permute-start.4) | collective-permute-done | bytes 24608 | tf_op jit(solution)/shard_map/ppermute | solution.py:597
  35.3 0.1 merge.1.base_ref
  35.4 4.8 %all-to-all-done.1.in_ref = bf16[8,80,128]{2,1,0:T(8,128)(2,1)S(1)} async-done(((bf16[8,80,128]{2,1,0:T(8,128)(2,1)}), bf16[8,80,128]{2,1,0:T(8,128)(2,1)S(1)}, u32[]{:S(2)}, u32[]{:S(2)}) %all-to-all-start.1) | async-done | bytes 163872 | tf_op jit(solution)/shard_map/all_to_all | solution.py:677
  40.3 1.3 %finish.1 = (f32[27,64,128]{2,1,0:T(8,128)S(1)}, f32[27,64,128]{2,1,0:T(8,128)}, f32[1,2,3456]{2,1,0:T(2,128)}) custom-call(f32[27,64,128]{2,1,0:T(8,128)S(1)} %merge.1.base_ref, bf16[8,80,128]{2,1,0:T(8,128)(2,1)S(1)} %all-to-all-done.1.in_ref, bf16[3,16,128]{2,1,0:T(8,128)(2,1)S(1)} %get-tuple-element.45.last_ref, ...), custom_call_target="tpu_custom_call", output_to_operand_aliasing={{0}: (0, {})} | custom-call | tf_op jit(solution)/shard_map/finish/pallas_call | solution.py:686
Async XLA Ops:
  2.4 4.9 %collective-permute-start = (bf16[2,32,128]{2,1,0:T(8,128)(2,1)S(1)}, bf16[2,32,128]{2,1,0:T(8,128)(2,1)S(1)}, u32[]{:S(2)}, u32[]{:S(2)}) collective-permute-start(bf16[2,32,128]{2,1,0:T(8,128)(2,1)S(1)} %get-tuple-element.29), channel_id=1, source_target_pairs={{0,1},{1,0},{2,3},{3,2},{4,5},{5,4},{6,7},{7,6},{8,9},{9,8},{10,11... | collective-permute-start | bytes 49160 | tf_op jit(solution)/shard_map/ppermute | solution.py:597
  3.7 4.1 %collective-permute-start.1 = (bf16[64,128]{1,0:T(8,128)(2,1)S(1)}, bf16[64,128]{1,0:T(8,128)(2,1)S(1)}, u32[]{:S(2)}, u32[]{:S(2)}) collective-permute-start(bf16[64,128]{1,0:T(8,128)(2,1)S(1)} %get-tuple-element.30), channel_id=1, source_target_pairs={{0,2},{1,3},{2,0},{3,1},{4,6},{5,7},{6,4},{7,5},{8,10},{9,11},{10,... | collective-permute-start | bytes 49160 | tf_op jit(solution)/shard_map/ppermute | solution.py:597
  6.1 10.9 %copy-start = (s32[1,128]{1,0:T(1,128)S(1)}, s32[1,128]{1,0:T(1,128)}, u32[]{:S(2)}) copy-start(s32[1,128]{1,0:T(1,128)} %pairs_ref.1) | copy-start | bytes 1540
  9.2 13.0 %all-to-all-start = ((bf16[8,80,128]{2,1,0:T(8,128)(2,1)}), bf16[8,80,128]{2,1,0:T(8,128)(2,1)S(1)}, u32[]{:S(2)}, u32[]{:S(2)}) async-start(bf16[8,80,128]{2,1,0:T(8,128)(2,1)} %get-tuple-element.40), calls=%async_computation | async-start | bytes 327680 | tf_op jit(solution)/shard_map/all_to_all | solution.py:653
  15.7 2.2 %collective-permute-start.2 = (f32[32,128]{1,0:T(8,128)S(1)}, f32[32,128]{1,0:T(8,128)S(1)}, u32[]{:S(2)}, u32[]{:S(2)}) collective-permute-start(f32[32,128]{1,0:T(8,128)S(1)} %get-tuple-element.41), channel_id=1, source_target_pairs={{0,4},{4,8},{8,12},{12,16},{16,20},{20,24},{24,28},{28,32},{32,36}... | collective-permute-start | bytes 49160 | tf_op jit(solution)/shard_map/ppermute | solution.py:655
  17.0 5.3 %collective-permute-start.3 = (f32[32,128]{1,0:T(8,128)S(1)}, f32[32,128]{1,0:T(8,128)S(1)}, u32[]{:S(2)}, u32[]{:S(2)}) collective-permute-start(f32[32,128]{1,0:T(8,128)S(1)} %get-tuple-element.42), channel_id=1, source_target_pairs={{4,0},{8,4},{12,8},{16,12},{20,16},{24,20},{28,24},{32,28},{36,32}... | collective-permute-start | bytes 49160 | tf_op jit(solution)/shard_map/ppermute | solution.py:656
  23.1 17.1 %all-to-all-start.1 = ((bf16[8,80,128]{2,1,0:T(8,128)(2,1)}), bf16[8,80,128]{2,1,0:T(8,128)(2,1)S(1)}, u32[]{:S(2)}, u32[]{:S(2)}) async-start(bf16[8,80,128]{2,1,0:T(8,128)(2,1)} %get-tuple-element.44), calls=%async_computation.1 | async-start | bytes 327680 | tf_op jit(solution)/shard_map/all_to_all | solution.py:677
  31.2 4.2 %collective-permute-start.4 = (f32[48,128]{1,0:T(8,128)S(1)}, f32[48,128]{1,0:T(8,128)S(1)}, u32[]{:S(2)}, u32[]{:S(2)}) collective-permute-start(f32[48,128]{1,0:T(8,128)S(1)} %get-tuple-element.43), channel_id=1, source_target_pairs={{0,3},{1,2},{2,1},{3,0},{4,7},{5,6},{6,5},{7,4},{8,11},{9,10},{10,... | collective-permute-start | bytes 73736 | tf_op jit(solution)/shard_map/ppermute | solution.py:597

commit v4 on v3

--- a/solution.py
+++ b/solution.py
@@ -15,6 +15,7 @@
 LANES = 128
 PLANE = 8
 BLOCKS = PLANE * PLANE
+TURN = 5
 LOW, HIGH, LAST_LOW, LAST_HIGH, CENTRE, RECORDS, ROWS = 54, 55, 56, 57, 58, 62, 80
 TILE = 16
 MIXED = 48
@@ -445,7 +446,7 @@
             chosen = (source(route) == lanes >> 4) & (place == lanes & (TILE - 1))
             ref[kind] = chosen.astype(F32).astype(BF16)
 
-    device = PLANE * (rows >> 4) + (me & (PLANE - 1))
+    device = PLANE * ((rows >> 4) + TURN & (PLANE - 1)) + (me & (PLANE - 1))
     pairs = jnp.broadcast_to(pairs, (LANES, LANES))
     owner = total(lanes == 2 * device, pairs >> 1)
     holder = total(pairs == 2 * device, lanes >> 1)
@@ -453,7 +454,7 @@
     rows, lanes, pairs = rows[0:TILE], lanes[0:TILE], pairs[0:TILE]
     serves = total(lanes == 2 * me, pairs)
     record = total(pairs == 2 * me, lanes)
-    matrices(last_ref, serves >> 1, record >> 1, lambda route: (route & (BLOCKS - 1)) >> 3, rows, lanes)
+    matrices(last_ref, serves >> 1, record >> 1, lambda route: (route >> 3) - TURN & (PLANE - 1), rows, lanes)
     flag_ref[...] = jnp.where(rows[0:8] == 0, record[0:8] & 1, serves[0:8] & 1)
 
 
@@ -649,7 +650,7 @@
     )(streamed, edge_y, edge_z, edge_yz, halves, pool, share, records, chosen)
 
     near = [[PLANE * i + j for j in range(PLANE)] for i in range(PLANE)]
-    far = [[PLANE * j + i for j in range(PLANE)] for i in range(PLANE)]
+    far = [[PLANE * ((j + TURN) % PLANE) + i for j in range(PLANE)] for i in range(PLANE)]
     payload = lax.all_to_all(payload, "blocks", 0, 0, axis_index_groups=near, tiled=True)
     ring = [(i, (i + 1) % BLOCKS) for i in range(BLOCKS)]
     right = lax.ppermute(right, "blocks", ring)

time: 42.3 us -> 39.2 us (0.927)
  waiting for transfers between devices: 12.6 us -> 7.46 us
  starting transfers between devices: 21.4 us -> 23.8 us
    all_to_all x1, waiting for transfers between devices: 4.82 us -> 0.01 us  [body(): lax.all_to_all(payload, 'blocks', 0, 0, axis_index_groups=far, tiled=True)]
    all_to_all x1, starting transfers between devices: 8.04 us -> 10.4 us  [body(): lax.all_to_all(payload, 'blocks', 0, 0, axis_index_groups=far, tiled=True)]
  transfers between devices with their start and end apart: 7 -> 7, of which waited for: 5 -> 4; matrix products, arithmetic and copies ran while one was open for 0% -> 0% of each run, Pallas kernels for 4% -> 4%
where the time goes in v4:
time: 39.2 us; the launch traced here: 38.8 us
  starting transfers between devices  23.8 us (61%)
  waiting for transfers between devices  7.46 us (19%)
  Pallas kernels  6.93 us (18%)
  between operations  0.68 us (2%)
    all_to_all x1, starting transfers between devices, body(): lax.all_to_all(payload, 'blocks', 0, 0, axis_index_groups=far, tiled=True)  10.4 us
    all_to_all x1, starting transfers between devices, body(): lax.all_to_all(payload, 'blocks', 0, 0, axis_index_groups=near, tiled=True)  6.43 us
    ppermute x3, starting transfers between devices, swapped(): return lax.ppermute(block, 'group', [(i, i ^ bits) for i in range(4)])  5.56 us
    ppermute x1, waiting for transfers between devices, body(): left = lax.ppermute(left, 'blocks', [(b, a) for a, b in ring])  4.4 us
    ppermute x3, waiting for transfers between devices, swapped(): return lax.ppermute(block, 'group', [(i, i ^ bits) for i in range(4)])  2.59 us
    pallas_call x1, Pallas kernels, body(): call(collide_kernel, 'collide', [((Q, SPAN, LANES), F32), ((2, NX, LANES)...  1.72 us
    pallas_call x1, Pallas kernels, body(): call(halo_kernel, 'halo', [((Q * PITCH, LANES), F32), ((ENDS, LANES), F32...  1.47 us
    ppermute x1, starting transfers between devices, body(): right = lax.ppermute(right, 'blocks', ring)  1.32 us
  transfers between devices with their start and end apart: 7, of which 4 were waited for; matrix products, arithmetic and copies ran while one was open for 0% of the time, Pallas kernels for 4%

profile of v4, /device:TPU:25, one launch (start us, length us, event | category | flops | bytes accessed | tf_op | source)
XLA Modules:
  0.0 38.8 jit_solution(13827032460583936594)
XLA Ops:
  0.6 1.7 %collide.1 = (f32[27,64,128]{2,1,0:T(8,128)S(1)}, bf16[2,32,128]{2,1,0:T(8,128)(2,1)S(1)}, bf16[64,128]{1,0:T(8,128)(2,1)S(1)}) custom-call(f32[27,64,128]{2,1,0:T(8,128)} %bitcast.3, s32[64,128]{1,0:T(8,128)} %bitcast.4, f32[27]{0:T(128)} %rates_hbm.1), custom_call_target="tpu_custom_call" | custom-call | tf_op jit(solution)/shard_map/collide/pallas_call | solution.py:602
  2.4 1.3 %collective-permute-start = (bf16[2,32,128]{2,1,0:T(8,128)(2,1)S(1)}, bf16[2,32,128]{2,1,0:T(8,128)(2,1)S(1)}, u32[]{:S(2)}, u32[]{:S(2)}) collective-permute-start(bf16[2,32,128]{2,1,0:T(8,128)(2,1)S(1)} %get-tuple-element.29), channel_id=1, source_target_pairs={{0,1},{1,0},{2,3},{3,2},{4,5},{5,4},{6,7},{7,6},{8,9},{9,8},{10,11... | collective-permute-start | bytes 49160 | tf_op jit(solution)/shard_map/ppermute | solution.py:598
  3.7 2.5 %collective-permute-start.1 = (bf16[64,128]{1,0:T(8,128)(2,1)S(1)}, bf16[64,128]{1,0:T(8,128)(2,1)S(1)}, u32[]{:S(2)}, u32[]{:S(2)}) collective-permute-start(bf16[64,128]{1,0:T(8,128)(2,1)S(1)} %get-tuple-element.30), channel_id=1, source_target_pairs={{0,2},{1,3},{2,0},{3,1},{4,6},{5,7},{6,4},{7,5},{8,10},{9,11},{10,... | collective-permute-start | bytes 49160 | tf_op jit(solution)/shard_map/ppermute | solution.py:598
  6.1 0.0 copy-start
  6.1 1.1 %stream.1 = (f32[2160,128]{1,0:T(8,128)S(1)}, f32[32,128]{1,0:T(8,128)S(1)}, bf16[256,128]{1,0:T(8,128)(2,1)S(1)}, f32[64,128]{1,0:T(8,128)S(1)}, f32[32,128]{1,...) custom-call(f32[27,64,128]{2,1,0:T(8,128)S(1)} %get-tuple-element.27.w_ref, bf16[1,2,3456]{2,1,0:T(2,128)(2,1)} %coarse_hbm.1), custom_call_target="tpu_custom_call" | custom-call | flops 10000000 | bytes 8000000 | tf_op jit(solution)/shard_map/stream/pallas_call | solution.py:621
  7.2 0.0 collective-permute-done.y_ref
  7.2 0.5 %collective-permute-done.1.z_ref = bf16[64,128]{1,0:T(8,128)(2,1)S(1)} collective-permute-done((bf16[64,128]{1,0:T(8,128)(2,1)S(1)}, bf16[64,128]{1,0:T(8,128)(2,1)S(1)}, u32[]{:S(2)}, u32[]{:S(2)}) %collective-permute-start.1) | collective-permute-done | bytes 16416 | tf_op jit(solution)/shard_map/ppermute | solution.py:598
  7.7 1.5 %halo.1 = (f32[2160,128]{1,0:T(8,128)S(1)}, f32[32,128]{1,0:T(8,128)S(1)}, f32[32,128]{1,0:T(8,128)S(1)}, bf16[8,80,128]{2,1,0:T(8,128)(2,1)}, f32[64,128]{1,0:T(8,128)S(1)}) custom-call(f32[2160,128]{1,0:T(8,128)S(1)} %get-tuple-element.28.t_ref, bf16[2,32,128]{2,1,0:T(8,128)(2,1)S(1)} %collective-permute-done.y_ref, ...), custom_call_target="tpu_custom_call", output_to_operand_aliasing={{0}: (0, {})} | custom-call | tf_op jit(solution)/shard_map/halo/pallas_call | solution.py:638
  9.2 6.4 %all-to-all-start = ((bf16[8,80,128]{2,1,0:T(8,128)(2,1)}), bf16[8,80,128]{2,1,0:T(8,128)(2,1)S(1)}, u32[]{:S(2)}, u32[]{:S(2)}) async-start(bf16[8,80,128]{2,1,0:T(8,128)(2,1)} %get-tuple-element.40), calls=%async_computation | async-start | bytes 327680 | tf_op jit(solution)/shard_map/all_to_all | solution.py:654
  15.7 1.3 %collective-permute-start.2 = (f32[32,128]{1,0:T(8,128)S(1)}, f32[32,128]{1,0:T(8,128)S(1)}, u32[]{:S(2)}, u32[]{:S(2)}) collective-permute-start(f32[32,128]{1,0:T(8,128)S(1)} %get-tuple-element.41), channel_id=1, source_target_pairs={{0,4},{4,8},{8,12},{12,16},{16,20},{20,24},{24,28},{28,32},{32,36}... | collective-permute-start | bytes 49160 | tf_op jit(solution)/shard_map/ppermute | solution.py:656
  17.0 0.0 collective-permute-start.3
  17.0 0.0 copy-done
  17.0 0.4 %tables.1 = (bf16[256,384]{1,0:T(8,128)(2,1)S(1)}, f32[16,128]{1,0:T(8,128)S(1)}, f32[64,128]{1,0:T(8,128)S(1)}, bf16[3,128,128]{2,1,0:T(8,128)(2,1)S(1)}, bf16[...) custom-call(f32[64,128]{1,0:T(8,128)S(1)} %get-tuple-element.38.p_ref, s32[1,128]{1,0:T(1,128)S(1)} %copy-done), custom_call_target="tpu_custom_call" | custom-call | flops 1000000 | bytes 4000000 | tf_op jit(solution)/shard_map/tables/pallas_call | solution.py:658
  17.4 0.5 %collective-permute-done.2.right_ref = f32[32,128]{1,0:T(8,128)S(1)} collective-permute-done((f32[32,128]{1,0:T(8,128)S(1)}, f32[32,128]{1,0:T(8,128)S(1)}, u32[]{:S(2)}, u32[]{:S(2)}) %collective-permute-start.2) | collective-permute-done | bytes 16416 | tf_op jit(solution)/shard_map/ppermute | solution.py:656
  17.8 4.4 %collective-permute-done.3.left_ref = f32[32,128]{1,0:T(8,128)S(1)} collective-permute-done((f32[32,128]{1,0:T(8,128)S(1)}, f32[32,128]{1,0:T(8,128)S(1)}, u32[]{:S(2)}, u32[]{:S(2)}) %collective-permute-start.3) | collective-permute-done | bytes 16416 | tf_op jit(solution)/shard_map/ppermute | solution.py:657
  22.2 0.0 all-to-all-done.in_ref
  22.3 0.9 %route.1 = (bf16[8,80,128]{2,1,0:T(8,128)(2,1)}, f32[48,128]{1,0:T(8,128)S(1)}) custom-call(bf16[3,128,128]{2,1,0:T(8,128)(2,1)S(1)} %get-tuple-element.39.route_ref, bf16[8,80,128]{2,1,0:T(8,128)(2,1)S(1)} %all-to-all-done.in_ref, f32[32,128]{1,0:T(8,128)S(1)} %get-tuple-element.31.e_ref, f32[32,128]{1,0:T(8,128)S(1)} %collective-permute-done.2.right_ref, ...), custom_call_target="tpu_custom_call" | custom-call | tf_op jit(solution)/shard_map/route/pallas_call | solution.py:672
  23.1 10.4 %all-to-all-start.1 = ((bf16[8,80,128]{2,1,0:T(8,128)(2,1)}), bf16[8,80,128]{2,1,0:T(8,128)(2,1)S(1)}, u32[]{:S(2)}, u32[]{:S(2)}) async-start(bf16[8,80,128]{2,1,0:T(8,128)(2,1)} %get-tuple-element.44), calls=%async_computation.1 | async-start | bytes 327680 | tf_op jit(solution)/shard_map/all_to_all | solution.py:678
  33.5 1.8 %collective-permute-start.4 = (f32[48,128]{1,0:T(8,128)S(1)}, f32[48,128]{1,0:T(8,128)S(1)}, u32[]{:S(2)}, u32[]{:S(2)}) collective-permute-start(f32[48,128]{1,0:T(8,128)S(1)} %get-tuple-element.43), channel_id=1, source_target_pairs={{0,3},{1,2},{2,1},{3,0},{4,7},{5,6},{6,5},{7,4},{8,11},{9,10},{10,... | collective-permute-start | bytes 73736 | tf_op jit(solution)/shard_map/ppermute | solution.py:598
  35.4 2.1 %collective-permute-done.4.e_ref = f32[48,128]{1,0:T(8,128)S(1)} collective-permute-done((f32[48,128]{1,0:T(8,128)S(1)}, f32[48,128]{1,0:T(8,128)S(1)}, u32[]{:S(2)}, u32[]{:S(2)}) %collective-permute-start.4) | collective-permute-done | bytes 24608 | tf_op jit(solution)/shard_map/ppermute | solution.py:598
  37.4 0.1 merge.1.base_ref
  37.5 0.0 all-to-all-done.1.in_ref
  37.5 1.3 %finish.1 = (f32[27,64,128]{2,1,0:T(8,128)S(1)}, f32[27,64,128]{2,1,0:T(8,128)}, f32[1,2,3456]{2,1,0:T(2,128)}) custom-call(f32[27,64,128]{2,1,0:T(8,128)S(1)} %merge.1.base_ref, bf16[8,80,128]{2,1,0:T(8,128)(2,1)S(1)} %all-to-all-done.1.in_ref, bf16[3,16,128]{2,1,0:T(8,128)(2,1)S(1)} %get-tuple-element.45.last_ref, ...), custom_call_target="tpu_custom_call", output_to_operand_aliasing={{0}: (0, {})} | custom-call | tf_op jit(solution)/shard_map/finish/pallas_call | solution.py:687
Async XLA Ops:
  2.4 4.9 %collective-permute-start = (bf16[2,32,128]{2,1,0:T(8,128)(2,1)S(1)}, bf16[2,32,128]{2,1,0:T(8,128)(2,1)S(1)}, u32[]{:S(2)}, u32[]{:S(2)}) collective-permute-start(bf16[2,32,128]{2,1,0:T(8,128)(2,1)S(1)} %get-tuple-element.29), channel_id=1, source_target_pairs={{0,1},{1,0},{2,3},{3,2},{4,5},{5,4},{6,7},{7,6},{8,9},{9,8},{10,11... | collective-permute-start | bytes 49160 | tf_op jit(solution)/shard_map/ppermute | solution.py:598
  3.7 4.1 %collective-permute-start.1 = (bf16[64,128]{1,0:T(8,128)(2,1)S(1)}, bf16[64,128]{1,0:T(8,128)(2,1)S(1)}, u32[]{:S(2)}, u32[]{:S(2)}) collective-permute-start(bf16[64,128]{1,0:T(8,128)(2,1)S(1)} %get-tuple-element.30), channel_id=1, source_target_pairs={{0,2},{1,3},{2,0},{3,1},{4,6},{5,7},{6,4},{7,5},{8,10},{9,11},{10,... | collective-permute-start | bytes 49160 | tf_op jit(solution)/shard_map/ppermute | solution.py:598
  6.1 10.9 %copy-start = (s32[1,128]{1,0:T(1,128)S(1)}, s32[1,128]{1,0:T(1,128)}, u32[]{:S(2)}) copy-start(s32[1,128]{1,0:T(1,128)} %pairs_ref.1) | copy-start | bytes 1540
  9.2 13.0 %all-to-all-start = ((bf16[8,80,128]{2,1,0:T(8,128)(2,1)}), bf16[8,80,128]{2,1,0:T(8,128)(2,1)S(1)}, u32[]{:S(2)}, u32[]{:S(2)}) async-start(bf16[8,80,128]{2,1,0:T(8,128)(2,1)} %get-tuple-element.40), calls=%async_computation | async-start | bytes 327680 | tf_op jit(solution)/shard_map/all_to_all | solution.py:654
  15.7 2.2 %collective-permute-start.2 = (f32[32,128]{1,0:T(8,128)S(1)}, f32[32,128]{1,0:T(8,128)S(1)}, u32[]{:S(2)}, u32[]{:S(2)}) collective-permute-start(f32[32,128]{1,0:T(8,128)S(1)} %get-tuple-element.41), channel_id=1, source_target_pairs={{0,4},{4,8},{8,12},{12,16},{16,20},{20,24},{24,28},{28,32},{32,36}... | collective-permute-start | bytes 49160 | tf_op jit(solution)/shard_map/ppermute | solution.py:656
  17.0 5.3 %collective-permute-start.3 = (f32[32,128]{1,0:T(8,128)S(1)}, f32[32,128]{1,0:T(8,128)S(1)}, u32[]{:S(2)}, u32[]{:S(2)}) collective-permute-start(f32[32,128]{1,0:T(8,128)S(1)} %get-tuple-element.42), channel_id=1, source_target_pairs={{4,0},{8,4},{12,8},{16,12},{20,16},{24,20},{28,24},{32,28},{36,32}... | collective-permute-start | bytes 49160 | tf_op jit(solution)/shard_map/ppermute | solution.py:657
  23.1 14.4 %all-to-all-start.1 = ((bf16[8,80,128]{2,1,0:T(8,128)(2,1)}), bf16[8,80,128]{2,1,0:T(8,128)(2,1)S(1)}, u32[]{:S(2)}, u32[]{:S(2)}) async-start(bf16[8,80,128]{2,1,0:T(8,128)(2,1)} %get-tuple-element.44), calls=%async_computation.1 | async-start | bytes 327680 | tf_op jit(solution)/shard_map/all_to_all | solution.py:678
  33.5 3.9 %collective-permute-start.4 = (f32[48,128]{1,0:T(8,128)S(1)}, f32[48,128]{1,0:T(8,128)S(1)}, u32[]{:S(2)}, u32[]{:S(2)}) collective-permute-start(f32[48,128]{1,0:T(8,128)S(1)} %get-tuple-element.43), channel_id=1, source_target_pairs={{0,3},{1,2},{2,1},{3,0},{4,7},{5,6},{6,5},{7,4},{8,11},{9,10},{10,... | collective-permute-start | bytes 73736 | tf_op jit(solution)/shard_map/ppermute | solution.py:598

commit v5 on v4

--- a/solution.py
+++ b/solution.py
@@ -285,18 +285,20 @@
 
 
 def stream_kernel(
-    w_ref, coarse_hbm, t_ref, e_ref, pool_ref, share_ref, rec_ref, p_ref, chosen_ref, coarse_ref, sem
+    w_ref, coarse_hbm, t_ref, e_ref, pool_ref, share_ref, rec_ref, p_ref, chosen_ref, centre_ref, coarse_ref, sem
 ):
     copy = pltpu.make_async_copy(coarse_hbm, coarse_ref, sem)
     copy.start()
     lanes = ids((8, LANES), 1)
     zeros = jnp.zeros((8, LANES), F32)
+    held = zeros
     for i, (a, b, c) in enumerate(PAIRS):
         for row in (0, 8, SPAN, SPAN + 8):
             t_ref[pl.ds(PITCH * i + row, 8), :] = zeros
         shift = (16 * (b - 1) + c - 1) % 128
         for row in range(0, SPAN, 8):
             value = w_ref[i, pl.ds(row, 8), :]
+            held = held + value
             if shift:
                 value = moved(value, b, shift)
             if c != 1:
@@ -332,10 +334,13 @@
     pool_ref[...] = pool_table()
     share_ref[...] = share_table()
     chosen_ref[...] = chosen_table()
+    held = jnp.sum(jnp.sum(held, axis=0, keepdims=True), axis=1, keepdims=True)
+    centre = (held * (1.0 / (Q * SPAN * LANES))).astype(BF16).astype(F32)
+    centre_ref[...] = jnp.broadcast_to(centre, (8, LANES))
 
 
 def halo_kernel(
-    t_ref, y_ref, z_ref, e_ref, rec_ref, pool_ref, share_ref, p_ref, chosen_ref,
+    t_ref, z_ref, y_ref, e_ref, rec_ref, pool_ref, share_ref, p_ref, chosen_ref, centre_ref,
     out_ref, right_ref, left_ref, pay_ref, kept_ref,
 ):
     del t_ref
@@ -396,12 +401,7 @@
 
     share = share_ref[...]
     rows, lane_a = ids((64, LANES), 0), ids((64, LANES), 1) >> 3 & 7
-    inside = rows < LOW
-    held = jnp.sum(jnp.where(inside, routed, 0.0), axis=0, keepdims=True)
-    held = jnp.sum(held, axis=1, keepdims=True)
-    parts = jnp.sum(jnp.where(inside, share, 0.0), axis=0, keepdims=True)
-    parts = jnp.sum(parts, axis=1, keepdims=True)
-    centre = (held / parts).astype(BF16).astype(F32)
+    centre = centre_ref[0:1, :]
     routed = routed - centre * share
     is_centre = (rows == CENTRE) | ((rows == LAST_LOW) & (lane_a == 6)) | ((rows == LAST_HIGH) & (lane_a == 1))
     routed = jnp.where(is_centre, centre, routed)
@@ -618,7 +618,7 @@
 
     edge_z = swapped(edge_z, 2)
     edge_y = swapped(edge_y, 1)
-    streamed, edge_yz, pool, share, halves, records, chosen = call(
+    streamed, edge_yz, pool, share, halves, records, chosen, centre = call(
         stream_kernel,
         "stream",
         [
@@ -629,6 +629,7 @@
             ((32, LANES), F32),
             ((64, LANES), F32),
             ((64, POOLED), BF16),
+            ((8, LANES), F32),
         ],
         [VMEM, HBM],
         scratch=[pltpu.VMEM((1, 2, Q * LANES), BF16), pltpu.SemaphoreType.DMA(())],
@@ -645,9 +646,9 @@
             ((PLANE, ROWS, LANES), BF16),
             ((64, LANES), F32),
         ],
-        [VMEM] * 9,
+        [VMEM] * 10,
         aliases={0: 0},
-    )(streamed, edge_y, edge_z, edge_yz, halves, pool, share, records, chosen)
+    )(streamed, edge_z, edge_y, edge_yz, halves, pool, share, records, chosen, centre)
 
     near = [[PLANE * i + j for j in range(PLANE)] for i in range(PLANE)]
     far = [[PLANE * ((j + TURN) % PLANE) + i for j in range(PLANE)] for i in range(PLANE)]

time: 39.2 us -> 39.1 us (level)
  waiting for transfers between devices: 7.46 us -> 8.99 us
  starting transfers between devices: 23.8 us -> 22.3 us
    ppermute x3, waiting for transfers between devices: 2.59 us -> 4.12 us  [swapped(): return lax.ppermute(block, 'group', [(i, i ^ bits) for i in range(4)])]
    ppermute x3, starting transfers between devices: 5.56 us -> 4.26 us  [swapped(): return lax.ppermute(block, 'group', [(i, i ^ bits) for i in range(4)])]
where the time goes in v5:
time: 39.1 us; the launch traced here: 38.8 us
  starting transfers between devices  22.3 us (57%)
  waiting for transfers between devices  8.99 us (23%)
  Pallas kernels  6.83 us (17%)
  between operations  0.68 us (2%)
    all_to_all x1, starting transfers between devices, body(): lax.all_to_all(payload, 'blocks', 0, 0, axis_index_groups=far, tiled=True)  10.4 us
    all_to_all x1, starting transfers between devices, body(): lax.all_to_all(payload, 'blocks', 0, 0, axis_index_groups=near, tiled=True)  6.25 us
    ppermute x1, waiting for transfers between devices, body(): left = lax.ppermute(left, 'blocks', [(b, a) for a, b in ring])  4.4 us
    ppermute x3, starting transfers between devices, swapped(): return lax.ppermute(block, 'group', [(i, i ^ bits) for i in range(4)])  4.26 us
    ppermute x3, waiting for transfers between devices, swapped(): return lax.ppermute(block, 'group', [(i, i ^ bits) for i in range(4)])  4.12 us
    pallas_call x1, Pallas kernels, body(): call(collide_kernel, 'collide', [((Q, SPAN, LANES), F32), ((2, NX, LANES)...  1.72 us
    pallas_call x1, Pallas kernels, body(): call(halo_kernel, 'halo', [((Q * PITCH, LANES), F32), ((ENDS, LANES), F32...  1.38 us
    ppermute x1, starting transfers between devices, body(): right = lax.ppermute(right, 'blocks', ring)  1.32 us
  transfers between devices with their start and end apart: 7, of which 4 were waited for; matrix products, arithmetic and copies ran while one was open for 0% of the time, Pallas kernels for 4%

profile of v5, /device:TPU:25, one launch (start us, length us, event | category | flops | bytes accessed | tf_op | source)
XLA Modules:
  0.0 38.8 jit_solution(3966434566150867667)
XLA Ops:
  0.6 1.7 %collide.1 = (f32[27,64,128]{2,1,0:T(8,128)S(1)}, bf16[2,32,128]{2,1,0:T(8,128)(2,1)S(1)}, bf16[64,128]{1,0:T(8,128)(2,1)S(1)}) custom-call(f32[27,64,128]{2,1,0:T(8,128)} %bitcast.3, s32[64,128]{1,0:T(8,128)} %bitcast.4, f32[27]{0:T(128)} %rates_hbm.1), custom_call_target="tpu_custom_call" | custom-call | tf_op jit(solution)/shard_map/collide/pallas_call | solution.py:602
  2.4 2.8 %collective-permute-start = (bf16[64,128]{1,0:T(8,128)(2,1)S(1)}, bf16[64,128]{1,0:T(8,128)(2,1)S(1)}, u32[]{:S(2)}, u32[]{:S(2)}) collective-permute-start(bf16[64,128]{1,0:T(8,128)(2,1)S(1)} %get-tuple-element.30), channel_id=1, source_target_pairs={{0,2},{1,3},{2,0},{3,1},{4,6},{5,7},{6,4},{7,5},{8,10},{9,11},{10,... | collective-permute-start | bytes 49160 | tf_op jit(solution)/shard_map/ppermute | solution.py:598
  5.2 0.3 collective-permute-start.1
  5.5 0.0 copy-start
  5.5 1.1 %stream.1 = (f32[2160,128]{1,0:T(8,128)S(1)}, f32[32,128]{1,0:T(8,128)S(1)}, bf16[256,128]{1,0:T(8,128)(2,1)S(1)}, f32[64,128]{1,0:T(8,128)S(1)}, f32[32,128]{1,...) custom-call(f32[27,64,128]{2,1,0:T(8,128)S(1)} %get-tuple-element.28.w_ref, ...), custom_call_target="tpu_custom_call" | custom-call | flops 10000000 | bytes 8000000 | tf_op jit(solution)/shard_map/stream/pallas_call | solution.py:621
  6.6 0.0 collective-permute-done.z_ref
  6.6 1.3 %collective-permute-done.1.y_ref = bf16[2,32,128]{2,1,0:T(8,128)(2,1)S(1)} collective-permute-done((bf16[2,32,128]{2,1,0:T(8,128)(2,1)S(1)}, bf16[2,32,128]{2,1,0:T(8,128)(2,1)S(1)}, u32[]{:S(2)}, u32[]{:S(2)}) %collective-permute-start.1) | collective-permute-done | bytes 16416 | tf_op jit(solution)/shard_map/ppermute | solution.py:598
  8.0 1.4 %halo.1 = (f32[2160,128]{1,0:T(8,128)S(1)}, f32[32,128]{1,0:T(8,128)S(1)}, f32[32,128]{1,0:T(8,128)S(1)}, bf16[8,80,128]{2,1,0:T(8,128)(2,1)}, f32[64,128]{1,0:T(8,128)S(1)}) custom-call(f32[2160,128]{1,0:T(8,128)S(1)} %get-tuple-element.29.t_ref, bf16[64,128]{1,0:T(8,128)(2,1)S(1)} %collective-permute-done.z_ref, ...), custom_call_target="tpu_custom_call", output_to_operand_aliasing={{0}: (0, {})} | custom-call | tf_op jit(solution)/shard_map/halo/pallas_call | solution.py:639
  9.3 6.2 %all-to-all-start = ((bf16[8,80,128]{2,1,0:T(8,128)(2,1)}), bf16[8,80,128]{2,1,0:T(8,128)(2,1)S(1)}, u32[]{:S(2)}, u32[]{:S(2)}) async-start(bf16[8,80,128]{2,1,0:T(8,128)(2,1)} %get-tuple-element.42), calls=%async_computation | async-start | bytes 327680 | tf_op jit(solution)/shard_map/all_to_all | solution.py:655
  15.6 1.3 %collective-permute-start.2 = (f32[32,128]{1,0:T(8,128)S(1)}, f32[32,128]{1,0:T(8,128)S(1)}, u32[]{:S(2)}, u32[]{:S(2)}) collective-permute-start(f32[32,128]{1,0:T(8,128)S(1)} %get-tuple-element.43), channel_id=1, source_target_pairs={{0,4},{4,8},{8,12},{12,16},{16,20},{20,24},{24,28},{28,32},{32,36}... | collective-permute-start | bytes 49160 | tf_op jit(solution)/shard_map/ppermute | solution.py:657
  16.9 0.0 collective-permute-start.3
  16.9 0.0 copy-done
  16.9 0.4 %tables.1 = (bf16[256,384]{1,0:T(8,128)(2,1)S(1)}, f32[16,128]{1,0:T(8,128)S(1)}, f32[64,128]{1,0:T(8,128)S(1)}, bf16[3,128,128]{2,1,0:T(8,128)(2,1)S(1)}, bf16[...) custom-call(f32[64,128]{1,0:T(8,128)S(1)} %get-tuple-element.40.p_ref, s32[1,128]{1,0:T(1,128)S(1)} %copy-done), custom_call_target="tpu_custom_call" | custom-call | flops 1000000 | bytes 4000000 | tf_op jit(solution)/shard_map/tables/pallas_call | solution.py:659
  17.3 0.5 %collective-permute-done.2.right_ref = f32[32,128]{1,0:T(8,128)S(1)} collective-permute-done((f32[32,128]{1,0:T(8,128)S(1)}, f32[32,128]{1,0:T(8,128)S(1)}, u32[]{:S(2)}, u32[]{:S(2)}) %collective-permute-start.2) | collective-permute-done | bytes 16416 | tf_op jit(solution)/shard_map/ppermute | solution.py:657
  17.8 4.4 %collective-permute-done.3.left_ref = f32[32,128]{1,0:T(8,128)S(1)} collective-permute-done((f32[32,128]{1,0:T(8,128)S(1)}, f32[32,128]{1,0:T(8,128)S(1)}, u32[]{:S(2)}, u32[]{:S(2)}) %collective-permute-start.3) | collective-permute-done | bytes 16416 | tf_op jit(solution)/shard_map/ppermute | solution.py:658
  22.2 0.0 all-to-all-done.in_ref
  22.2 0.9 %route.1 = (bf16[8,80,128]{2,1,0:T(8,128)(2,1)}, f32[48,128]{1,0:T(8,128)S(1)}) custom-call(bf16[3,128,128]{2,1,0:T(8,128)(2,1)S(1)} %get-tuple-element.41.route_ref, bf16[8,80,128]{2,1,0:T(8,128)(2,1)S(1)} %all-to-all-done.in_ref, f32[32,128]{1,0:T(8,128)S(1)} %get-tuple-element.32.e_ref, f32[32,128]{1,0:T(8,128)S(1)} %collective-permute-done.2.right_ref, ...), custom_call_target="tpu_custom_call" | custom-call | tf_op jit(solution)/shard_map/route/pallas_call | solution.py:673
  23.0 10.4 %all-to-all-start.1 = ((bf16[8,80,128]{2,1,0:T(8,128)(2,1)}), bf16[8,80,128]{2,1,0:T(8,128)(2,1)S(1)}, u32[]{:S(2)}, u32[]{:S(2)}) async-start(bf16[8,80,128]{2,1,0:T(8,128)(2,1)} %get-tuple-element.46), calls=%async_computation.1 | async-start | bytes 327680 | tf_op jit(solution)/shard_map/all_to_all | solution.py:679
  33.5 1.1 %collective-permute-start.4 = (f32[48,128]{1,0:T(8,128)S(1)}, f32[48,128]{1,0:T(8,128)S(1)}, u32[]{:S(2)}, u32[]{:S(2)}) collective-permute-start(f32[48,128]{1,0:T(8,128)S(1)} %get-tuple-element.45), channel_id=1, source_target_pairs={{0,3},{1,2},{2,1},{3,0},{4,7},{5,6},{6,5},{7,4},{8,11},{9,10},{10,... | collective-permute-start | bytes 73736 | tf_op jit(solution)/shard_map/ppermute | solution.py:598
  34.6 2.8 %collective-permute-done.4.e_ref = f32[48,128]{1,0:T(8,128)S(1)} collective-permute-done((f32[48,128]{1,0:T(8,128)S(1)}, f32[48,128]{1,0:T(8,128)S(1)}, u32[]{:S(2)}, u32[]{:S(2)}) %collective-permute-start.4) | collective-permute-done | bytes 24608 | tf_op jit(solution)/shard_map/ppermute | solution.py:598
  37.4 0.1 merge.1.base_ref
  37.5 0.0 all-to-all-done.1.in_ref
  37.5 1.3 %finish.1 = (f32[27,64,128]{2,1,0:T(8,128)S(1)}, f32[27,64,128]{2,1,0:T(8,128)}, f32[1,2,3456]{2,1,0:T(2,128)}) custom-call(f32[27,64,128]{2,1,0:T(8,128)S(1)} %merge.1.base_ref, bf16[8,80,128]{2,1,0:T(8,128)(2,1)S(1)} %all-to-all-done.1.in_ref, bf16[3,16,128]{2,1,0:T(8,128)(2,1)S(1)} %get-tuple-element.47.last_ref, ...), custom_call_target="tpu_custom_call", output_to_operand_aliasing={{0}: (0, {})} | custom-call | tf_op jit(solution)/shard_map/finish/pallas_call | solution.py:688
Async XLA Ops:
  2.4 4.3 %collective-permute-start = (bf16[64,128]{1,0:T(8,128)(2,1)S(1)}, bf16[64,128]{1,0:T(8,128)(2,1)S(1)}, u32[]{:S(2)}, u32[]{:S(2)}) collective-permute-start(bf16[64,128]{1,0:T(8,128)(2,1)S(1)} %get-tuple-element.30), channel_id=1, source_target_pairs={{0,2},{1,3},{2,0},{3,1},{4,6},{5,7},{6,4},{7,5},{8,10},{9,11},{10,... | collective-permute-start | bytes 49160 | tf_op jit(solution)/shard_map/ppermute | solution.py:598
  5.2 2.8 %collective-permute-start.1 = (bf16[2,32,128]{2,1,0:T(8,128)(2,1)S(1)}, bf16[2,32,128]{2,1,0:T(8,128)(2,1)S(1)}, u32[]{:S(2)}, u32[]{:S(2)}) collective-permute-start(bf16[2,32,128]{2,1,0:T(8,128)(2,1)S(1)} %get-tuple-element.31), channel_id=1, source_target_pairs={{0,1},{1,0},{2,3},{3,2},{4,5},{5,4},{6,7},{7,6},{8,9},{9,8},{10,11... | collective-permute-start | bytes 49160 | tf_op jit(solution)/shard_map/ppermute | solution.py:598
  5.5 11.4 %copy-start = (s32[1,128]{1,0:T(1,128)S(1)}, s32[1,128]{1,0:T(1,128)}, u32[]{:S(2)}) copy-start(s32[1,128]{1,0:T(1,128)} %pairs_ref.1) | copy-start | bytes 1540
  9.3 12.8 %all-to-all-start = ((bf16[8,80,128]{2,1,0:T(8,128)(2,1)}), bf16[8,80,128]{2,1,0:T(8,128)(2,1)S(1)}, u32[]{:S(2)}, u32[]{:S(2)}) async-start(bf16[8,80,128]{2,1,0:T(8,128)(2,1)} %get-tuple-element.42), calls=%async_computation | async-start | bytes 327680 | tf_op jit(solution)/shard_map/all_to_all | solution.py:655
  15.6 2.2 %collective-permute-start.2 = (f32[32,128]{1,0:T(8,128)S(1)}, f32[32,128]{1,0:T(8,128)S(1)}, u32[]{:S(2)}, u32[]{:S(2)}) collective-permute-start(f32[32,128]{1,0:T(8,128)S(1)} %get-tuple-element.43), channel_id=1, source_target_pairs={{0,4},{4,8},{8,12},{12,16},{16,20},{20,24},{24,28},{28,32},{32,36}... | collective-permute-start | bytes 49160 | tf_op jit(solution)/shard_map/ppermute | solution.py:657
  16.9 5.3 %collective-permute-start.3 = (f32[32,128]{1,0:T(8,128)S(1)}, f32[32,128]{1,0:T(8,128)S(1)}, u32[]{:S(2)}, u32[]{:S(2)}) collective-permute-start(f32[32,128]{1,0:T(8,128)S(1)} %get-tuple-element.44), channel_id=1, source_target_pairs={{4,0},{8,4},{12,8},{16,12},{20,16},{24,20},{28,24},{32,28},{36,32}... | collective-permute-start | bytes 49160 | tf_op jit(solution)/shard_map/ppermute | solution.py:658
  23.0 14.4 %all-to-all-start.1 = ((bf16[8,80,128]{2,1,0:T(8,128)(2,1)}), bf16[8,80,128]{2,1,0:T(8,128)(2,1)S(1)}, u32[]{:S(2)}, u32[]{:S(2)}) async-start(bf16[8,80,128]{2,1,0:T(8,128)(2,1)} %get-tuple-element.46), calls=%async_computation.1 | async-start | bytes 327680 | tf_op jit(solution)/shard_map/all_to_all | solution.py:679
  33.5 3.9 %collective-permute-start.4 = (f32[48,128]{1,0:T(8,128)S(1)}, f32[48,128]{1,0:T(8,128)S(1)}, u32[]{:S(2)}, u32[]{:S(2)}) collective-permute-start(f32[48,128]{1,0:T(8,128)S(1)} %get-tuple-element.45), channel_id=1, source_target_pairs={{0,3},{1,2},{2,1},{3,0},{4,7},{5,6},{6,5},{7,4},{8,11},{9,10},{10,... | collective-permute-start | bytes 73736 | tf_op jit(solution)/shard_map/ppermute | solution.py:598

commit v6 on v5

--- a/solution.py
+++ b/solution.py
@@ -97,6 +97,27 @@
     half_x = (row >= LOW) | low | high
     share = jnp.where(half_y, 0.5, 1.0) * jnp.where(half_z, 0.5, 1.0) * jnp.where(half_x, 0.5, 1.0)
     held = (row <= HIGH) | ((row == LAST_LOW) & (a == 7)) | ((row == LAST_HIGH) & (a == 0))
+    return jnp.where(held, share, 0.0)
+
+
+def pooled_share_table():
+    side_y, side_z = sides()
+    shape = (POOLED, LANES)
+    row = ids(shape, 0)
+    block, place = row >> 3, row & 7
+    face, a, b = record_ids(shape, 1)
+    column, index = block & 1, block >> 1
+    index = jnp.where(block == 54, 18 + place, jnp.where(block == 55, 26, index))
+    index = jnp.where(block == 56, place, jnp.where(block == 57, 8, index))
+    by_x, by_y, by_z = digits(index)
+    in_y, in_z = by_y == 2 * (1 - side_y), by_z == 2 * (1 - side_z)
+    half_y = in_y & ((face == 0) | (b == 7 * side_y))
+    half_z = in_z & ((face == 1) | (b == 7 * side_z))
+    low = (by_x == 2) & (column == 0) & (a == 0)
+    high = (by_x == 0) & (column == 1) & (a == HALF - 1)
+    half_x = (block >= 54) | low | high
+    share = jnp.where(half_y, 0.5, 1.0) * jnp.where(half_z, 0.5, 1.0) * jnp.where(half_x, 0.5, 1.0)
+    held = (place == a) & ((block != 55) | (place == 7)) & ((block != 57) | (place == 0))
     return jnp.where(held, share, 0.0)
 
 
@@ -285,7 +306,8 @@
 
 
 def stream_kernel(
-    w_ref, coarse_hbm, t_ref, e_ref, pool_ref, share_ref, rec_ref, p_ref, chosen_ref, centre_ref, coarse_ref, sem
+    w_ref, coarse_hbm, t_ref, e_ref, pool_ref, share_ref, rec_ref, p_ref, chosen_ref, centre_ref, pooled_share_ref,
+    coarse_ref, sem
 ):
     copy = pltpu.make_async_copy(coarse_hbm, coarse_ref, sem)
     copy.start()
@@ -334,13 +356,14 @@
     pool_ref[...] = pool_table()
     share_ref[...] = share_table()
     chosen_ref[...] = chosen_table()
+    pooled_share_ref[...] = pooled_share_table()
     held = jnp.sum(jnp.sum(held, axis=0, keepdims=True), axis=1, keepdims=True)
     centre = (held * (1.0 / (Q * SPAN * LANES))).astype(BF16).astype(F32)
     centre_ref[...] = jnp.broadcast_to(centre, (8, LANES))
 
 
 def halo_kernel(
-    t_ref, z_ref, y_ref, e_ref, rec_ref, pool_ref, share_ref, p_ref, chosen_ref, centre_ref,
+    t_ref, z_ref, y_ref, e_ref, rec_ref, pool_ref, pooled_share_ref, p_ref, chosen_ref, centre_ref,
     out_ref, right_ref, left_ref, pay_ref, kept_ref,
 ):
     del t_ref
@@ -395,14 +418,10 @@
     high, low = split_bf16(jnp.concatenate(tiles, 1))
     pooled = dot(high, pool) + dot(low, pool)
     pooled = jnp.where(ids((POOLED, LANES), 0) & 7 == ids((POOLED, LANES), 1) >> 3 & 7, pooled, 0.0)
-    chosen = chosen_ref[...]
-    high, low = split_bf16(pooled)
-    routed = dot(chosen, high) + dot(chosen, low)
-
-    share = share_ref[...]
+    centre = centre_ref[0:1, :]
+    pooled = pooled - centre * pooled_share_ref[...]
+    routed = dot(chosen_ref[...], pooled.astype(BF16))
     rows, lane_a = ids((64, LANES), 0), ids((64, LANES), 1) >> 3 & 7
-    centre = centre_ref[0:1, :]
-    routed = routed - centre * share
     is_centre = (rows == CENTRE) | ((rows == LAST_LOW) & (lane_a == 6)) | ((rows == LAST_HIGH) & (lane_a == 1))
     routed = jnp.where(is_centre, centre, routed)
     payload = jnp.where(rows[MIXED:64] >= RECORDS, rec_ref[0:16], routed[MIXED:64])
@@ -618,7 +637,7 @@
 
     edge_z = swapped(edge_z, 2)
     edge_y = swapped(edge_y, 1)
-    streamed, edge_yz, pool, share, halves, records, chosen, centre = call(
+    streamed, edge_yz, pool, share, halves, records, chosen, centre, pooled_share = call(
         stream_kernel,
         "stream",
         [
@@ -630,6 +649,7 @@
             ((64, LANES), F32),
             ((64, POOLED), BF16),
             ((8, LANES), F32),
+            ((POOLED, LANES), F32),
         ],
         [VMEM, HBM],
         scratch=[pltpu.VMEM((1, 2, Q * LANES), BF16), pltpu.SemaphoreType.DMA(())],
@@ -648,7 +668,7 @@
         ],
         [VMEM] * 10,
         aliases={0: 0},
-    )(streamed, edge_z, edge_y, edge_yz, halves, pool, share, records, chosen, centre)
+    )(streamed, edge_z, edge_y, edge_yz, halves, pool, pooled_share, records, chosen, centre)
 
     near = [[PLANE * i + j for j in range(PLANE)] for i in range(PLANE)]
     far = [[PLANE * ((j + TURN) % PLANE) + i for j in range(PLANE)] for i in range(PLANE)]

time: 39.1 us -> 39 us (level)
  waiting for transfers between devices: 8.99 us -> 8.39 us
  Pallas kernels: 6.83 us -> 7.36 us
    ppermute x3, waiting for transfers between devices: 4.12 us -> 3.52 us  [swapped(): return lax.ppermute(block, 'group', [(i, i ^ bits) for i in range(4)])]
    pallas_call x1, Pallas kernels: 1.11 us -> 1.7 us  [body(): call(stream_kernel, 'stream', [((Q * PITCH, LANES), F32), ((NX, LANES), F...]
  transfers between devices with their start and end apart: 7 -> 7, of which waited for: 4 -> 4; matrix products, arithmetic and copies ran while one was open for 0% -> 0% of each run, Pallas kernels for 4% -> 6%
where the time goes in v6:
time: 39 us; the launch traced here: 38.7 us
  starting transfers between devices  22.3 us (57%)
  waiting for transfers between devices  8.39 us (22%)
  Pallas kernels  7.36 us (19%)
  between operations  0.69 us (2%)
    all_to_all x1, starting transfers between devices, body(): lax.all_to_all(payload, 'blocks', 0, 0, axis_index_groups=far, tiled=True)  10.4 us
    all_to_all x1, starting transfers between devices, body(): lax.all_to_all(payload, 'blocks', 0, 0, axis_index_groups=near, tiled=True)  6.25 us
    ppermute x1, waiting for transfers between devices, body(): left = lax.ppermute(left, 'blocks', [(b, a) for a, b in ring])  4.4 us
    ppermute x3, starting transfers between devices, swapped(): return lax.ppermute(block, 'group', [(i, i ^ bits) for i in range(4)])  4.26 us
    ppermute x3, waiting for transfers between devices, swapped(): return lax.ppermute(block, 'group', [(i, i ^ bits) for i in range(4)])  3.52 us
    pallas_call x1, Pallas kernels, body(): call(collide_kernel, 'collide', [((Q, SPAN, LANES), F32), ((2, NX, LANES)...  1.72 us
    pallas_call x1, Pallas kernels, body(): call(stream_kernel, 'stream', [((Q * PITCH, LANES), F32), ((NX, LANES), F...  1.7 us
    ppermute x1, starting transfers between devices, body(): right = lax.ppermute(right, 'blocks', ring)  1.32 us
  transfers between devices with their start and end apart: 7, of which 4 were waited for; matrix products, arithmetic and copies ran while one was open for 0% of the time, Pallas kernels for 6%

profile of v6, /device:TPU:25, one launch (start us, length us, event | category | flops | bytes accessed | tf_op | source)
XLA Modules:
  0.0 38.7 jit_solution(2611523523883404293)
XLA Ops:
  0.6 1.7 %collide.1 = (f32[27,64,128]{2,1,0:T(8,128)S(1)}, bf16[2,32,128]{2,1,0:T(8,128)(2,1)S(1)}, bf16[64,128]{1,0:T(8,128)(2,1)S(1)}) custom-call(f32[27,64,128]{2,1,0:T(8,128)} %bitcast.3, s32[64,128]{1,0:T(8,128)} %bitcast.4, f32[27]{0:T(128)} %rates_hbm.1), custom_call_target="tpu_custom_call" | custom-call | tf_op jit(solution)/shard_map/collide/pallas_call | solution.py:621
  2.4 2.8 %collective-permute-start = (bf16[64,128]{1,0:T(8,128)(2,1)S(1)}, bf16[64,128]{1,0:T(8,128)(2,1)S(1)}, u32[]{:S(2)}, u32[]{:S(2)}) collective-permute-start(bf16[64,128]{1,0:T(8,128)(2,1)S(1)} %get-tuple-element.31), channel_id=1, source_target_pairs={{0,2},{1,3},{2,0},{3,1},{4,6},{5,7},{6,4},{7,5},{8,10},{9,11},{10,... | collective-permute-start | bytes 49160 | tf_op jit(solution)/shard_map/ppermute | solution.py:617
  5.2 0.3 collective-permute-start.1
  5.5 1.7 %stream.1 = (f32[2160,128]{1,0:T(8,128)S(1)}, f32[32,128]{1,0:T(8,128)S(1)}, bf16[256,128]{1,0:T(8,128)(2,1)S(1)}, f32[64,128]{1,0:T(8,128)S(1)}, f32[32,128]{1,...) custom-call(f32[27,64,128]{2,1,0:T(8,128)S(1)} %get-tuple-element.29, ...), custom_call_target="tpu_custom_call" | custom-call | flops 10000000 | bytes 8000000 | tf_op jit(solution)/shard_map/stream/pallas_call | solution.py:640
  7.2 0.0 copy-start
  7.2 0.0 collective-permute-done.z_ref
  7.2 0.7 %collective-permute-done.1.y_ref = bf16[2,32,128]{2,1,0:T(8,128)(2,1)S(1)} collective-permute-done((bf16[2,32,128]{2,1,0:T(8,128)(2,1)S(1)}, bf16[2,32,128]{2,1,0:T(8,128)(2,1)S(1)}, u32[]{:S(2)}, u32[]{:S(2)}) %collective-permute-start.1) | collective-permute-done | bytes 16416 | tf_op jit(solution)/shard_map/ppermute | solution.py:617
  8.0 1.3 %halo.1 = (f32[2160,128]{1,0:T(8,128)S(1)}, f32[32,128]{1,0:T(8,128)S(1)}, f32[32,128]{1,0:T(8,128)S(1)}, bf16[8,80,128]{2,1,0:T(8,128)(2,1)}, f32[64,128]{1,0:T(8,128)S(1)}) custom-call(f32[2160,128]{1,0:T(8,128)S(1)} %get-tuple-element.30.t_ref, bf16[64,128]{1,0:T(8,128)(2,1)S(1)} %collective-permute-done.z_ref, ...), custom_call_target="tpu_custom_call", output_to_operand_aliasing={{0}: (0, {})} | custom-call | tf_op jit(solution)/shard_map/halo/pallas_call | solution.py:659
  9.3 6.2 %all-to-all-start = ((bf16[8,80,128]{2,1,0:T(8,128)(2,1)}), bf16[8,80,128]{2,1,0:T(8,128)(2,1)S(1)}, u32[]{:S(2)}, u32[]{:S(2)}) async-start(bf16[8,80,128]{2,1,0:T(8,128)(2,1)} %get-tuple-element.43), calls=%async_computation | async-start | bytes 327680 | tf_op jit(solution)/shard_map/all_to_all | solution.py:675
  15.5 1.3 %collective-permute-start.2 = (f32[32,128]{1,0:T(8,128)S(1)}, f32[32,128]{1,0:T(8,128)S(1)}, u32[]{:S(2)}, u32[]{:S(2)}) collective-permute-start(f32[32,128]{1,0:T(8,128)S(1)} %get-tuple-element.44), channel_id=1, source_target_pairs={{0,4},{4,8},{8,12},{12,16},{16,20},{20,24},{24,28},{28,32},{32,36}... | collective-permute-start | bytes 49160 | tf_op jit(solution)/shard_map/ppermute | solution.py:677
  16.9 0.0 collective-permute-start.3
  16.9 0.0 copy-done
  16.9 0.4 %tables.1 = (bf16[256,384]{1,0:T(8,128)(2,1)S(1)}, f32[16,128]{1,0:T(8,128)S(1)}, f32[64,128]{1,0:T(8,128)S(1)}, bf16[3,128,128]{2,1,0:T(8,128)(2,1)S(1)}, bf16[...) custom-call(f32[64,128]{1,0:T(8,128)S(1)} %get-tuple-element.41.p_ref, s32[1,128]{1,0:T(1,128)S(1)} %copy-done), custom_call_target="tpu_custom_call" | custom-call | flops 1000000 | bytes 4000000 | tf_op jit(solution)/shard_map/tables/pallas_call | solution.py:679
  17.3 0.5 %collective-permute-done.2.right_ref = f32[32,128]{1,0:T(8,128)S(1)} collective-permute-done((f32[32,128]{1,0:T(8,128)S(1)}, f32[32,128]{1,0:T(8,128)S(1)}, u32[]{:S(2)}, u32[]{:S(2)}) %collective-permute-start.2) | collective-permute-done | bytes 16416 | tf_op jit(solution)/shard_map/ppermute | solution.py:677
  17.7 4.4 %collective-permute-done.3.left_ref = f32[32,128]{1,0:T(8,128)S(1)} collective-permute-done((f32[32,128]{1,0:T(8,128)S(1)}, f32[32,128]{1,0:T(8,128)S(1)}, u32[]{:S(2)}, u32[]{:S(2)}) %collective-permute-start.3) | collective-permute-done | bytes 16416 | tf_op jit(solution)/shard_map/ppermute | solution.py:678
  22.1 0.0 all-to-all-done.in_ref
  22.1 0.9 %route.1 = (bf16[8,80,128]{2,1,0:T(8,128)(2,1)}, f32[48,128]{1,0:T(8,128)S(1)}) custom-call(bf16[3,128,128]{2,1,0:T(8,128)(2,1)S(1)} %get-tuple-element.42.route_ref, bf16[8,80,128]{2,1,0:T(8,128)(2,1)S(1)} %all-to-all-done.in_ref, f32[32,128]{1,0:T(8,128)S(1)} %get-tuple-element.33.e_ref, f32[32,128]{1,0:T(8,128)S(1)} %collective-permute-done.2.right_ref, ...), custom_call_target="tpu_custom_call" | custom-call | tf_op jit(solution)/shard_map/route/pallas_call | solution.py:693
  23.0 10.4 %all-to-all-start.1 = ((bf16[8,80,128]{2,1,0:T(8,128)(2,1)}), bf16[8,80,128]{2,1,0:T(8,128)(2,1)S(1)}, u32[]{:S(2)}, u32[]{:S(2)}) async-start(bf16[8,80,128]{2,1,0:T(8,128)(2,1)} %get-tuple-element.47), calls=%async_computation.1 | async-start | bytes 327680 | tf_op jit(solution)/shard_map/all_to_all | solution.py:699
  33.4 1.1 %collective-permute-start.4 = (f32[48,128]{1,0:T(8,128)S(1)}, f32[48,128]{1,0:T(8,128)S(1)}, u32[]{:S(2)}, u32[]{:S(2)}) collective-permute-start(f32[48,128]{1,0:T(8,128)S(1)} %get-tuple-element.46), channel_id=1, source_target_pairs={{0,3},{1,2},{2,1},{3,0},{4,7},{5,6},{6,5},{7,4},{8,11},{9,10},{10,... | collective-permute-start | bytes 73736 | tf_op jit(solution)/shard_map/ppermute | solution.py:617
  34.5 2.8 %collective-permute-done.4.e_ref = f32[48,128]{1,0:T(8,128)S(1)} collective-permute-done((f32[48,128]{1,0:T(8,128)S(1)}, f32[48,128]{1,0:T(8,128)S(1)}, u32[]{:S(2)}, u32[]{:S(2)}) %collective-permute-start.4) | collective-permute-done | bytes 24608 | tf_op jit(solution)/shard_map/ppermute | solution.py:617
  37.3 0.1 merge.1.base_ref
  37.4 0.0 all-to-all-done.1.in_ref
  37.4 1.3 %finish.1 = (f32[27,64,128]{2,1,0:T(8,128)S(1)}, f32[27,64,128]{2,1,0:T(8,128)}, f32[1,2,3456]{2,1,0:T(2,128)}) custom-call(f32[27,64,128]{2,1,0:T(8,128)S(1)} %merge.1.base_ref, bf16[8,80,128]{2,1,0:T(8,128)(2,1)S(1)} %all-to-all-done.1.in_ref, bf16[3,16,128]{2,1,0:T(8,128)(2,1)S(1)} %get-tuple-element.48.last_ref, ...), custom_call_target="tpu_custom_call", output_to_operand_aliasing={{0}: (0, {})} | custom-call | tf_op jit(solution)/shard_map/finish/pallas_call | solution.py:708
Async XLA Ops:
  2.4 4.9 %collective-permute-start = (bf16[64,128]{1,0:T(8,128)(2,1)S(1)}, bf16[64,128]{1,0:T(8,128)(2,1)S(1)}, u32[]{:S(2)}, u32[]{:S(2)}) collective-permute-start(bf16[64,128]{1,0:T(8,128)(2,1)S(1)} %get-tuple-element.31), channel_id=1, source_target_pairs={{0,2},{1,3},{2,0},{3,1},{4,6},{5,7},{6,4},{7,5},{8,10},{9,11},{10,... | collective-permute-start | bytes 49160 | tf_op jit(solution)/shard_map/ppermute | solution.py:617
  5.2 2.8 %collective-permute-start.1 = (bf16[2,32,128]{2,1,0:T(8,128)(2,1)S(1)}, bf16[2,32,128]{2,1,0:T(8,128)(2,1)S(1)}, u32[]{:S(2)}, u32[]{:S(2)}) collective-permute-start(bf16[2,32,128]{2,1,0:T(8,128)(2,1)S(1)} %get-tuple-element.32), channel_id=1, source_target_pairs={{0,1},{1,0},{2,3},{3,2},{4,5},{5,4},{6,7},{7,6},{8,9},{9,8},{10,11... | collective-permute-start | bytes 49160 | tf_op jit(solution)/shard_map/ppermute | solution.py:617
  7.2 9.7 %copy-start = (s32[1,128]{1,0:T(1,128)S(1)}, s32[1,128]{1,0:T(1,128)}, u32[]{:S(2)}) copy-start(s32[1,128]{1,0:T(1,128)} %pairs_ref.1) | copy-start | bytes 1540
  9.3 12.8 %all-to-all-start = ((bf16[8,80,128]{2,1,0:T(8,128)(2,1)}), bf16[8,80,128]{2,1,0:T(8,128)(2,1)S(1)}, u32[]{:S(2)}, u32[]{:S(2)}) async-start(bf16[8,80,128]{2,1,0:T(8,128)(2,1)} %get-tuple-element.43), calls=%async_computation | async-start | bytes 327680 | tf_op jit(solution)/shard_map/all_to_all | solution.py:675
  15.5 2.2 %collective-permute-start.2 = (f32[32,128]{1,0:T(8,128)S(1)}, f32[32,128]{1,0:T(8,128)S(1)}, u32[]{:S(2)}, u32[]{:S(2)}) collective-permute-start(f32[32,128]{1,0:T(8,128)S(1)} %get-tuple-element.44), channel_id=1, source_target_pairs={{0,4},{4,8},{8,12},{12,16},{16,20},{20,24},{24,28},{28,32},{32,36}... | collective-permute-start | bytes 49160 | tf_op jit(solution)/shard_map/ppermute | solution.py:677
  16.9 5.3 %collective-permute-start.3 = (f32[32,128]{1,0:T(8,128)S(1)}, f32[32,128]{1,0:T(8,128)S(1)}, u32[]{:S(2)}, u32[]{:S(2)}) collective-permute-start(f32[32,128]{1,0:T(8,128)S(1)} %get-tuple-element.45), channel_id=1, source_target_pairs={{4,0},{8,4},{12,8},{16,12},{20,16},{24,20},{28,24},{32,28},{36,32}... | collective-permute-start | bytes 49160 | tf_op jit(solution)/shard_map/ppermute | solution.py:678
  23.0 14.4 %all-to-all-start.1 = ((bf16[8,80,128]{2,1,0:T(8,128)(2,1)}), bf16[8,80,128]{2,1,0:T(8,128)(2,1)S(1)}, u32[]{:S(2)}, u32[]{:S(2)}) async-start(bf16[8,80,128]{2,1,0:T(8,128)(2,1)} %get-tuple-element.47), calls=%async_computation.1 | async-start | bytes 327680 | tf_op jit(solution)/shard_map/all_to_all | solution.py:699
  33.4 3.9 %collective-permute-start.4 = (f32[48,128]{1,0:T(8,128)S(1)}, f32[48,128]{1,0:T(8,128)S(1)}, u32[]{:S(2)}, u32[]{:S(2)}) collective-permute-start(f32[48,128]{1,0:T(8,128)S(1)} %get-tuple-element.46), channel_id=1, source_target_pairs={{0,3},{1,2},{2,1},{3,0},{4,7},{5,6},{6,5},{7,4},{8,11},{9,10},{10,... | collective-permute-start | bytes 73736 | tf_op jit(solution)/shard_map/ppermute | solution.py:617

commit v7 on v5

--- a/solution.py
+++ b/solution.py
@@ -510,33 +510,6 @@
         copies.append(copy)
 
     rows = jnp.concatenate([tile for _, tile in passed_on(last_ref, in_ref)], 0)
-    swap = flag_ref[0:1, :] == 1
-    lines = line_ref[...]
-    scaled = []
-    for k in range(9):
-        row = RECORDS + k
-        first, second = rows[row : row + 1], rows[row + 9 : row + 10]
-        scaled.append(lines * jnp.where(swap, second, first))
-        scaled.append(lines * jnp.where(swap, first, second))
-    scaled = jnp.concatenate(scaled, 0)
-    ghost = dot(jnp.concatenate(split_bf16(scaled), 1), ghost_ref[...])
-    lanes = ids((NX, LANES), 1)
-    outer = lanes >> 4 == 7 * side_y
-    for a in range(3):
-        for b in range(3):
-            k = 3 * a + b
-            for h in range(2):
-                at = pl.ds(h, NX, stride=2)
-                part = ghost[NX * k : NX * (k + 1), LANES * (h + 1) : LANES * (h + 2)]
-                value_ref[9 * a + 3 * b + in_z, at, :] = value_ref[9 * a + 3 * b + in_z, at, :] + part
-        for c in range(3):
-            k = 3 * a + c
-            at = pl.ds(side_y, NX, stride=2)
-            part = ghost[NX * k : NX * (k + 1), 0:LANES]
-            value = value_ref[9 * a + 3 * in_y + c, at, :]
-            value_ref[9 * a + 3 * in_y + c, at, :] = jnp.where(outer, part, value)
-        send(value_ref.at[pl.ds(9 * a, 9)], next_hbm.at[pl.ds(9 * a, 9)])
-
     share = share_ref[...]
     lane_1 = ids((1, LANES), 1)
     low_centre = jnp.sum(jnp.where(lane_1 == 48, rows[LAST_LOW : LAST_LOW + 1], 0.0), axis=1, keepdims=True)
@@ -568,6 +541,33 @@
         for i in range(Q):
             update_ref[0, t : t + 1, LANES * i : LANES * (i + 1)] = value[i : i + 1]
     send(update_ref, update_hbm)
+
+    swap = flag_ref[0:1, :] == 1
+    lines = line_ref[...]
+    scaled = []
+    for k in range(9):
+        row = RECORDS + k
+        first, second = rows[row : row + 1], rows[row + 9 : row + 10]
+        scaled.append(lines * jnp.where(swap, second, first))
+        scaled.append(lines * jnp.where(swap, first, second))
+    scaled = jnp.concatenate(scaled, 0)
+    ghost = dot(jnp.concatenate(split_bf16(scaled), 1), ghost_ref[...])
+    lanes = ids((NX, LANES), 1)
+    outer = lanes >> 4 == 7 * side_y
+    for a in range(3):
+        for b in range(3):
+            k = 3 * a + b
+            for h in range(2):
+                at = pl.ds(h, NX, stride=2)
+                part = ghost[NX * k : NX * (k + 1), LANES * (h + 1) : LANES * (h + 2)]
+                value_ref[9 * a + 3 * b + in_z, at, :] = value_ref[9 * a + 3 * b + in_z, at, :] + part
+        for c in range(3):
+            k = 3 * a + c
+            at = pl.ds(side_y, NX, stride=2)
+            part = ghost[NX * k : NX * (k + 1), 0:LANES]
+            value = value_ref[9 * a + 3 * in_y + c, at, :]
+            value_ref[9 * a + 3 * in_y + c, at, :] = jnp.where(outer, part, value)
+        send(value_ref.at[pl.ds(9 * a, 9)], next_hbm.at[pl.ds(9 * a, 9)])
     for copy in copies:
         copy.wait()
 

time: 39.1 us -> 39.2 us (level)
  no operation moved by 1% of the time
where the time goes in v7:
time: 39.2 us; the launch traced here: 38.9 us
  starting transfers between devices  22.3 us (57%)
  waiting for transfers between devices  8.99 us (23%)
  Pallas kernels  6.92 us (18%)
  between operations  0.68 us (2%)
    all_to_all x1, starting transfers between devices, body(): lax.all_to_all(payload, 'blocks', 0, 0, axis_index_groups=far, tiled=True)  10.4 us
    all_to_all x1, starting transfers between devices, body(): lax.all_to_all(payload, 'blocks', 0, 0, axis_index_groups=near, tiled=True)  6.25 us
    ppermute x1, waiting for transfers between devices, body(): left = lax.ppermute(left, 'blocks', [(b, a) for a, b in ring])  4.4 us
    ppermute x3, starting transfers between devices, swapped(): return lax.ppermute(block, 'group', [(i, i ^ bits) for i in range(4)])  4.26 us
    ppermute x3, waiting for transfers between devices, swapped(): return lax.ppermute(block, 'group', [(i, i ^ bits) for i in range(4)])  4.12 us
    pallas_call x1, Pallas kernels, body(): call(collide_kernel, 'collide', [((Q, SPAN, LANES), F32), ((2, NX, LANES)...  1.72 us
    pallas_call x1, Pallas kernels, body(): call(finish_kernel, 'finish', [((Q, SPAN, LANES), F32), ((Q, SPAN, LANES)...  1.38 us
    pallas_call x1, Pallas kernels, body(): call(halo_kernel, 'halo', [((Q * PITCH, LANES), F32), ((ENDS, LANES), F32...  1.38 us
  transfers between devices with their start and end apart: 7, of which 4 were waited for; matrix products, arithmetic and copies ran while one was open for 0% of the time, Pallas kernels for 4%

profile of v7, /device:TPU:25, one launch (start us, length us, event | category | flops | bytes accessed | tf_op | source)
XLA Modules:
  0.0 38.9 jit_solution(1291146478817445569)
XLA Ops:
  0.6 1.7 %collide.1 = (f32[27,64,128]{2,1,0:T(8,128)S(1)}, bf16[2,32,128]{2,1,0:T(8,128)(2,1)S(1)}, bf16[64,128]{1,0:T(8,128)(2,1)S(1)}) custom-call(f32[27,64,128]{2,1,0:T(8,128)} %bitcast.3, s32[64,128]{1,0:T(8,128)} %bitcast.4, f32[27]{0:T(128)} %rates_hbm.1), custom_call_target="tpu_custom_call" | custom-call | tf_op jit(solution)/shard_map/collide/pallas_call | solution.py:602
  2.4 2.8 %collective-permute-start = (bf16[64,128]{1,0:T(8,128)(2,1)S(1)}, bf16[64,128]{1,0:T(8,128)(2,1)S(1)}, u32[]{:S(2)}, u32[]{:S(2)}) collective-permute-start(bf16[64,128]{1,0:T(8,128)(2,1)S(1)} %get-tuple-element.30), channel_id=1, source_target_pairs={{0,2},{1,3},{2,0},{3,1},{4,6},{5,7},{6,4},{7,5},{8,10},{9,11},{10,... | collective-permute-start | bytes 49160 | tf_op jit(solution)/shard_map/ppermute | solution.py:598
  5.2 0.3 collective-permute-start.1
  5.5 0.0 copy-start
  5.5 1.1 %stream.1 = (f32[2160,128]{1,0:T(8,128)S(1)}, f32[32,128]{1,0:T(8,128)S(1)}, bf16[256,128]{1,0:T(8,128)(2,1)S(1)}, f32[64,128]{1,0:T(8,128)S(1)}, f32[32,128]{1,...) custom-call(f32[27,64,128]{2,1,0:T(8,128)S(1)} %get-tuple-element.28.w_ref, ...), custom_call_target="tpu_custom_call" | custom-call | flops 10000000 | bytes 8000000 | tf_op jit(solution)/shard_map/stream/pallas_call | solution.py:621
  6.6 0.0 collective-permute-done.z_ref
  6.6 1.3 %collective-permute-done.1.y_ref = bf16[2,32,128]{2,1,0:T(8,128)(2,1)S(1)} collective-permute-done((bf16[2,32,128]{2,1,0:T(8,128)(2,1)S(1)}, bf16[2,32,128]{2,1,0:T(8,128)(2,1)S(1)}, u32[]{:S(2)}, u32[]{:S(2)}) %collective-permute-start.1) | collective-permute-done | bytes 16416 | tf_op jit(solution)/shard_map/ppermute | solution.py:598
  8.0 1.4 %halo.1 = (f32[2160,128]{1,0:T(8,128)S(1)}, f32[32,128]{1,0:T(8,128)S(1)}, f32[32,128]{1,0:T(8,128)S(1)}, bf16[8,80,128]{2,1,0:T(8,128)(2,1)}, f32[64,128]{1,0:T(8,128)S(1)}) custom-call(f32[2160,128]{1,0:T(8,128)S(1)} %get-tuple-element.29.t_ref, bf16[64,128]{1,0:T(8,128)(2,1)S(1)} %collective-permute-done.z_ref, ...), custom_call_target="tpu_custom_call", output_to_operand_aliasing={{0}: (0, {})} | custom-call | tf_op jit(solution)/shard_map/halo/pallas_call | solution.py:639
  9.3 6.2 %all-to-all-start = ((bf16[8,80,128]{2,1,0:T(8,128)(2,1)}), bf16[8,80,128]{2,1,0:T(8,128)(2,1)S(1)}, u32[]{:S(2)}, u32[]{:S(2)}) async-start(bf16[8,80,128]{2,1,0:T(8,128)(2,1)} %get-tuple-element.42), calls=%async_computation | async-start | bytes 327680 | tf_op jit(solution)/shard_map/all_to_all | solution.py:655
  15.6 1.3 %collective-permute-start.2 = (f32[32,128]{1,0:T(8,128)S(1)}, f32[32,128]{1,0:T(8,128)S(1)}, u32[]{:S(2)}, u32[]{:S(2)}) collective-permute-start(f32[32,128]{1,0:T(8,128)S(1)} %get-tuple-element.43), channel_id=1, source_target_pairs={{0,4},{4,8},{8,12},{12,16},{16,20},{20,24},{24,28},{28,32},{32,36}... | collective-permute-start | bytes 49160 | tf_op jit(solution)/shard_map/ppermute | solution.py:657
  16.9 0.0 collective-permute-start.3
  16.9 0.0 copy-done
  16.9 0.4 %tables.1 = (bf16[256,384]{1,0:T(8,128)(2,1)S(1)}, f32[16,128]{1,0:T(8,128)S(1)}, f32[64,128]{1,0:T(8,128)S(1)}, bf16[3,128,128]{2,1,0:T(8,128)(2,1)S(1)}, bf16[...) custom-call(f32[64,128]{1,0:T(8,128)S(1)} %get-tuple-element.40.p_ref, s32[1,128]{1,0:T(1,128)S(1)} %copy-done), custom_call_target="tpu_custom_call" | custom-call | flops 1000000 | bytes 4000000 | tf_op jit(solution)/shard_map/tables/pallas_call | solution.py:659
  17.3 0.5 %collective-permute-done.2.right_ref = f32[32,128]{1,0:T(8,128)S(1)} collective-permute-done((f32[32,128]{1,0:T(8,128)S(1)}, f32[32,128]{1,0:T(8,128)S(1)}, u32[]{:S(2)}, u32[]{:S(2)}) %collective-permute-start.2) | collective-permute-done | bytes 16416 | tf_op jit(solution)/shard_map/ppermute | solution.py:657
  17.8 4.4 %collective-permute-done.3.left_ref = f32[32,128]{1,0:T(8,128)S(1)} collective-permute-done((f32[32,128]{1,0:T(8,128)S(1)}, f32[32,128]{1,0:T(8,128)S(1)}, u32[]{:S(2)}, u32[]{:S(2)}) %collective-permute-start.3) | collective-permute-done | bytes 16416 | tf_op jit(solution)/shard_map/ppermute | solution.py:658
  22.2 0.0 all-to-all-done.in_ref
  22.2 0.9 %route.1 = (bf16[8,80,128]{2,1,0:T(8,128)(2,1)}, f32[48,128]{1,0:T(8,128)S(1)}) custom-call(bf16[3,128,128]{2,1,0:T(8,128)(2,1)S(1)} %get-tuple-element.41.route_ref, bf16[8,80,128]{2,1,0:T(8,128)(2,1)S(1)} %all-to-all-done.in_ref, f32[32,128]{1,0:T(8,128)S(1)} %get-tuple-element.32.e_ref, f32[32,128]{1,0:T(8,128)S(1)} %collective-permute-done.2.right_ref, ...), custom_call_target="tpu_custom_call" | custom-call | tf_op jit(solution)/shard_map/route/pallas_call | solution.py:673
  23.0 10.4 %all-to-all-start.1 = ((bf16[8,80,128]{2,1,0:T(8,128)(2,1)}), bf16[8,80,128]{2,1,0:T(8,128)(2,1)S(1)}, u32[]{:S(2)}, u32[]{:S(2)}) async-start(bf16[8,80,128]{2,1,0:T(8,128)(2,1)} %get-tuple-element.46), calls=%async_computation.1 | async-start | bytes 327680 | tf_op jit(solution)/shard_map/all_to_all | solution.py:679
  33.5 1.1 %collective-permute-start.4 = (f32[48,128]{1,0:T(8,128)S(1)}, f32[48,128]{1,0:T(8,128)S(1)}, u32[]{:S(2)}, u32[]{:S(2)}) collective-permute-start(f32[48,128]{1,0:T(8,128)S(1)} %get-tuple-element.45), channel_id=1, source_target_pairs={{0,3},{1,2},{2,1},{3,0},{4,7},{5,6},{6,5},{7,4},{8,11},{9,10},{10,... | collective-permute-start | bytes 73736 | tf_op jit(solution)/shard_map/ppermute | solution.py:598
  34.6 2.8 %collective-permute-done.4.e_ref = f32[48,128]{1,0:T(8,128)S(1)} collective-permute-done((f32[48,128]{1,0:T(8,128)S(1)}, f32[48,128]{1,0:T(8,128)S(1)}, u32[]{:S(2)}, u32[]{:S(2)}) %collective-permute-start.4) | collective-permute-done | bytes 24608 | tf_op jit(solution)/shard_map/ppermute | solution.py:598
  37.4 0.1 merge.1.base_ref
  37.5 0.0 all-to-all-done.1.in_ref
  37.5 1.4 %finish.1 = (f32[27,64,128]{2,1,0:T(8,128)S(1)}, f32[27,64,128]{2,1,0:T(8,128)}, f32[1,2,3456]{2,1,0:T(2,128)}) custom-call(f32[27,64,128]{2,1,0:T(8,128)S(1)} %merge.1.base_ref, bf16[8,80,128]{2,1,0:T(8,128)(2,1)S(1)} %all-to-all-done.1.in_ref, bf16[3,16,128]{2,1,0:T(8,128)(2,1)S(1)} %get-tuple-element.47.last_ref, ...), custom_call_target="tpu_custom_call", output_to_operand_aliasing={{0}: (0, {})} | custom-call | tf_op jit(solution)/shard_map/finish/pallas_call | solution.py:688
Async XLA Ops:
  2.4 4.3 %collective-permute-start = (bf16[64,128]{1,0:T(8,128)(2,1)S(1)}, bf16[64,128]{1,0:T(8,128)(2,1)S(1)}, u32[]{:S(2)}, u32[]{:S(2)}) collective-permute-start(bf16[64,128]{1,0:T(8,128)(2,1)S(1)} %get-tuple-element.30), channel_id=1, source_target_pairs={{0,2},{1,3},{2,0},{3,1},{4,6},{5,7},{6,4},{7,5},{8,10},{9,11},{10,... | collective-permute-start | bytes 49160 | tf_op jit(solution)/shard_map/ppermute | solution.py:598
  5.2 2.8 %collective-permute-start.1 = (bf16[2,32,128]{2,1,0:T(8,128)(2,1)S(1)}, bf16[2,32,128]{2,1,0:T(8,128)(2,1)S(1)}, u32[]{:S(2)}, u32[]{:S(2)}) collective-permute-start(bf16[2,32,128]{2,1,0:T(8,128)(2,1)S(1)} %get-tuple-element.31), channel_id=1, source_target_pairs={{0,1},{1,0},{2,3},{3,2},{4,5},{5,4},{6,7},{7,6},{8,9},{9,8},{10,11... | collective-permute-start | bytes 49160 | tf_op jit(solution)/shard_map/ppermute | solution.py:598
  5.5 11.4 %copy-start = (s32[1,128]{1,0:T(1,128)S(1)}, s32[1,128]{1,0:T(1,128)}, u32[]{:S(2)}) copy-start(s32[1,128]{1,0:T(1,128)} %pairs_ref.1) | copy-start | bytes 1540
  9.3 12.8 %all-to-all-start = ((bf16[8,80,128]{2,1,0:T(8,128)(2,1)}), bf16[8,80,128]{2,1,0:T(8,128)(2,1)S(1)}, u32[]{:S(2)}, u32[]{:S(2)}) async-start(bf16[8,80,128]{2,1,0:T(8,128)(2,1)} %get-tuple-element.42), calls=%async_computation | async-start | bytes 327680 | tf_op jit(solution)/shard_map/all_to_all | solution.py:655
  15.6 2.2 %collective-permute-start.2 = (f32[32,128]{1,0:T(8,128)S(1)}, f32[32,128]{1,0:T(8,128)S(1)}, u32[]{:S(2)}, u32[]{:S(2)}) collective-permute-start(f32[32,128]{1,0:T(8,128)S(1)} %get-tuple-element.43), channel_id=1, source_target_pairs={{0,4},{4,8},{8,12},{12,16},{16,20},{20,24},{24,28},{28,32},{32,36}... | collective-permute-start | bytes 49160 | tf_op jit(solution)/shard_map/ppermute | solution.py:657
  16.9 5.3 %collective-permute-start.3 = (f32[32,128]{1,0:T(8,128)S(1)}, f32[32,128]{1,0:T(8,128)S(1)}, u32[]{:S(2)}, u32[]{:S(2)}) collective-permute-start(f32[32,128]{1,0:T(8,128)S(1)} %get-tuple-element.44), channel_id=1, source_target_pairs={{4,0},{8,4},{12,8},{16,12},{20,16},{24,20},{28,24},{32,28},{36,32}... | collective-permute-start | bytes 49160 | tf_op jit(solution)/shard_map/ppermute | solution.py:658
  23.0 14.4 %all-to-all-start.1 = ((bf16[8,80,128]{2,1,0:T(8,128)(2,1)}), bf16[8,80,128]{2,1,0:T(8,128)(2,1)S(1)}, u32[]{:S(2)}, u32[]{:S(2)}) async-start(bf16[8,80,128]{2,1,0:T(8,128)(2,1)} %get-tuple-element.46), calls=%async_computation.1 | async-start | bytes 327680 | tf_op jit(solution)/shard_map/all_to_all | solution.py:679
  33.5 3.9 %collective-permute-start.4 = (f32[48,128]{1,0:T(8,128)S(1)}, f32[48,128]{1,0:T(8,128)S(1)}, u32[]{:S(2)}, u32[]{:S(2)}) collective-permute-start(f32[48,128]{1,0:T(8,128)S(1)} %get-tuple-element.45), channel_id=1, source_target_pairs={{0,3},{1,2},{2,1},{3,0},{4,7},{5,6},{6,5},{7,4},{8,11},{9,10},{10,... | collective-permute-start | bytes 73736 | tf_op jit(solution)/shard_map/ppermute | solution.py:598
